TPU v7x, 512 devices: a whole 4x4x16 slice. The times are simulated.
512 devices in a mesh: dp: 16 (over y, x), seq: 32 (over z, core).
Axes of the slice: x: 4, y: 4, z: 16, core: 2. Of those that a mesh axis runs over, the one named last changes fastest.
Arguments:
- q_in: bfloat16 [65536, 2560], P(('dp', 'seq')), may hold values from -6 to 6
- k_in: bfloat16 [65536, 2560], P(('dp', 'seq')), may hold values from -6 to 6
- v_in: bfloat16 [65536, 2560], P(('dp', 'seq')), may hold values from -6 to 6
- gain_q: float32 [2560], replicated, may hold values from 0.5 to 1.5
- gain_k: float32 [2560], replicated, may hold values from 0.5 to 1.5
- d_out: bfloat16 [65536, 2560], P(('dp', 'seq')), may hold values from -6 to 6
- video: int32 [512], P(('dp', 'seq')), may hold values from 0 to 127, never falling along the last dimension, each value on 1 to 8 neighbouring positions
Outputs:
- dq_in: bfloat16 [65536, 2560], P(('dp', 'seq'))
- dk_in: bfloat16 [65536, 2560], P(('dp', 'seq'))
- dv_in: bfloat16 [65536, 2560], P(('dp', 'seq'))
- dgain_q: float32 [2560], replicated
- dgain_k: float32 [2560], replicated
Inputs may be any that keep to these rules, and one draw needn't show every extreme that they name: Video ids never fall along the group order; each video holds 1 to 8 consecutive groups and one holds exactly 8.
All inputs are finite; a program needn't handle non-finite values.
Results may differ from a plain program's by a relative error of at most 0.0079.
Values may be sent and summed in bfloat16 or wider, within the bound.
No kernel may reach another device: no remote copies, remote signals or barrier semaphores. Data moves between devices by JAX's collectives and lax.ppermute only.
A program may use at most 128 MiB of HBM per device.

v0:
```python
import math

import jax
import jax.numpy as jnp
from jax import lax
from jax.sharding import PartitionSpec as P

HSIZE = 128
WIN = 4


EPS = 1e-06
NEG = -1e30


def passed_along(shard, axis, by):
    peers = lax.axis_size(axis)
    pairs = [(i, i + by) for i in range(peers) if 0 <= i + by < peers]
    return lax.ppermute(shard, axis, pairs)


def normed(values, gain):
    factor = lax.rsqrt(jnp.mean(values * values, axis=-1, keepdims=True) + EPS)
    return values * factor * gain


def body(q_in, k_in, v_in, gain_q, gain_k, d_out, video):
    row_count = q_in.shape[0]
    feat_width = q_in.shape[1]
    head_count = feat_width // HSIZE
    score_scale = 1.0 / math.sqrt(HSIZE)
    q_float, q_pull = jax.vjp(normed, q_in.astype(jnp.float32), gain_q)
    k_float, k_pull = jax.vjp(normed, k_in.astype(jnp.float32), gain_k)
    q_norm = q_float.astype(jnp.bfloat16)
    k_norm = k_float.astype(jnp.bfloat16)
    marker = (video % 64 + 1).astype(jnp.bfloat16)
    key_list = [k_norm]
    value_list = [v_in]
    mark_list = [marker]
    for distance in range(1, WIN):
        got_keys, got_values, got_mark = passed_along(
            (k_norm, v_in, marker), ("dp", "seq"), distance
        )
        key_list.append(got_keys)
        value_list.append(got_values)
        mark_list.append(got_mark)
    keys_all = jnp.concatenate(key_list, 0).reshape(WIN * row_count, head_count, HSIZE)
    values_all = jnp.concatenate(value_list, 0).reshape(WIN * row_count, head_count, HSIZE)
    key_ok = jnp.repeat(jnp.concatenate(mark_list, 0) == marker, row_count)
    query_heads = q_norm.reshape(row_count, head_count, HSIZE)
    grad_heads = d_out.reshape(row_count, head_count, HSIZE)
    scores = (
        jnp.einsum("qhd,khd->hqk", query_heads, keys_all, preferred_element_type=jnp.float32)
        * score_scale
    )
    masked = jnp.where(key_ok[None, None, :], scores, NEG)
    row_max = jnp.max(masked, axis=-1)
    log_total = row_max + jnp.log(jnp.sum(jnp.exp(masked - row_max[..., None]), axis=-1))
    prob = jnp.exp(masked - log_total[..., None])
    prob_bf = prob.astype(jnp.bfloat16)
    attn_out = jnp.einsum("hqk,khd->qhd", prob_bf, values_all, preferred_element_type=jnp.float32)
    delta = jnp.transpose(jnp.sum(grad_heads.astype(jnp.float32) * attn_out, axis=-1))
    dprob = jnp.einsum("qhd,khd->hqk", grad_heads, values_all, preferred_element_type=jnp.float32)
    dscore = prob * (dprob - delta[..., None])
    dscore_bf = (dscore * score_scale).astype(jnp.bfloat16)
    dq_norm = jnp.einsum("hqk,khd->qhd", dscore_bf, keys_all, preferred_element_type=jnp.float32)
    dk_part = (
        jnp.einsum("hqk,qhd->khd", dscore_bf, query_heads, preferred_element_type=jnp.float32)
        .astype(jnp.bfloat16)
        .reshape(WIN, row_count, feat_width)
    )
    dv_part = (
        jnp.einsum("hqk,qhd->khd", prob_bf, grad_heads, preferred_element_type=jnp.float32)
        .astype(jnp.bfloat16)
        .reshape(WIN, row_count, feat_width)
    )
    dk_part, dv_part = lax.optimization_barrier((dk_part, dv_part))
    dk_total = dk_part[0].astype(jnp.float32)
    dv_total = dv_part[0].astype(jnp.float32)
    for distance in range(1, WIN):
        back_keys, back_values = passed_along(
            (dk_part[distance], dv_part[distance]), ("dp", "seq"), -distance
        )
        dk_total = dk_total + back_keys.astype(jnp.float32)
        dv_total = dv_total + back_values.astype(jnp.float32)
    dq_float, dgain_q_part = q_pull(dq_norm.reshape(row_count, feat_width))
    dk_float, dgain_k_part = k_pull(dk_total)
    dgain_q, dgain_k = lax.psum((dgain_q_part, dgain_k_part), ("dp", "seq"))
    return (
        dq_float.astype(jnp.bfloat16),
        dk_float.astype(jnp.bfloat16),
        dv_total.astype(jnp.bfloat16),
        dgain_q,
        dgain_k,
    )


def solution(mesh):
    placed = (
        P(("dp", "seq"), None),
        P(("dp", "seq"), None),
        P(("dp", "seq"), None),
        P(),
        P(),
        P(("dp", "seq"), None),
        P(("dp", "seq")),
    )
    return jax.shard_map(
        body,
        mesh=mesh,
        in_specs=placed,
        out_specs=(
            P(("dp", "seq"), None),
            P(("dp", "seq"), None),
            P(("dp", "seq"), None),
            P(),
            P(),
        ),
        check_vma=False,
    )
```

profile of v0, /device:TPU:1, one launch (start us, length us, event | category | flops | bytes accessed | tf_op | source)
XLA Modules:
  0.0 338.2 jit_solution(9514368303020900518)
XLA Ops:
  1.4 7.0 %collective-permute-start.5 = (bf16[1]{0:T(256)(128)(2,1)}, bf16[1]{0:T(256)(128)(2,1)}, u32[]{:S(2)}, u32[]{:S(2)}) collective-permute-start(bf16[1]{0:T(256)(128)(2,1)} %convert_element_type.77), channel_id=1, source_target_pairs={{0,3},{1,4},{2,5},{3,6},{4,7},{5,8},{6,9},{7,10},{8,11},{9,12},{10... | collective-permute-start | bytes 14 | tf_op jit(solution)/shard_map/ppermute | solution.py:19
  8.4 4.2 %collective-permute-start.4 = (bf16[1]{0:T(256)(128)(2,1)}, bf16[1]{0:T(256)(128)(2,1)}, u32[]{:S(2)}, u32[]{:S(2)}) collective-permute-start(bf16[1]{0:T(256)(128)(2,1)} %convert_element_type.77), channel_id=1, source_target_pairs={{0,2},{1,3},{2,4},{3,5},{4,6},{5,7},{6,8},{7,9},{8,10},{9,11},{10,... | collective-permute-start | bytes 14 | tf_op jit(solution)/shard_map/ppermute | solution.py:19
  15.5 5.9 %collective-permute-start.2 = (bf16[128,2560]{0,1:T(8,128)(2,1)S(1)}, bf16[128,2560]{0,1:T(8,128)(2,1)S(1)}, u32[]{:S(2)}, u32[]{:S(2)}) collective-permute-start(bf16[128,2560]{0,1:T(8,128)(2,1)S(1)} %fusion.11), channel_id=1, source_target_pairs={{0,3},{1,4},{2,5},{3,6},{4,7},{5,8},{6,9},{7,10},{8,11},{9,12},{10... | collective-permute-start | bytes 1966088 | tf_op jit(solution)/shard_map/ppermute | solution.py:19
  21.5 4.4 %collective-permute-start.1 = (bf16[128,2560]{0,1:T(8,128)(2,1)S(1)}, bf16[128,2560]{0,1:T(8,128)(2,1)}, u32[]{:S(2)}, u32[]{:S(2)}) collective-permute-start(bf16[128,2560]{0,1:T(8,128)(2,1)S(1)} %fusion.11), channel_id=1, source_target_pairs={{0,2},{1,3},{2,4},{3,5},{4,6},{5,7},{6,8},{7,9},{8,10},{9,11},{10,... | collective-permute-start | bytes 1966088 | tf_op jit(solution)/shard_map/ppermute | solution.py:19
  25.8 2.1 collective-permute-start
  29.1 2.4 copy.112
  31.5 2.2 copy.113
  33.7 29.9 %collective-permute-start.3 = (bf16[1]{0:T(256)(128)(2,1)}, bf16[1]{0:T(256)(128)(2,1)}, u32[]{:S(2)}, u32[]{:S(2)}) collective-permute-start(bf16[1]{0:T(256)(128)(2,1)} %convert_element_type.77), channel_id=1, source_target_pairs={{0,1},{1,2},{2,3},{3,4},{4,5},{5,6},{6,7},{7,8},{8,9},{9,10},{10,1... | collective-permute-start | bytes 14 | tf_op jit(solution)/shard_map/ppermute | solution.py:19
  64.9 4.2 %collective-permute-start.7 = (bf16[128,2560]{0,1:T(8,128)(2,1)}, bf16[128,2560]{0,1:T(8,128)(2,1)S(1)}, u32[]{:S(2)}, u32[]{:S(2)}) collective-permute-start(bf16[128,2560]{0,1:T(8,128)(2,1)} %copy.112), channel_id=1, source_target_pairs={{0,2},{1,3},{2,4},{3,5},{4,6},{5,7},{6,8},{7,9},{8,10},{9,11},{10,... | collective-permute-start | bytes 1966088 | tf_op jit(solution)/shard_map/ppermute | solution.py:19
  69.0 1.9 maximum_compare_fusion
  71.0 5.9 %collective-permute-start.6 = (bf16[128,2560]{0,1:T(8,128)(2,1)}, bf16[128,2560]{0,1:T(8,128)(2,1)S(1)}, u32[]{:S(2)}, u32[]{:S(2)}) collective-permute-start(bf16[128,2560]{0,1:T(8,128)(2,1)} %copy.112), channel_id=1, source_target_pairs={{0,1},{1,2},{2,3},{3,4},{4,5},{5,6},{6,7},{7,8},{8,9},{9,10},{10,1... | collective-permute-start | bytes 1966088 | tf_op jit(solution)/shard_map/ppermute | solution.py:19
  81.2 2.1 convert_bitcast_fusion
  83.3 15.2 %collective-permute-done.7 = bf16[128,2560]{0,1:T(8,128)(2,1)S(1)} collective-permute-done((bf16[128,2560]{0,1:T(8,128)(2,1)}, bf16[128,2560]{0,1:T(8,128)(2,1)S(1)}, u32[]{:S(2)}, u32[]{:S(2)}) %collective-permute-start.7) | collective-permute-done | bytes 655392 | tf_op jit(solution)/shard_map/ppermute | solution.py:19
  98.5 9.3 %collective-permute-done.6 = bf16[128,2560]{0,1:T(8,128)(2,1)S(1)} collective-permute-done((bf16[128,2560]{0,1:T(8,128)(2,1)}, bf16[128,2560]{0,1:T(8,128)(2,1)S(1)}, u32[]{:S(2)}, u32[]{:S(2)}) %collective-permute-start.6) | collective-permute-done | bytes 655392 | tf_op jit(solution)/shard_map/ppermute | solution.py:19
  110.9 2.2 fusion.1
  113.1 2.0 fusion.31
  115.0 2.3 convert_bitcast_fusion.1
  117.4 4.9 %reshape.91 = bf16[4,128,2560]{1,0,2:T(4,128)(2,1)} reshape(bf16[512,20,128]{0,2,1:T(8,128)(2,1)} %convert_bitcast_fusion.1) | data formatting | bytes 5242880 | tf_op jit(solution)/shard_map/reshape | solution.py:70
  122.3 2.6 copy.119
  124.9 3.5 %reshape.92 = bf16[4,128,2560]{1,0,2:T(4,128)(2,1)S(1)} reshape(bf16[512,20,128]{0,2,1:T(8,128)(2,1)} %copy.119) | data formatting | bytes 5242880 | tf_op jit(solution)/shard_map/reshape | solution.py:75
  128.4 3.7 %copy.120 = bf16[4,128,2560]{1,2,0:T(8,128)(2,1)} copy(bf16[4,128,2560]{1,0,2:T(4,128)(2,1)} %reshape.91) | data formatting | bytes 5242880 | tf_op jit(solution)/shard_map/optimization_barrier | solution.py:77
  134.2 2.2 copy.130
  138.0 1.9 collective-permute-start.9
  142.5 4.5 %fusion.30 = (bf16[1,128,2560]{1,0,2:T(2,128)(2,1)S(1)}, bf16[1,128,2560]{1,0,2:T(2,128)(2,1)S(1)}, bf16[1,128,2560]{1,0,2:T(2,128)(2,1)S(1)}, f32[1,128,2560]{1,0,2:T(1,128)}) fusion(bf16[4,128,2560]{1,0,2:T(4,128)(2,1)S(1)} %reshape.92), kind=kLoop, calls=%fused_computation.65 | loop fusion | flops 327680 | bytes 5898240 | tf_op jit(solution)/shard_map/slice | solution.py:82
  151.6 4.4 %collective-permute-done.9 = bf16[128,2560]{0,1:T(8,128)(2,1)S(1)} collective-permute-done((bf16[128,2560]{0,1:T(8,128)(2,1)S(1)}, bf16[128,2560]{0,1:T(8,128)(2,1)S(1)}, u32[]{:S(2)}, u32[]{:S(2)}) %collective-permute-start.9) | collective-permute-done | bytes 655392 | tf_op jit(solution)/shard_map/ppermute | solution.py:19
  156.0 2.1 collective-permute-start.12
  158.2 18.5 %collective-permute-done.11 = bf16[128,2560]{0,1:T(8,128)(2,1)S(1)} collective-permute-done((bf16[128,2560]{0,1:T(8,128)(2,1)S(1)}, bf16[128,2560]{0,1:T(8,128)(2,1)S(1)}, u32[]{:S(2)}, u32[]{:S(2)}) %collective-permute-start.11) | collective-permute-done | bytes 655392 | tf_op jit(solution)/shard_map/ppermute | solution.py:19
  176.7 4.1 %collective-permute-done.10 = bf16[128,2560]{0,1:T(8,128)(2,1)S(1)} collective-permute-done((bf16[128,2560]{0,1:T(8,128)(2,1)S(1)}, bf16[128,2560]{0,1:T(8,128)(2,1)S(1)}, u32[]{:S(2)}, u32[]{:S(2)}) %collective-permute-start.10) | collective-permute-done | bytes 655392 | tf_op jit(solution)/shard_map/ppermute | solution.py:19
  183.5 11.1 %collective-permute-done.13 = bf16[128,2560]{0,1:T(8,128)(2,1)} collective-permute-done((bf16[128,2560]{0,1:T(8,128)(2,1)}, bf16[128,2560]{0,1:T(8,128)(2,1)}, u32[]{:S(2)}, u32[]{:S(2)}) %collective-permute-start.13) | collective-permute-done | bytes 655392 | tf_op jit(solution)/shard_map/ppermute | solution.py:19
  194.6 27.2 %collective-permute-done.14 = bf16[128,2560]{0,1:T(8,128)(2,1)} collective-permute-done((bf16[128,2560]{0,1:T(8,128)(2,1)}, bf16[128,2560]{0,1:T(8,128)(2,1)}, u32[]{:S(2)}, u32[]{:S(2)}) %collective-permute-start.14) | collective-permute-done | bytes 655392 | tf_op jit(solution)/shard_map/ppermute | solution.py:19
  221.8 1.8 add_convert_fusion
  224.6 113.6 %all-reduce = (f32[2560]{0:T(1024)}, f32[2560]{0:T(1024)}) all-reduce(f32[2560]{0:T(1024)S(1)} %get-tuple-element.31, f32[2560]{0:T(1024)S(1)} %get-tuple-element.29), channel_id=1, replica_groups=mesh['dp'=16,'seq'=32] {'dp','seq'}, use_global_device_ids=true, to_apply=%region_8.9 | all-reduce | flops 5120 | bytes 40960 | tf_op jit(solution)/shard_map/psum | solution.py:88
  (62 shorter events, 27.2 us)
Async XLA Ops:
  0.6 27.3 %copy-start.8 = (bf16[128,2560]{1,0:T(8,128)(2,1)S(1)}, bf16[128,2560]{1,0:T(8,128)(2,1)}, u32[]{:S(2)}) copy-start(bf16[128,2560]{1,0:T(8,128)(2,1)} %param.7) | copy-start | bytes 1966084
  1.4 27.3 %copy-start.9 = (f32[2560]{0:T(1024)S(1)}, f32[2560]{0:T(1024)}, u32[]{:S(2)}) copy-start(f32[2560]{0:T(1024)} %param.10) | copy-start | bytes 30724
  1.4 32.3 %collective-permute-start.5 = (bf16[1]{0:T(256)(128)(2,1)}, bf16[1]{0:T(256)(128)(2,1)}, u32[]{:S(2)}, u32[]{:S(2)}) collective-permute-start(bf16[1]{0:T(256)(128)(2,1)} %convert_element_type.77), channel_id=1, source_target_pairs={{0,3},{1,4},{2,5},{3,6},{4,7},{5,8},{6,9},{7,10},{8,11},{9,12},{10... | collective-permute-start | bytes 14 | tf_op jit(solution)/shard_map/ppermute | solution.py:19
  8.4 55.1 %collective-permute-start.4 = (bf16[1]{0:T(256)(128)(2,1)}, bf16[1]{0:T(256)(128)(2,1)}, u32[]{:S(2)}, u32[]{:S(2)}) collective-permute-start(bf16[1]{0:T(256)(128)(2,1)} %convert_element_type.77), channel_id=1, source_target_pairs={{0,2},{1,3},{2,4},{3,5},{4,6},{5,7},{6,8},{7,9},{8,10},{9,11},{10,... | collective-permute-start | bytes 14 | tf_op jit(solution)/shard_map/ppermute | solution.py:19
  15.5 55.5 %collective-permute-start.2 = (bf16[128,2560]{0,1:T(8,128)(2,1)S(1)}, bf16[128,2560]{0,1:T(8,128)(2,1)S(1)}, u32[]{:S(2)}, u32[]{:S(2)}) collective-permute-start(bf16[128,2560]{0,1:T(8,128)(2,1)S(1)} %fusion.11), channel_id=1, source_target_pairs={{0,3},{1,4},{2,5},{3,6},{4,7},{5,8},{6,9},{7,10},{8,11},{9,12},{10... | collective-permute-start | bytes 1966088 | tf_op jit(solution)/shard_map/ppermute | solution.py:19
  21.5 55.4 %collective-permute-start.1 = (bf16[128,2560]{0,1:T(8,128)(2,1)S(1)}, bf16[128,2560]{0,1:T(8,128)(2,1)}, u32[]{:S(2)}, u32[]{:S(2)}) collective-permute-start(bf16[128,2560]{0,1:T(8,128)(2,1)S(1)} %fusion.11), channel_id=1, source_target_pairs={{0,2},{1,3},{2,4},{3,5},{4,6},{5,7},{6,8},{7,9},{8,10},{9,11},{10,... | collective-permute-start | bytes 1966088 | tf_op jit(solution)/shard_map/ppermute | solution.py:19
  25.8 51.1 %collective-permute-start = (bf16[128,2560]{0,1:T(8,128)(2,1)S(1)}, bf16[128,2560]{0,1:T(8,128)(2,1)}, u32[]{:S(2)}, u32[]{:S(2)}) collective-permute-start(bf16[128,2560]{0,1:T(8,128)(2,1)S(1)} %fusion.11), channel_id=1, source_target_pairs={{0,1},{1,2},{2,3},{3,4},{4,5},{5,6},{6,7},{7,8},{8,9},{9,10},{10,1... | collective-permute-start | bytes 1966088 | tf_op jit(solution)/shard_map/ppermute | solution.py:19
  28.3 50.2 %copy-start = (bf16[128,2560]{0,1:T(8,128)(2,1)}, bf16[128,2560]{0,1:T(8,128)(2,1)S(1)}, u32[]{:S(2)}) copy-start(bf16[128,2560]{0,1:T(8,128)(2,1)S(1)} %copy.106) | copy-start | bytes 1966084
  29.1 49.4 %copy-start.4 = (bf16[128,2560]{0,1:T(8,128)(2,1)}, bf16[128,2560]{0,1:T(8,128)(2,1)S(1)}, u32[]{:S(2)}) copy-start(bf16[128,2560]{0,1:T(8,128)(2,1)S(1)} %fusion.9) | copy-start | bytes 1966084
  33.7 31.2 %collective-permute-start.3 = (bf16[1]{0:T(256)(128)(2,1)}, bf16[1]{0:T(256)(128)(2,1)}, u32[]{:S(2)}, u32[]{:S(2)}) collective-permute-start(bf16[1]{0:T(256)(128)(2,1)} %convert_element_type.77), channel_id=1, source_target_pairs={{0,1},{1,2},{2,3},{3,4},{4,5},{5,6},{6,7},{7,8},{8,9},{9,10},{10,1... | collective-permute-start | bytes 14 | tf_op jit(solution)/shard_map/ppermute | solution.py:19
  63.5 19.7 %collective-permute-start.8 = (bf16[128,2560]{0,1:T(8,128)(2,1)}, bf16[128,2560]{0,1:T(8,128)(2,1)S(1)}, u32[]{:S(2)}, u32[]{:S(2)}) collective-permute-start(bf16[128,2560]{0,1:T(8,128)(2,1)} %copy.112), channel_id=1, source_target_pairs={{0,3},{1,4},{2,5},{3,6},{4,7},{5,8},{6,9},{7,10},{8,11},{9,12},{10... | collective-permute-start | bytes 1966088 | tf_op jit(solution)/shard_map/ppermute | solution.py:19
  64.9 33.6 %collective-permute-start.7 = (bf16[128,2560]{0,1:T(8,128)(2,1)}, bf16[128,2560]{0,1:T(8,128)(2,1)S(1)}, u32[]{:S(2)}, u32[]{:S(2)}) collective-permute-start(bf16[128,2560]{0,1:T(8,128)(2,1)} %copy.112), channel_id=1, source_target_pairs={{0,2},{1,3},{2,4},{3,5},{4,6},{5,7},{6,8},{7,9},{8,10},{9,11},{10,... | collective-permute-start | bytes 1966088 | tf_op jit(solution)/shard_map/ppermute | solution.py:19
  71.0 36.7 %collective-permute-start.6 = (bf16[128,2560]{0,1:T(8,128)(2,1)}, bf16[128,2560]{0,1:T(8,128)(2,1)S(1)}, u32[]{:S(2)}, u32[]{:S(2)}) collective-permute-start(bf16[128,2560]{0,1:T(8,128)(2,1)} %copy.112), channel_id=1, source_target_pairs={{0,1},{1,2},{2,3},{3,4},{4,5},{5,6},{6,7},{7,8},{8,9},{9,10},{10,1... | collective-permute-start | bytes 1966088 | tf_op jit(solution)/shard_map/ppermute | solution.py:19
  79.7 1.5 copy-start.7
  113.1 2.0 copy-start.5
  128.4 3.7 %copy-start.1 = (bf16[128,2560]{0,1:T(8,128)(2,1)S(1)}, bf16[128,2560]{0,1:T(8,128)(2,1)}, u32[]{:S(2)}) copy-start(bf16[128,2560]{0,1:T(8,128)(2,1)} %copy-done) | copy-start | bytes 1966084
  128.4 3.7 %copy-start.3 = (f32[20,128,128]{2,1,0:T(8,128)S(1)}, f32[20,128,128]{2,1,0:T(8,128)}, u32[]{:S(2)}) copy-start(f32[20,128,128]{2,1,0:T(8,128)} %fusion.31) | copy-start | bytes 3932164
  138.0 18.1 %collective-permute-start.9 = (bf16[128,2560]{0,1:T(8,128)(2,1)S(1)}, bf16[128,2560]{0,1:T(8,128)(2,1)S(1)}, u32[]{:S(2)}, u32[]{:S(2)}) collective-permute-start(bf16[128,2560]{0,1:T(8,128)(2,1)S(1)} %get-tuple-element.39), channel_id=1, source_target_pairs={{1,0},{2,1},{3,2},{4,3},{5,4},{6,5},{7,6},{8,7},{9,8},{10,9},{11,1... | collective-permute-start | bytes 1966088 | tf_op jit(solution)/shard_map/ppermute | solution.py:19
  139.9 36.8 %collective-permute-start.11 = (bf16[128,2560]{0,1:T(8,128)(2,1)S(1)}, bf16[128,2560]{0,1:T(8,128)(2,1)S(1)}, u32[]{:S(2)}, u32[]{:S(2)}) collective-permute-start(bf16[128,2560]{0,1:T(8,128)(2,1)S(1)} %get-tuple-element.40), channel_id=1, source_target_pairs={{3,0},{4,1},{5,2},{6,3},{7,4},{8,5},{9,6},{10,7},{11,8},{12,9},{13... | collective-permute-start | bytes 1966088 | tf_op jit(solution)/shard_map/ppermute | solution.py:19
  141.2 39.6 %collective-permute-start.10 = (bf16[128,2560]{0,1:T(8,128)(2,1)S(1)}, bf16[128,2560]{0,1:T(8,128)(2,1)S(1)}, u32[]{:S(2)}, u32[]{:S(2)}) collective-permute-start(bf16[128,2560]{0,1:T(8,128)(2,1)S(1)} %get-tuple-element.41), channel_id=1, source_target_pairs={{2,0},{3,1},{4,2},{5,3},{6,4},{7,5},{8,6},{9,7},{10,8},{11,9},{12,... | collective-permute-start | bytes 1966088 | tf_op jit(solution)/shard_map/ppermute | solution.py:19
  147.0 33.8 %copy-start.2 = (bf16[4,128,2560]{1,2,0:T(8,128)(2,1)S(1)}, bf16[4,128,2560]{1,2,0:T(8,128)(2,1)}, u32[]{:S(2)}) copy-start(bf16[4,128,2560]{1,2,0:T(8,128)(2,1)} %copy.120) | copy-start | bytes 7864324
  147.0 33.8 %copy-start.10 = (f32[2560]{0:T(1024)S(1)}, f32[2560]{0:T(1024)}, u32[]{:S(2)}) copy-start(f32[2560]{0:T(1024)} %param.11) | copy-start | bytes 30724
  149.0 45.6 %collective-permute-start.13 = (bf16[128,2560]{0,1:T(8,128)(2,1)}, bf16[128,2560]{0,1:T(8,128)(2,1)}, u32[]{:S(2)}, u32[]{:S(2)}) collective-permute-start(bf16[128,2560]{0,1:T(8,128)(2,1)} %bitcast.75), channel_id=1, source_target_pairs={{2,0},{3,1},{4,2},{5,3},{6,4},{7,5},{8,6},{9,7},{10,8},{11,9},{12,... | collective-permute-start | bytes 1966088 | tf_op jit(solution)/shard_map/ppermute | solution.py:19
  150.3 71.4 %collective-permute-start.14 = (bf16[128,2560]{0,1:T(8,128)(2,1)}, bf16[128,2560]{0,1:T(8,128)(2,1)}, u32[]{:S(2)}, u32[]{:S(2)}) collective-permute-start(bf16[128,2560]{0,1:T(8,128)(2,1)} %bitcast.74), channel_id=1, source_target_pairs={{3,0},{4,1},{5,2},{6,3},{7,4},{8,5},{9,6},{10,7},{11,8},{12,9},{13... | collective-permute-start | bytes 1966088 | tf_op jit(solution)/shard_map/ppermute | solution.py:19
  156.0 65.7 %collective-permute-start.12 = (bf16[128,2560]{0,1:T(8,128)(2,1)S(1)}, bf16[128,2560]{0,1:T(8,128)(2,1)}, u32[]{:S(2)}, u32[]{:S(2)}) collective-permute-start(bf16[128,2560]{0,1:T(8,128)(2,1)S(1)} %bitcast.87), channel_id=1, source_target_pairs={{1,0},{2,1},{3,2},{4,3},{5,4},{6,5},{7,6},{8,7},{9,8},{10,9},{11,1... | collective-permute-start | bytes 1966088 | tf_op jit(solution)/shard_map/ppermute | solution.py:19
  181.8 40.0 %copy-start.6 = (f32[1,128,2560]{1,0,2:T(1,128)S(1)}, f32[1,128,2560]{1,0,2:T(1,128)}, u32[]{:S(2)}) copy-start(f32[1,128,2560]{1,0,2:T(1,128)} %get-tuple-element.38) | copy-start | bytes 3932164
where the time goes:
time: 339 us; the launch traced here: 338 us
  blocking collectives  114 us (34%)
  waiting for transfers between devices  89.8 us (26%)
  starting transfers between devices  74.1 us (22%)
  local copies, waits for them, and re-layouts  29.1 us (9%)
  other arithmetic  18.6 us (5%)
  matrix products  11.4 us (3%)
    psum x1, blocking collectives, body(): dgain_q, dgain_k = lax.psum((dgain_q_part, dgain_k_part), ('dp', 'seq'))  114 us
    ppermute x15, waiting for transfers between devices, passed_along(): return lax.ppermute(shard, axis, pairs)  89.8 us
    ppermute x15, starting transfers between devices, passed_along(): return lax.ppermute(shard, axis, pairs)  74.1 us
    unnamed x29, local copies, waits for them, and re-layouts  10.7 us
  transfers between devices with their start and end apart: 15, of which 7 were waited for; matrix products, arithmetic and copies ran while one was open for 8% of the time, Pallas kernels for 0%

commit v1 on v0

v1 whole, which is shorter than its diff:
```python
import functools
import math

import jax
import jax.numpy as jnp
from jax import lax
from jax.experimental import pallas as pl
from jax.experimental.pallas import tpu as pltpu
from jax.sharding import PartitionSpec as P

HSIZE = 128
WIN = 4
EPS = 1e-06
NEG = -1e30
MARK_ROWS = 16
AXES = ("dp", "seq")
VMEM_LIMIT = 40 * 1024 * 1024
F32 = jnp.float32
BF16 = jnp.bfloat16


def dot_nt(a, b):
    return lax.dot_general(a, b, (((1,), (1,)), ((), ())), preferred_element_type=F32)


def dot_nn(a, b):
    return lax.dot_general(a, b, (((1,), (0,)), ((), ())), preferred_element_type=F32)


def pack_kernel(heads, odd_ref, video_ref, q_ref, k_ref, v_ref, d_ref, gq_ref, gk_ref, a_ref, b_ref, rq_ref, rk_ref):
    odd = odd_ref[0] == 1
    rows = q_ref.shape[0]
    width = q_ref.shape[1]
    q_raw = q_ref[...].astype(F32)
    k_raw = k_ref[...].astype(F32)
    rq = lax.rsqrt(jnp.sum(q_raw * q_raw, axis=-1, keepdims=True) * (1.0 / width) + EPS)
    rk = lax.rsqrt(jnp.sum(k_raw * k_raw, axis=-1, keepdims=True) * (1.0 / width) + EPS)
    rq_ref[...] = jnp.broadcast_to(rq, rq_ref.shape)
    rk_ref[...] = jnp.broadcast_to(rk, rk_ref.shape)
    for h in range(heads):
        cols = slice(h * HSIZE, (h + 1) * HSIZE)
        qn = (q_ref[:, cols].astype(F32) * rq * gq_ref[:, cols]).astype(BF16)
        kn = (k_ref[:, cols].astype(F32) * rk * gk_ref[:, cols]).astype(BF16)
        v = v_ref[:, cols]
        d = d_ref[:, cols]
        top = slice(2 * h * rows, (2 * h + 1) * rows)
        low = slice((2 * h + 1) * rows, (2 * h + 2) * rows)
        a_ref[top, :] = jnp.where(odd, kn, qn)
        b_ref[top, :] = jnp.where(odd, qn, kn)
        a_ref[low, :] = jnp.where(odd, v, d)
        b_ref[low, :] = jnp.where(odd, d, v)
    mark = jnp.full((MARK_ROWS, HSIZE), (video_ref[0] + 1).astype(F32), F32).astype(BF16)
    a_ref[2 * heads * rows :, :] = mark
    b_ref[2 * heads * rows :, :] = mark


def bias_of(odd, own_mark, x_mark, s_mark, take_s):
    mark = jnp.where(odd == take_s, s_mark[0:1, 0:1].astype(F32), x_mark[0:1, 0:1].astype(F32))
    return jnp.where(mark == own_mark, 0.0, NEG)


def query_kernel(heads, per, factor, odd_ref, a, b, x1, s1, x2, s2, x3, s3, am, x1m, s1m, x2m, s2m, x3m, s3m,
                 q_ref, gq_ref, rq_ref, t_ref, w_ref, u_ref, stat_ref, stat_acc):
    step = pl.program_id(0)
    odd = odd_ref[0] == 1
    rows = q_ref.shape[0]
    own_mark = am[0:1, 0:1].astype(F32)
    biases = [bias_of(odd, own_mark, xm, sm, True) for xm, sm in ((x1m, s1m), (x2m, s2m), (x3m, s3m))]
    lane = lax.broadcasted_iota(jnp.int32, (rows, HSIZE), 1)
    scale = 1.0 / math.sqrt(HSIZE)

    @pl.when(step == 0)
    def _():
        u_ref[...] = jnp.zeros_like(u_ref)
        stat_acc[...] = jnp.zeros_like(stat_acc)

    for j in range(per):
        top = slice(2 * j * rows, (2 * j + 1) * rows)
        low = slice((2 * j + 1) * rows, (2 * j + 2) * rows)
        cols = slice(j * HSIZE, (j + 1) * HSIZE)
        q = jnp.where(odd, b[top, :], a[top, :])
        d_out = jnp.where(odd, b[low, :], a[low, :])
        keys = [jnp.where(odd, a[top, :], b[top, :])] + [
            jnp.where(odd, s[top, :], x[top, :]) for x, s in ((x1, s1), (x2, s2), (x3, s3))
        ]
        vals = [jnp.where(odd, a[low, :], b[low, :])] + [
            jnp.where(odd, s[low, :], x[low, :]) for x, s in ((x1, s1), (x2, s2), (x3, s3))
        ]
        scores = [dot_nt(q, key) for key in keys]
        dprobs = [dot_nt(d_out, val) for val in vals]
        top_of = jnp.max(scores[0], axis=-1, keepdims=True) * factor
        for score, bias in zip(scores[1:], biases):
            top_of = jnp.maximum(top_of, jnp.max(score, axis=-1, keepdims=True) * factor + bias)
        probs = [jnp.exp2(scores[0] * factor - top_of)] + [
            jnp.exp2(score * factor + (bias - top_of)) for score, bias in zip(scores[1:], biases)
        ]
        total = jnp.sum(probs[0] + probs[1] + probs[2] + probs[3], axis=-1, keepdims=True)
        mixed = jnp.sum(
            probs[0] * dprobs[0] + probs[1] * dprobs[1] + probs[2] * dprobs[2] + probs[3] * dprobs[3],
            axis=-1, keepdims=True,
        )
        inverse = 1.0 / total
        delta = mixed * inverse
        dq = None
        for prob, dprob, key in zip(probs, dprobs, keys):
            term = dot_nn(((prob * inverse) * (dprob - delta)).astype(BF16), key)
            dq = term if dq is None else dq + term
        dq = dq * scale
        raw = q_ref[:, cols].astype(F32)
        tilted = dq * gq_ref[:, cols]
        t_ref[:, cols] = tilted
        u_ref[...] += jnp.sum(raw * tilted, axis=-1, keepdims=True)
        w_ref[0, j : j + 1, :] = jnp.sum(dq * (raw * rq_ref[...]), axis=0, keepdims=True)
        head = step * per + j
        log_total = top_of + jnp.log2(total)
        stat_acc[...] = jnp.where(
            lane == head, log_total, jnp.where(lane == head + heads, delta, stat_acc[...])
        )

    @pl.when(step == heads // per - 1)
    def _():
        stat_ref[...] = jnp.transpose(stat_acc[...])[: 2 * heads, :]


def key_kernel(heads, per, factor, odd_ref, a, b, x1, s1, x2, s2, x3, s3, am, x1m, s1m, x2m, s2m, x3m, s3m,
               t0_ref, t1_ref, t2_ref, t3_ref, k_ref, gk_ref, rk_ref, dk_ref, dv_ref, tilt, u_acc):
    step = pl.program_id(0)
    odd = odd_ref[0] == 1
    rows = k_ref.shape[0]
    width = k_ref.shape[1]
    own_mark = am[0:1, 0:1].astype(F32)
    biases = [jnp.zeros((1, 1), F32)] + [
        bias_of(odd, own_mark, xm, sm, False) for xm, sm in ((x1m, s1m), (x2m, s2m), (x3m, s3m))
    ]
    scale = 1.0 / math.sqrt(HSIZE)

    @pl.when(step == 0)
    def _():
        u_acc[...] = jnp.zeros_like(u_acc)

    for j in range(per):
        top = slice(2 * j * rows, (2 * j + 1) * rows)
        low = slice((2 * j + 1) * rows, (2 * j + 2) * rows)
        head = step * per + j
        key = jnp.where(odd, a[top, :], b[top, :])
        val = jnp.where(odd, a[low, :], b[low, :])
        queries = [jnp.where(odd, b[top, :], a[top, :])] + [
            jnp.where(odd, x[top, :], s[top, :]) for x, s in ((x1, s1), (x2, s2), (x3, s3))
        ]
        d_outs = [jnp.where(odd, b[low, :], a[low, :])] + [
            jnp.where(odd, x[low, :], s[low, :]) for x, s in ((x1, s1), (x2, s2), (x3, s3))
        ]
        dk = None
        dv = None
        for query, d_out, stat, bias in zip(queries, d_outs, (t0_ref, t1_ref, t2_ref, t3_ref), biases):
            log_total = stat[pl.ds(head, 1), :]
            delta = stat[pl.ds(head + heads, 1), :]
            prob = jnp.exp2(dot_nt(key, query) * factor + (bias - log_total))
            dscore = prob * (dot_nt(val, d_out) - delta)
            dv_term = dot_nn(prob.astype(BF16), d_out)
            dk_term = dot_nn(dscore.astype(BF16), query)
            dv = dv_term if dv is None else dv + dv_term
            dk = dk_term if dk is None else dk + dk_term
        dv_ref[:, j * HSIZE : (j + 1) * HSIZE] = dv.astype(BF16)
        cols = pl.ds(pl.multiple_of(head * HSIZE, HSIZE), HSIZE)
        tilted = dk * scale * gk_ref[:, cols]
        tilt[:, cols] = tilted
        u_acc[...] += jnp.sum(k_ref[:, cols].astype(F32) * tilted, axis=-1, keepdims=True)

    @pl.when(step == heads // per - 1)
    def _():
        rk = rk_ref[...]
        low_part = rk * rk * rk * u_acc[...] * (1.0 / width)
        for h in range(heads):
            cols = slice(h * HSIZE, (h + 1) * HSIZE)
            dk_ref[:, cols] = (rk * tilt[:, cols] - k_ref[:, cols].astype(F32) * low_part).astype(BF16)


def close_kernel(heads, q_ref, t_ref, u_ref, rq_ref, dq_ref):
    rq = rq_ref[...]
    low_part = rq * rq * rq * u_ref[...] * (1.0 / q_ref.shape[1])
    for h in range(heads):
        cols = slice(h * HSIZE, (h + 1) * HSIZE)
        dq_ref[:, cols] = (rq * t_ref[:, cols] - q_ref[:, cols].astype(F32) * low_part).astype(BF16)


def smem():
    return pl.BlockSpec(memory_space=pltpu.SMEM)


def vmem():
    return pl.BlockSpec(memory_space=pltpu.VMEM)


def body(q_in, k_in, v_in, gain_q, gain_k, d_out, video):
    rows, width = q_in.shape
    heads = width // HSIZE
    per = 4
    steps = heads // per
    factor = math.log2(math.e) / math.sqrt(HSIZE)
    groups = lax.axis_size("dp") * lax.axis_size("seq")
    odd = (lax.axis_index("seq") % 2).astype(jnp.int32).reshape(1)
    gq = gain_q.reshape(1, width)
    gk = gain_k.reshape(1, width)
    params = pltpu.CompilerParams(vmem_limit_bytes=VMEM_LIMIT, dimension_semantics=("arbitrary",))
    packed = jax.ShapeDtypeStruct((2 * heads * rows + MARK_ROWS, HSIZE), BF16)
    wide = jax.ShapeDtypeStruct((rows, HSIZE), F32)
    a, b, rq, rk = pl.pallas_call(
        functools.partial(pack_kernel, heads),
        out_shape=(packed, packed, wide, wide),
        in_specs=[smem(), smem()] + [vmem()] * 6,
        out_specs=[vmem()] * 4,
        compiler_params=pltpu.CompilerParams(vmem_limit_bytes=VMEM_LIMIT),
        name="pack",
    )(odd, video, q_in, k_in, v_in, d_out, gq, gk)

    cross = [(i, i + 1) for i in range(1, groups - 1, 2)] + [(i, i - 1) for i in range(2, groups, 2)]
    chip = [(i, i ^ 1) for i in range(groups)]

    def over(value):
        return lax.ppermute(value, AXES, cross)

    def within(value):
        return lax.ppermute(value, AXES, chip)

    x1 = over(a)
    s1 = within(b)
    x2 = over(s1)
    s2 = within(x1)
    x3 = over(s2)
    s3 = within(x2)
    blocks = (a, b, x1, s1, x2, s2, x3, s3)
    marks = (a, x1, s1, x2, s2, x3, s3)
    block_spec = pl.BlockSpec((2 * per * rows, HSIZE), lambda i: (i, 0))
    mark_spec = pl.BlockSpec((MARK_ROWS, HSIZE), lambda i: (2 * heads * rows // MARK_ROWS, 0))
    col_spec = pl.BlockSpec((rows, per * HSIZE), lambda i: (0, i))
    gain_spec = pl.BlockSpec((1, per * HSIZE), lambda i: (0, i))
    still = lambda shape: pl.BlockSpec(shape, lambda i: (0, 0))
    pair_flops = 2 * rows * rows * HSIZE * heads
    stats_shape = (2 * heads, rows)
    tilted, w, u, stats = pl.pallas_call(
        functools.partial(query_kernel, heads, per, factor),
        grid=(steps,),
        out_shape=(
            jax.ShapeDtypeStruct((rows, width), F32),
            jax.ShapeDtypeStruct((steps, per, HSIZE), F32),
            wide,
            jax.ShapeDtypeStruct(stats_shape, F32),
        ),
        in_specs=[smem()] + [block_spec] * 8 + [mark_spec] * 7 + [col_spec, gain_spec, still((rows, HSIZE))],
        out_specs=[
            col_spec,
            pl.BlockSpec((1, per, HSIZE), lambda i: (i, 0, 0)),
            still((rows, HSIZE)),
            still(stats_shape),
        ],
        scratch_shapes=[pltpu.VMEM((rows, HSIZE), F32)],
        compiler_params=params,
        cost_estimate=pl.CostEstimate(flops=12 * pair_flops, bytes_accessed=8 * 2**20, transcendentals=0),
        name="query_side",
    )(odd, *blocks, *marks, q_in, gq, rq)

    dp, seq = lax.axis_size("dp"), lax.axis_size("seq")
    w = w.reshape(heads, HSIZE)
    w = lax.all_to_all(jnp.broadcast_to(w[None], (dp, heads, HSIZE)), "dp", 0, 0)
    w = jnp.sum(w, axis=0).astype(BF16)
    w = lax.all_to_all(jnp.broadcast_to(w[None], (seq, heads, HSIZE)), "seq", 0, 0)
    dgain_q = jnp.sum(w.astype(F32), axis=0).reshape(width)
    dgain_k = dgain_q * gain_q / gain_k

    from_one = lax.ppermute(stats, AXES, [(i, i - 1) for i in range(1, groups)])
    from_two = lax.ppermute(stats, AXES, [(i, i - 2) for i in range(2, groups)])
    from_three = lax.ppermute(stats, AXES, [(i, i - 3) for i in range(3, groups)])

    dk_in, dv_in = pl.pallas_call(
        functools.partial(key_kernel, heads, per, factor),
        grid=(steps,),
        out_shape=(
            jax.ShapeDtypeStruct((rows, width), BF16),
            jax.ShapeDtypeStruct((rows, width), BF16),
        ),
        in_specs=[smem()] + [block_spec] * 8 + [mark_spec] * 7 + [still(stats_shape)] * 4
        + [still((rows, width)), still((1, width)), still((rows, HSIZE))],
        out_specs=[still((rows, width)), col_spec],
        scratch_shapes=[pltpu.VMEM((rows, width), F32), pltpu.VMEM((rows, HSIZE), F32)],
        compiler_params=params,
        cost_estimate=pl.CostEstimate(flops=16 * pair_flops, bytes_accessed=8 * 2**20, transcendentals=0),
        name="key_side",
    )(odd, *blocks, *marks, stats, from_one, from_two, from_three, k_in, gk, rk)

    dq_in = pl.pallas_call(
        functools.partial(close_kernel, heads),
        out_shape=jax.ShapeDtypeStruct((rows, width), BF16),
        in_specs=[vmem()] * 4,
        out_specs=vmem(),
        compiler_params=pltpu.CompilerParams(vmem_limit_bytes=VMEM_LIMIT),
        name="close_q",
    )(q_in, tilted, u, rq)
    return dq_in, dk_in, dv_in, dgain_q, dgain_k


def solution(mesh):
    rows = P(("dp", "seq"), None)
    return jax.shard_map(
        body,
        mesh=mesh,
        in_specs=(rows, rows, rows, P(), P(), rows, P(("dp", "seq"))),
        out_specs=(rows, rows, rows, P(), P()),
        check_vma=False,
    )
```

time: 339 us -> 149 us (0.44)
  the two profiles are of different devices: /device:TPU:1 before, /device:TPU:9 now
where the time goes in v1:
time: 149 us; the launch traced here: 148 us
  starting transfers between devices  61.8 us (41%)
  Pallas kernels  28.9 us (19%)
  waiting for transfers between devices  26.8 us (18%)
  local copies, waits for them, and re-layouts  16.2 us (11%)
  blocking collectives  10.4 us (7%)
  other arithmetic  2.52 us (2%)
  between operations  1.53 us (1%)
    ppermute x3, starting transfers between devices, within(): return lax.ppermute(value, AXES, chip)  28.3 us
    ppermute x3, waiting for transfers between devices, over(): return lax.ppermute(value, AXES, cross)  26.1 us
    pallas_call x1, Pallas kernels, body(): pl.pallas_call(functools.partial(key_kernel, heads, per, factor), grid=(s...  14.3 us
    unnamed x46, local copies, waits for them, and re-layouts  14 us
    pallas_call x1, Pallas kernels, body(): pl.pallas_call(functools.partial(query_kernel, heads, per, factor), grid=...  12.6 us
    all_to_all x1, starting transfers between devices, body(): lax.all_to_all(jnp.broadcast_to(w[None], (seq, heads, HSIZE)), 'seq', 0, 0)  11.6 us
    all_to_all x1, blocking collectives, body(): lax.all_to_all(jnp.broadcast_to(w[None], (dp, heads, HSIZE)), 'dp', 0, 0)  10.4 us
    ppermute x3, starting transfers between devices, over(): return lax.ppermute(value, AXES, cross)  8.99 us
  transfers between devices with their start and end apart: 10, of which 4 were waited for; matrix products, arithmetic and copies ran while one was open for 0% of the time, Pallas kernels for 10%

profile of v1, /device:TPU:9, one launch (start us, length us, event | category | flops | bytes accessed | tf_op | source)
XLA Modules:
  0.0 148.1 jit_solution(1552294517751163547)
XLA Ops:
  1.3 0.7 reshape.27.gq_ref
  2.7 1.1 copy-done.10
  3.8 1.1 copy-done.14
  4.9 1.1 copy-done.18
  6.0 1.1 copy-done.19
  7.1 0.9 pack.1
  8.0 4.1 %collective-permute-start = (bf16[5136,128]{1,0:T(8,128)(2,1)S(1)}, bf16[5136,128]{1,0:T(8,128)(2,1)S(1)}, u32[]{:S(2)}, u32[]{:S(2)}) collective-permute-start(bf16[5136,128]{1,0:T(8,128)(2,1)S(1)} %get-tuple-element.15.a.am), channel_id=1, source_target_pairs={{1,2},{3,4},{5,6},{7,8},{9,10},{11,12},{13,14},{15,16},{17,18},{19... | collective-permute-start | bytes 3944456 | tf_op jit(solution)/shard_map/ppermute | solution.py:221
  12.1 11.4 %collective-permute-start.1 = (bf16[5136,128]{1,0:T(8,128)(2,1)S(1)}, bf16[5136,128]{1,0:T(8,128)(2,1)S(1)}, u32[]{:S(2)}, u32[]{:S(2)}) collective-permute-start(bf16[5136,128]{1,0:T(8,128)(2,1)S(1)} %get-tuple-element.16.b), channel_id=1, source_target_pairs={{0,1},{1,0},{2,3},{3,2},{4,5},{5,4},{6,7},{7,6},{8,9},{9,8},{10,11... | collective-permute-start | bytes 3944456 | tf_op jit(solution)/shard_map/ppermute | solution.py:224
  23.5 4.2 %collective-permute-done.x1.x1m = bf16[5136,128]{1,0:T(8,128)(2,1)S(1)} collective-permute-done((bf16[5136,128]{1,0:T(8,128)(2,1)S(1)}, bf16[5136,128]{1,0:T(8,128)(2,1)S(1)}, u32[]{:S(2)}, u32[]{:S(2)}) %collective-permute-start) | collective-permute-done | bytes 1314848 | tf_op jit(solution)/shard_map/ppermute | solution.py:221
  27.7 11.1 %collective-permute-start.3 = (bf16[5136,128]{1,0:T(8,128)(2,1)S(1)}, bf16[5136,128]{1,0:T(8,128)(2,1)S(1)}, u32[]{:S(2)}, u32[]{:S(2)}) collective-permute-start(bf16[5136,128]{1,0:T(8,128)(2,1)S(1)} %collective-permute-done.x1.x1m), channel_id=1, source_target_pairs={{0,1},{1,0},{2,3},{3,2},{4,5},{5,4},{6,7},{7,6},{8,9},{9,8},{10,11... | collective-permute-start | bytes 3944456 | tf_op jit(solution)/shard_map/ppermute | solution.py:224
  38.8 1.9 %collective-permute-start.2 = (bf16[5136,128]{1,0:T(8,128)(2,1)S(1)}, bf16[5136,128]{1,0:T(8,128)(2,1)S(1)}, u32[]{:S(2)}, u32[]{:S(2)}) collective-permute-start(bf16[5136,128]{1,0:T(8,128)(2,1)S(1)} %collective-permute-done.1.s1.s1m), channel_id=1, source_target_pairs={{1,2},{3,4},{5,6},{7,8},{9,10},{11,12},{13,14},{15,16},{17,18},{19... | collective-permute-start | bytes 3944456 | tf_op jit(solution)/shard_map/ppermute | solution.py:221
  41.5 3.0 %collective-permute-start.4 = (bf16[5136,128]{1,0:T(8,128)(2,1)S(1)}, bf16[5136,128]{1,0:T(8,128)(2,1)S(1)}, u32[]{:S(2)}, u32[]{:S(2)}) collective-permute-start(bf16[5136,128]{1,0:T(8,128)(2,1)S(1)} %collective-permute-done.3.s2.s2m), channel_id=1, source_target_pairs={{1,2},{3,4},{5,6},{7,8},{9,10},{11,12},{13,14},{15,16},{17,18},{19... | collective-permute-start | bytes 3944456 | tf_op jit(solution)/shard_map/ppermute | solution.py:221
  44.4 13.7 %collective-permute-done.2.x2.x2m = bf16[5136,128]{1,0:T(8,128)(2,1)S(1)} collective-permute-done((bf16[5136,128]{1,0:T(8,128)(2,1)S(1)}, bf16[5136,128]{1,0:T(8,128)(2,1)S(1)}, u32[]{:S(2)}, u32[]{:S(2)}) %collective-permute-start.2) | collective-permute-done | bytes 1314848 | tf_op jit(solution)/shard_map/ppermute | solution.py:221
  58.1 5.8 %collective-permute-start.5 = (bf16[5136,128]{1,0:T(8,128)(2,1)S(1)}, bf16[5136,128]{1,0:T(8,128)(2,1)S(1)}, u32[]{:S(2)}, u32[]{:S(2)}) collective-permute-start(bf16[5136,128]{1,0:T(8,128)(2,1)S(1)} %collective-permute-done.2.x2.x2m), channel_id=1, source_target_pairs={{0,1},{1,0},{2,3},{3,2},{4,5},{5,4},{6,7},{7,6},{8,9},{9,8},{10,11... | collective-permute-start | bytes 3944456 | tf_op jit(solution)/shard_map/ppermute | solution.py:224
  63.9 8.2 %collective-permute-done.4.x3.x3m = bf16[5136,128]{1,0:T(8,128)(2,1)S(1)} collective-permute-done((bf16[5136,128]{1,0:T(8,128)(2,1)S(1)}, bf16[5136,128]{1,0:T(8,128)(2,1)S(1)}, u32[]{:S(2)}, u32[]{:S(2)}) %collective-permute-start.4) | collective-permute-done | bytes 1314848 | tf_op jit(solution)/shard_map/ppermute | solution.py:221
  72.2 12.6 %query_side.1 = (f32[128,2560]{1,0:T(8,128)S(1)}, f32[5,4,128]{2,1,0:T(4,128)S(1)}, f32[128,128]{1,0:T(8,128)S(1)}, f32[40,128]{1,0:T(8,128)S(1)}) custom-call(s32[1]{0:T(128)} %bitcast.odd_ref, bf16[5136,128]{1,0:T(8,128)(2,1)S(1)} %get-tuple-element.15.a.am, bf16[5136,128]{1,0:T(8,128)(2,1)S(1)} %get-tuple-element.16.b, ...), custom_call_target="tpu_custom_call" | custom-call | flops 1006632960 | bytes 8388608 | tf_op jit(solution)/shard_map/query_side/pallas_call | solution.py:241
  84.9 1.1 copy-done.16
  86.0 10.4 %all_to_all.10 = f32[16,20,128]{2,1,0:T(8,128)} all-to-all(f32[16,20,128]{2,1,0:T(8,128)S(1)} %broadcast_in_dim.14), channel_id=1, replica_groups=mesh['dp'=16,'seq'=32] {'dp'}, dimensions={0} | all-to-all | bytes 327680 | tf_op jit(solution)/shard_map/all_to_all | solution.py:265
  96.4 0.9 reduce_sum.18
  98.1 11.6 %all-to-all-start.1 = ((bf16[32,20,128]{2,1,0:T(8,128)(2,1)}), bf16[32,20,128]{2,1,0:T(8,128)(2,1)}, u32[]{:S(2)}, u32[]{:S(2)}) async-start(bf16[32,20,128]{2,1,0:T(8,128)(2,1)} %broadcast_in_dim.15), calls=%async_computation.1 | async-start | bytes 393216 | tf_op jit(solution)/shard_map/all_to_all | solution.py:267
  109.7 6.6 %collective-permute-start.8 = (f32[40,128]{1,0:T(8,128)S(1)}, f32[40,128]{1,0:T(8,128)S(1)}, u32[]{:S(2)}, u32[]{:S(2)}) collective-permute-start(f32[40,128]{1,0:T(8,128)S(1)} %get-tuple-element.20.t0_ref), channel_id=1, source_target_pairs={{3,0},{4,1},{5,2},{6,3},{7,4},{8,5},{9,6},{10,7},{11,8},{12,9},{13... | collective-permute-start | bytes 61448 | tf_op jit(solution)/shard_map/ppermute | solution.py:273
  116.3 3.1 %collective-permute-start.7 = (f32[40,128]{1,0:T(8,128)S(1)}, f32[40,128]{1,0:T(8,128)S(1)}, u32[]{:S(2)}, u32[]{:S(2)}) collective-permute-start(f32[40,128]{1,0:T(8,128)S(1)} %get-tuple-element.20.t0_ref), channel_id=1, source_target_pairs={{2,0},{3,1},{4,2},{5,3},{6,4},{7,5},{8,6},{9,7},{10,8},{11,9},{12,... | collective-permute-start | bytes 61448 | tf_op jit(solution)/shard_map/ppermute | solution.py:272
  119.4 3.2 %collective-permute-start.6 = (f32[40,128]{1,0:T(8,128)S(1)}, f32[40,128]{1,0:T(8,128)S(1)}, u32[]{:S(2)}, u32[]{:S(2)}) collective-permute-start(f32[40,128]{1,0:T(8,128)S(1)} %get-tuple-element.20.t0_ref), channel_id=1, source_target_pairs={{1,0},{2,1},{3,2},{4,3},{5,4},{6,5},{7,6},{8,7},{9,8},{10,9},{11,1... | collective-permute-start | bytes 61448 | tf_op jit(solution)/shard_map/ppermute | solution.py:271
  122.6 1.3 copy-done.17
  123.9 1.1 close_q.1
  125.9 1.3 copy-done.5
  127.2 1.3 copy-done.7
  128.5 1.3 copy-done.9
  129.8 1.3 copy-done.13
  131.2 1.1 copy-done.15
  132.3 14.3 %key_side.1 = (bf16[128,2560]{1,0:T(8,128)(2,1)}, bf16[128,2560]{1,0:T(8,128)(2,1)}) custom-call(s32[1]{0:T(128)} %bitcast.odd_ref, bf16[5136,128]{1,0:T(8,128)(2,1)S(1)} %get-tuple-element.15.a.am, bf16[5136,128]{1,0:T(8,128)(2,1)S(1)} %copy-done.13, bf16[5136,128]{1,0:T(8,128)(2,1)S(1)} %collective-permute-done.x1.x1m, bf16[5136,128]{1,0:T(8,128)(2,1)S(1)} %copy-done.1, ...), custom_call_target="tpu_custom_call" | custom-call | flops 1342177280 | bytes 8388608 | tf_op jit(solution)/shard_map/key_side/pallas_call | solution.py:275
  146.5 1.0 convert_reduce_fusion
  (47 shorter events, 3.6 us)
Async XLA Ops:
  2.7 1.1 copy-start.10
  3.8 1.1 copy-start.14
  4.9 1.1 copy-start.18
  6.0 1.1 copy-start.19
  8.0 76.8 %copy-start.12 = (bf16[5136,128]{1,0:T(8,128)(2,1)}, bf16[5136,128]{1,0:T(8,128)(2,1)S(1)}, u32[]{:S(2)}) copy-start(bf16[5136,128]{1,0:T(8,128)(2,1)S(1)} %get-tuple-element.16.b) | copy-start | bytes 3944452
  8.0 19.7 %collective-permute-start = (bf16[5136,128]{1,0:T(8,128)(2,1)S(1)}, bf16[5136,128]{1,0:T(8,128)(2,1)S(1)}, u32[]{:S(2)}, u32[]{:S(2)}) collective-permute-start(bf16[5136,128]{1,0:T(8,128)(2,1)S(1)} %get-tuple-element.15.a.am), channel_id=1, source_target_pairs={{1,2},{3,4},{5,6},{7,8},{9,10},{11,12},{13,14},{15,16},{17,18},{19... | collective-permute-start | bytes 3944456 | tf_op jit(solution)/shard_map/ppermute | solution.py:221
  12.1 26.7 %collective-permute-start.1 = (bf16[5136,128]{1,0:T(8,128)(2,1)S(1)}, bf16[5136,128]{1,0:T(8,128)(2,1)S(1)}, u32[]{:S(2)}, u32[]{:S(2)}) collective-permute-start(bf16[5136,128]{1,0:T(8,128)(2,1)S(1)} %get-tuple-element.16.b), channel_id=1, source_target_pairs={{0,1},{1,0},{2,3},{3,2},{4,5},{5,4},{6,7},{7,6},{8,9},{9,8},{10,11... | collective-permute-start | bytes 3944456 | tf_op jit(solution)/shard_map/ppermute | solution.py:224
  27.7 13.7 %collective-permute-start.3 = (bf16[5136,128]{1,0:T(8,128)(2,1)S(1)}, bf16[5136,128]{1,0:T(8,128)(2,1)S(1)}, u32[]{:S(2)}, u32[]{:S(2)}) collective-permute-start(bf16[5136,128]{1,0:T(8,128)(2,1)S(1)} %collective-permute-done.x1.x1m), channel_id=1, source_target_pairs={{0,1},{1,0},{2,3},{3,2},{4,5},{5,4},{6,7},{7,6},{8,9},{9,8},{10,11... | collective-permute-start | bytes 3944456 | tf_op jit(solution)/shard_map/ppermute | solution.py:224
  38.8 46.0 %copy-start = (bf16[5136,128]{1,0:T(8,128)(2,1)}, bf16[5136,128]{1,0:T(8,128)(2,1)S(1)}, u32[]{:S(2)}) copy-start(bf16[5136,128]{1,0:T(8,128)(2,1)S(1)} %collective-permute-done.1.s1.s1m) | copy-start | bytes 3944452
  38.8 19.3 %collective-permute-start.2 = (bf16[5136,128]{1,0:T(8,128)(2,1)S(1)}, bf16[5136,128]{1,0:T(8,128)(2,1)S(1)}, u32[]{:S(2)}, u32[]{:S(2)}) collective-permute-start(bf16[5136,128]{1,0:T(8,128)(2,1)S(1)} %collective-permute-done.1.s1.s1m), channel_id=1, source_target_pairs={{1,2},{3,4},{5,6},{7,8},{9,10},{11,12},{13,14},{15,16},{17,18},{19... | collective-permute-start | bytes 3944456 | tf_op jit(solution)/shard_map/ppermute | solution.py:221
  41.5 43.4 %copy-start.2 = (bf16[5136,128]{1,0:T(8,128)(2,1)}, bf16[5136,128]{1,0:T(8,128)(2,1)S(1)}, u32[]{:S(2)}) copy-start(bf16[5136,128]{1,0:T(8,128)(2,1)S(1)} %collective-permute-done.3.s2.s2m) | copy-start | bytes 3944452
  41.5 30.7 %collective-permute-start.4 = (bf16[5136,128]{1,0:T(8,128)(2,1)S(1)}, bf16[5136,128]{1,0:T(8,128)(2,1)S(1)}, u32[]{:S(2)}, u32[]{:S(2)}) collective-permute-start(bf16[5136,128]{1,0:T(8,128)(2,1)S(1)} %collective-permute-done.3.s2.s2m), channel_id=1, source_target_pairs={{1,2},{3,4},{5,6},{7,8},{9,10},{11,12},{13,14},{15,16},{17,18},{19... | collective-permute-start | bytes 3944456 | tf_op jit(solution)/shard_map/ppermute | solution.py:221
  58.1 26.7 %copy-start.4 = (bf16[5136,128]{1,0:T(8,128)(2,1)}, bf16[5136,128]{1,0:T(8,128)(2,1)S(1)}, u32[]{:S(2)}) copy-start(bf16[5136,128]{1,0:T(8,128)(2,1)S(1)} %collective-permute-done.2.x2.x2m) | copy-start | bytes 3944452
  58.1 14.1 %collective-permute-start.5 = (bf16[5136,128]{1,0:T(8,128)(2,1)S(1)}, bf16[5136,128]{1,0:T(8,128)(2,1)S(1)}, u32[]{:S(2)}, u32[]{:S(2)}) collective-permute-start(bf16[5136,128]{1,0:T(8,128)(2,1)S(1)} %collective-permute-done.2.x2.x2m), channel_id=1, source_target_pairs={{0,1},{1,0},{2,3},{3,2},{4,5},{5,4},{6,7},{7,6},{8,9},{9,8},{10,11... | collective-permute-start | bytes 3944456 | tf_op jit(solution)/shard_map/ppermute | solution.py:224
  72.2 12.7 %copy-start.6 = (bf16[5136,128]{1,0:T(8,128)(2,1)}, bf16[5136,128]{1,0:T(8,128)(2,1)S(1)}, u32[]{:S(2)}) copy-start(bf16[5136,128]{1,0:T(8,128)(2,1)S(1)} %collective-permute-done.4.x3.x3m) | copy-start | bytes 3944452
  72.2 12.7 %copy-start.8 = (bf16[5136,128]{1,0:T(8,128)(2,1)}, bf16[5136,128]{1,0:T(8,128)(2,1)S(1)}, u32[]{:S(2)}) copy-start(bf16[5136,128]{1,0:T(8,128)(2,1)S(1)} %collective-permute-done.5.s3.s3m) | copy-start | bytes 3944452
  84.9 1.1 copy-start.16
  86.0 36.6 %copy-start.11 = (bf16[128,2560]{1,0:T(8,128)(2,1)S(1)}, bf16[128,2560]{1,0:T(8,128)(2,1)}, u32[]{:S(2)}) copy-start(bf16[128,2560]{1,0:T(8,128)(2,1)} %q_ref.5) | copy-start | bytes 1966084
  98.1 48.5 %all-to-all-start.1 = ((bf16[32,20,128]{2,1,0:T(8,128)(2,1)}), bf16[32,20,128]{2,1,0:T(8,128)(2,1)}, u32[]{:S(2)}, u32[]{:S(2)}) async-start(bf16[32,20,128]{2,1,0:T(8,128)(2,1)} %broadcast_in_dim.15), calls=%async_computation.1 | async-start | bytes 393216 | tf_op jit(solution)/shard_map/all_to_all | solution.py:267
  109.7 15.4 %collective-permute-start.8 = (f32[40,128]{1,0:T(8,128)S(1)}, f32[40,128]{1,0:T(8,128)S(1)}, u32[]{:S(2)}, u32[]{:S(2)}) collective-permute-start(f32[40,128]{1,0:T(8,128)S(1)} %get-tuple-element.20.t0_ref), channel_id=1, source_target_pairs={{3,0},{4,1},{5,2},{6,3},{7,4},{8,5},{9,6},{10,7},{11,8},{12,9},{13... | collective-permute-start | bytes 61448 | tf_op jit(solution)/shard_map/ppermute | solution.py:273
  116.3 8.8 %collective-permute-start.7 = (f32[40,128]{1,0:T(8,128)S(1)}, f32[40,128]{1,0:T(8,128)S(1)}, u32[]{:S(2)}, u32[]{:S(2)}) collective-permute-start(f32[40,128]{1,0:T(8,128)S(1)} %get-tuple-element.20.t0_ref), channel_id=1, source_target_pairs={{2,0},{3,1},{4,2},{5,3},{6,4},{7,5},{8,6},{9,7},{10,8},{11,9},{12,... | collective-permute-start | bytes 61448 | tf_op jit(solution)/shard_map/ppermute | solution.py:272
  119.4 5.7 %collective-permute-start.6 = (f32[40,128]{1,0:T(8,128)S(1)}, f32[40,128]{1,0:T(8,128)S(1)}, u32[]{:S(2)}, u32[]{:S(2)}) collective-permute-start(f32[40,128]{1,0:T(8,128)S(1)} %get-tuple-element.20.t0_ref), channel_id=1, source_target_pairs={{1,0},{2,1},{3,2},{4,3},{5,4},{6,5},{7,6},{8,7},{9,8},{10,9},{11,1... | collective-permute-start | bytes 61448 | tf_op jit(solution)/shard_map/ppermute | solution.py:271
  122.6 1.3 copy-start.17
  123.9 1.5 %copy-start.1 = (bf16[5136,128]{1,0:T(8,128)(2,1)S(1)}, bf16[5136,128]{1,0:T(8,128)(2,1)}, u32[]{:S(2)}) copy-start(bf16[5136,128]{1,0:T(8,128)(2,1)} %copy-done) | copy-start | bytes 3944452
  123.9 1.9 %copy-start.3 = (bf16[5136,128]{1,0:T(8,128)(2,1)S(1)}, bf16[5136,128]{1,0:T(8,128)(2,1)}, u32[]{:S(2)}) copy-start(bf16[5136,128]{1,0:T(8,128)(2,1)} %copy-done.2) | copy-start | bytes 3944452
  125.9 1.3 copy-start.5
  127.2 1.3 copy-start.7
  128.5 1.3 copy-start.9
  129.8 1.3 copy-start.13
  131.2 1.1 copy-start.15
  132.2 15.3 %copy-start.21 = (f32[2560]{0:T(1024)S(1)}, f32[2560]{0:T(1024)}, u32[]{:S(2)}) copy-start(f32[2560]{0:T(1024)} %param.10) | copy-start | bytes 30724
  132.2 15.3 %copy-start.22 = (f32[2560]{0:T(1024)S(1)}, f32[2560]{0:T(1024)}, u32[]{:S(2)}) copy-start(f32[2560]{0:T(1024)} %param.11) | copy-start | bytes 30724
  (1 other events, 0.6 us)

commit v2 on v0

v2 whole, which is shorter than its diff:
```python
import functools
import math

import jax
import jax.numpy as jnp
from jax import lax
from jax.experimental import pallas as pl
from jax.experimental.pallas import tpu as pltpu
from jax.sharding import Mesh
from jax.sharding import PartitionSpec as P

HSIZE = 128
WIN = 4
EPS = 1e-06
NEG = -1e30
MARK_ROWS = 16
PER = 5
SPLIT = 4
AXES = ("dp", "z", "core")
CORES = 2
VMEM_LIMIT = 63 * 1024 * 1024
F32 = jnp.float32
BF16 = jnp.bfloat16


def dot_nt(a, b):
    return lax.dot_general(a, b, (((1,), (1,)), ((), ())), preferred_element_type=F32)


def dot_nn(a, b):
    return lax.dot_general(a, b, (((1,), (0,)), ((), ())), preferred_element_type=F32)


def head_rows(j, rows):
    return slice(j * rows, (j + 1) * rows)


def head_cols(j):
    return slice(j * HSIZE, (j + 1) * HSIZE)


def pack_kernel(heads, odd_ref, video_ref, q_hbm, k_hbm, d_hbm, v_hbm, gq_hbm, gk_hbm,
                a_hbm, b_hbm, rq_ref, rk_ref, main, stage, gain, mark, in_sems, out_sems):
    odd = odd_ref[0] == 1
    rows, width = q_hbm.shape
    size = rows // SPLIT
    steps = heads // PER
    span = PER * rows

    def load(which, src):
        return [
            pltpu.make_async_copy(
                src.at[pl.ds(part * size, size), :], main.at[which, pl.ds(part * size, size), :], in_sems.at[which, part]
            )
            for part in range(SPLIT)
        ]

    loads = [load(which, src) for which, src in enumerate((q_hbm, k_hbm, d_hbm, v_hbm))]
    gains = [
        pltpu.make_async_copy(src, gain.at[which], in_sems.at[which, SPLIT]) for which, src in enumerate((gq_hbm, gk_hbm))
    ]
    for copy in gains + loads[0] + loads[1] + loads[2] + loads[3]:
        copy.start()

    def store(which, step, dst):
        if step == steps:
            return pltpu.make_async_copy(
                mark, dst.at[pl.ds(2 * steps * span, MARK_ROWS), :], out_sems.at[which, steps]
            )
        return pltpu.make_async_copy(
            stage.at[which, pl.ds(step * span, span), :],
            dst.at[pl.ds((2 * step + which // 2) * span, span), :],
            out_sems.at[which, step],
        )

    def start_store(which, step):
        with_a = odd == (which % 2 == 1)

        @pl.when(with_a)
        def _():
            store(which, step, a_hbm).start()

        @pl.when(jnp.logical_not(with_a))
        def _():
            store(which, step, b_hbm).start()

    mark[...] = jnp.full((MARK_ROWS, HSIZE), (video_ref[0] + 1).astype(F32), F32).astype(BF16)
    for which in range(2):
        start_store(which, steps)
    for copy in gains:
        copy.wait()
    for which, scale_ref in enumerate((rq_ref, rk_ref)):
        for copy in loads[which]:
            copy.wait()
        raw = main[which].astype(F32)
        scale = lax.rsqrt(jnp.sum(raw * raw, axis=-1, keepdims=True) * (1.0 / width) + EPS)
        scale_ref[...] = jnp.broadcast_to(scale, scale_ref.shape)
        for step in range(steps):
            for h in range(step * PER, (step + 1) * PER):
                normed = main[which, :, head_cols(h)].astype(F32) * scale * gain[which, h : h + 1, :]
                stage[which, head_rows(h, rows), :] = normed.astype(BF16)
            start_store(which, step)
    for which in (2, 3):
        for copy in loads[which]:
            copy.wait()
        for step in range(steps):
            for h in range(step * PER, (step + 1) * PER):
                stage[which, head_rows(h, rows), :] = main[which, :, head_cols(h)]
            start_store(which, step)
    for which in range(4):
        for step in range(steps + (which < 2)):
            store(which, step, a_hbm).wait()


def gate_kernel(*refs):
    del refs


def mark_of(ref):
    return ref[0:1, 0:1].astype(F32)


def bias_of(own_ref, odd, if_odd, if_even):
    mark = jnp.where(odd, mark_of(if_odd), mark_of(if_even))
    return jnp.where(mark == mark_of(own_ref), 0.0, NEG)


def bias_row(biases, rows):
    return jnp.concatenate([jnp.broadcast_to(bias, (1, rows)) for bias in biases], axis=1)


def near_kernel(rows, factor, odd_ref, a, b, x1, s1, x2, s2, am, x1m, s1m, x2m, s2m, g_ref, h_ref, part_ref):
    odd = odd_ref[0] == 1
    bias = bias_row([jnp.zeros((1, 1), F32), bias_of(am, odd, s1m, x1m), bias_of(am, odd, s2m, x2m)], rows)
    pairs = ((a, b), (s1, x1), (s2, x2))
    lane = lax.broadcasted_iota(jnp.int32, (rows, HSIZE), 1)
    keys, scores, dprobs = [], [], []
    for j in range(PER):
        top = head_rows(j, rows)
        low = head_rows(PER + j, rows)
        q = jnp.where(odd, b[top, :], a[top, :])
        d_out = jnp.where(odd, b[low, :], a[low, :])
        keys.append(jnp.concatenate([jnp.where(odd, o[top, :], e[top, :]) for o, e in pairs], axis=0))
        vals = jnp.concatenate([jnp.where(odd, o[low, :], e[low, :]) for o, e in pairs], axis=0)
        scores.append(dot_nt(q, keys[j]))
        dprobs.append(dot_nt(d_out, vals))
    part = jnp.zeros((rows, HSIZE), F32)
    for j in range(PER):
        out = head_rows(j, rows)
        score = scores[j] * factor + bias
        best = jnp.max(score, axis=-1, keepdims=True)
        probs = jnp.exp2(score - best)
        total = jnp.sum(probs, axis=-1, keepdims=True)
        delta = jnp.sum(probs * dprobs[j], axis=-1, keepdims=True) / total
        both = jnp.concatenate([(probs * (dprobs[j] - delta)).astype(BF16), probs.astype(BF16)], axis=0)
        sums = dot_nn(both, keys[j])
        g_ref[out, :] = sums[:rows]
        h_ref[out, :] = sums[rows:]
        for place, value in enumerate((best, total, delta)):
            part = jnp.where(lane == 3 * j + place, value, part)
    part_ref[0] = part


def query_kernel(rows, steps, factor, odd_ref, a, b, x3, s3, am, x3m, s3m, g_ref, h_ref, part_ref,
                 q_ref, gq_ref, rq_ref, dq_ref, w_ref, stat_ref, u_acc, acc_lse, acc_delta, acc_w, tilt):
    step = pl.program_id(0)
    heads = steps * PER
    width = q_ref.shape[1]
    odd = odd_ref[0] == 1
    bias = bias_of(am, odd, s3m, x3m)
    rq = rq_ref[...]
    lane = lax.broadcasted_iota(jnp.int32, (rows, HSIZE), 1)
    scale = 1.0 / math.sqrt(HSIZE)

    @pl.when(step == 0)
    def _():
        u_acc[...] = jnp.zeros_like(u_acc)
        acc_lse[...] = jnp.zeros_like(acc_lse)
        acc_delta[...] = jnp.zeros_like(acc_delta)

    keys, scores, dprobs = [], [], []
    for j in range(PER):
        top = head_rows(j, rows)
        low = head_rows(PER + j, rows)
        q = jnp.where(odd, b[top, :], a[top, :])
        d_out = jnp.where(odd, b[low, :], a[low, :])
        keys.append(jnp.where(odd, s3[top, :], x3[top, :]))
        vals = jnp.where(odd, s3[low, :], x3[low, :])
        scores.append(dot_nt(q, keys[j]))
        dprobs.append(dot_nt(d_out, vals))
    lse = acc_lse[...]
    deltas = acc_delta[...]
    fars, nears = [], []
    for j in range(PER):
        old_best, old_total, old_delta = [
            jnp.sum(jnp.where(lane == 3 * j + place, part_ref[0], 0.0), axis=-1, keepdims=True) for place in range(3)
        ]
        score = scores[j] * factor + bias
        best = jnp.maximum(old_best, jnp.max(score, axis=-1, keepdims=True))
        prob = jnp.exp2(score - best)
        shrink = jnp.exp2(old_best - best)
        old_total = old_total * shrink
        total = old_total + jnp.sum(prob, axis=-1, keepdims=True)
        inverse = 1.0 / total
        delta = (old_total * old_delta + jnp.sum(prob * dprobs[j], axis=-1, keepdims=True)) * inverse
        fars.append(((prob * inverse) * (dprobs[j] - delta)).astype(BF16))
        nears.append((shrink * inverse, old_delta - delta))
        head = step * PER + j
        lse = jnp.where(lane == head, best + jnp.log2(total), lse)
        deltas = jnp.where(lane == head, delta, deltas)
    acc_lse[...] = lse
    acc_delta[...] = deltas
    u_sum = u_acc[...]
    for j in range(PER):
        out = head_rows(j, rows)
        head = step * PER + j
        cols = pl.ds(pl.multiple_of(head * HSIZE, HSIZE), HSIZE)
        part, moved = nears[j]
        dq = (dot_nn(fars[j], keys[j]) + part * (g_ref[out, :] + moved * h_ref[out, :])) * scale
        raw = q_ref[:, cols].astype(F32)
        tilted = dq * gq_ref[pl.ds(head, 1), :]
        tilt[:, cols] = tilted
        u_sum = u_sum + raw * tilted
        acc_w[pl.ds(head, 1), :] = jnp.sum(dq * (raw * rq), axis=0, keepdims=True)
    u_acc[...] = u_sum

    @pl.when(step == steps - 1)
    def _():
        stat_ref[:heads, :] = jnp.transpose(acc_lse[...])[:heads, :]
        stat_ref[heads:, :] = jnp.transpose(acc_delta[...])[:heads, :]
        w_ref[...] = jnp.broadcast_to(acc_w[...].astype(BF16)[None], w_ref.shape)
        low_part = rq * rq * rq * jnp.sum(u_sum, axis=-1, keepdims=True) * (1.0 / width)
        for h in range(heads):
            cols = head_cols(h)
            dq_ref[:, cols] = (rq * tilt[:, cols] - q_ref[:, cols].astype(F32) * low_part).astype(BF16)


def key_kernel(rows, steps, factor, odd_ref, a, b, x1, s1, x2, s2, x3, s3, am, x1m, s1m, x2m, s2m, x3m, s3m,
               t0_ref, t1_ref, t2_ref, t3_ref, k_ref, gk_ref, rk_ref, dk_ref, dv_ref, tilt, u_acc):
    step = pl.program_id(0)
    heads = steps * PER
    odd = odd_ref[0] == 1
    width = k_ref.shape[1]
    bias = bias_row(
        [jnp.zeros((1, 1), F32), bias_of(am, odd, x1m, s1m), bias_of(am, odd, x2m, s2m), bias_of(am, odd, x3m, s3m)],
        rows,
    )
    scale = 1.0 / math.sqrt(HSIZE)
    pairs = ((b, a), (x1, s1), (x2, s2), (x3, s3))
    stats = (t0_ref, t1_ref, t2_ref, t3_ref)

    @pl.when(step == 0)
    def _():
        u_acc[...] = jnp.zeros_like(u_acc)

    for j in range(PER):
        top = head_rows(j, rows)
        low = head_rows(PER + j, rows)
        head = step * PER + j
        key = jnp.where(odd, a[top, :], b[top, :])
        val = jnp.where(odd, a[low, :], b[low, :])
        queries = jnp.concatenate([jnp.where(odd, o[top, :], e[top, :]) for o, e in pairs], axis=0)
        d_outs = jnp.concatenate([jnp.where(odd, o[low, :], e[low, :]) for o, e in pairs], axis=0)
        log_total = jnp.concatenate([stat[pl.ds(head, 1), :] for stat in stats], axis=1)
        delta = jnp.concatenate([stat[pl.ds(head + heads, 1), :] for stat in stats], axis=1)
        probs = jnp.exp2(dot_nt(key, queries) * factor + (bias - log_total))
        dscores = probs * (dot_nt(val, d_outs) - delta)
        dv_ref[:, head_cols(j)] = dot_nn(probs.astype(BF16), d_outs).astype(BF16)
        cols = pl.ds(pl.multiple_of(head * HSIZE, HSIZE), HSIZE)
        tilted = dot_nn(dscores.astype(BF16), queries) * (scale * gk_ref[pl.ds(head, 1), :])
        tilt[:, cols] = tilted
        u_acc[...] += k_ref[:, cols].astype(F32) * tilted

    @pl.when(step == steps - 1)
    def _():
        rk = rk_ref[...]
        low_part = rk * rk * rk * jnp.sum(u_acc[...], axis=-1, keepdims=True) * (1.0 / width)
        for h in range(heads):
            cols = head_cols(h)
            dk_ref[:, cols] = (rk * tilt[:, cols] - k_ref[:, cols].astype(F32) * low_part).astype(BF16)


def spread_kernel(part_ref, one_ref, two_ref, three_ref, out_ref):
    del one_ref, two_ref, three_ref
    out_ref[...] = jnp.broadcast_to(jnp.sum(part_ref[...].astype(F32), axis=0).astype(BF16)[None], out_ref.shape)


def gains_kernel(part_ref, gq_ref, gk_ref, dq_ref, dk_ref):
    total = jnp.sum(part_ref[...].astype(F32), axis=0)
    dq_ref[...] = total
    dk_ref[...] = total * gq_ref[...] / gk_ref[...]


def params(limit=VMEM_LIMIT):
    return pltpu.CompilerParams(vmem_limit_bytes=limit)


def cost(flops, data=2**20):
    return pl.CostEstimate(flops=flops, bytes_accessed=data, transcendentals=0)


def shape(*dims, dtype=F32):
    return jax.ShapeDtypeStruct(dims, dtype)


def still(*dims):
    return pl.BlockSpec(dims, lambda i, odd: (0,) * len(dims))


def head_blocks(rows, used_if=None):
    def place(i, odd):
        if used_if is None:
            return (i, 0)
        return (i * odd[0] if used_if else i * (1 - odd[0]), 0)

    return pl.BlockSpec((PER * rows, HSIZE), place)


def body(q_in, k_in, v_in, gain_q, gain_k, d_out, video):
    rows, width = q_in.shape
    heads = width // HSIZE
    steps = heads // PER
    factor = math.log2(math.e) / math.sqrt(HSIZE)
    near_by, along = lax.axis_size("dp") * CORES, lax.axis_size("z")
    groups = near_by * along
    odd = lax.axis_index("core").astype(jnp.int32).reshape(1)
    gq = gain_q.reshape(heads, HSIZE)
    gk = gain_k.reshape(heads, HSIZE)
    packed_rows = 2 * heads * rows + MARK_ROWS
    pair_flops = 2 * rows * rows * HSIZE * heads
    smem = pl.BlockSpec(memory_space=pltpu.SMEM)
    vmem = pl.BlockSpec(memory_space=pltpu.VMEM)
    hbm = pl.BlockSpec(memory_space=pl.ANY)

    def after(value, *others):
        return pl.pallas_call(
            gate_kernel,
            out_shape=jax.ShapeDtypeStruct(value.shape, value.dtype),
            in_specs=[hbm] * (1 + len(others)),
            out_specs=hbm,
            input_output_aliases={0: 0},
            compiler_params=params(),
            name="gate",
        )(value, *others)

    def gridded(kernel, name, flops, in_specs, out_specs, out_shape, scratch=()):
        return pl.pallas_call(
            kernel,
            grid_spec=pltpu.PrefetchScalarGridSpec(
                num_scalar_prefetch=1, grid=(steps,), in_specs=in_specs, out_specs=out_specs, scratch_shapes=scratch
            ),
            out_shape=out_shape,
            compiler_params=params(),
            cost_estimate=cost(flops),
            name=name,
        )

    packed = shape(packed_rows, HSIZE, dtype=BF16)
    a, b, rq, rk = pl.pallas_call(
        functools.partial(pack_kernel, heads),
        out_shape=(packed, packed, shape(rows, HSIZE), shape(rows, HSIZE)),
        in_specs=[smem, smem] + [hbm] * 6,
        out_specs=(hbm, hbm, vmem, vmem),
        scratch_shapes=[
            pltpu.VMEM((4, rows, width), BF16),
            pltpu.VMEM((4, heads * rows, HSIZE), BF16),
            pltpu.VMEM((2, heads, HSIZE), F32),
            pltpu.VMEM((MARK_ROWS, HSIZE), BF16),
            pltpu.SemaphoreType.DMA((4, SPLIT + 1)),
            pltpu.SemaphoreType.DMA((4, steps + 1)),
        ],
        compiler_params=params(),
        cost_estimate=cost(pair_flops),
        name="pack",
    )(odd, video, q_in, k_in, d_out, v_in, gq, gk)

    cross = [(i, i + 1) for i in range(1, groups - 1, 2)] + [(i, i - 1) for i in range(2, groups, 2)]
    chip = [(i, i ^ 1) for i in range(groups)]
    x1 = lax.ppermute(a, AXES, cross)
    s1 = lax.ppermute(b, AXES, chip)
    x2 = lax.ppermute(s1, AXES, cross)
    x1 = after(x1, s1)
    s2 = lax.ppermute(x1, AXES, chip)
    x3 = lax.ppermute(s2, AXES, cross)
    x2 = after(x2, s2)
    s3 = lax.ppermute(x2, AXES, chip)

    both = head_blocks(2 * rows)
    if_odd = head_blocks(2 * rows, True)
    if_even = head_blocks(2 * rows, False)
    tall = head_blocks(rows)
    mark = pl.BlockSpec((MARK_ROWS, HSIZE), lambda i, odd: (2 * heads * rows // MARK_ROWS, 0))
    cols = pl.BlockSpec((rows, PER * HSIZE), lambda i, odd: (0, i))
    parts = pl.BlockSpec((1, rows, HSIZE), lambda i, odd: (i, 0, 0))
    square = still(rows, HSIZE)
    whole = still(rows, width)
    near = gridded(
        functools.partial(near_kernel, rows, factor), "near", 1024,
        [both, both, if_even, if_odd, if_even, if_odd] + [mark] * 5,
        (tall, tall, parts),
        (shape(heads * rows, HSIZE), shape(heads * rows, HSIZE), shape(steps, rows, HSIZE)),
    )(odd, a, b, x1, s1, x2, s2, a, x1, s1, x2, s2)
    dq_in, w, stats = gridded(
        functools.partial(query_kernel, rows, steps, factor), "query_side", 1024,
        [if_even, if_odd] + [if_even, if_odd] + [mark] * 3
        + [tall, tall, parts, whole, still(heads, HSIZE), square],
        (whole, still(near_by, heads, HSIZE), still(2 * heads, rows)),
        (shape(rows, width, dtype=BF16), shape(near_by, heads, HSIZE, dtype=BF16), shape(2 * heads, rows)),
        [pltpu.VMEM((rows, HSIZE), F32)] * 3 + [pltpu.VMEM((heads, HSIZE), F32), pltpu.VMEM((rows, width), F32)],
    )(odd, a, b, x3, s3, a, x3, s3, *near, q_in, gq, rq)

    def back(value, by):
        return lax.ppermute(value, AXES, [(i, i - by) for i in range(by, groups)])

    w = lax.all_to_all(w, ("dp", "core"), 0, 0)
    later = [back(stats, by) for by in range(1, WIN)]
    w = pl.pallas_call(
        spread_kernel,
        out_shape=shape(along, heads, HSIZE, dtype=BF16),
        in_specs=[vmem] + [hbm] * 3,
        out_specs=vmem,
        compiler_params=params(),
        cost_estimate=cost(2**20),
        name="spread",
    )(w, *later)
    w = lax.all_to_all(w, "z", 0, 0)
    dgain_q, dgain_k = pl.pallas_call(
        gains_kernel,
        out_shape=(shape(heads, HSIZE),) * 2,
        in_specs=[vmem] * 3,
        out_specs=(vmem,) * 2,
        compiler_params=params(),
        cost_estimate=cost(2**20),
        name="gains",
    )(w, gq, gk)

    dk_in, dv_in = gridded(
        functools.partial(key_kernel, rows, steps, factor), "key_side", 16 * pair_flops,
        [both, both] + [if_odd, if_even] * 3 + [mark] * 7 + [still(2 * heads, rows)] * 4
        + [whole, still(heads, HSIZE), square],
        (whole, cols),
        (shape(rows, width, dtype=BF16),) * 2,
        [pltpu.VMEM((rows, width), F32), pltpu.VMEM((rows, HSIZE), F32)],
    )(odd, a, b, x1, s1, x2, s2, x3, s3, a, x1, s1, x2, s2, x3, s3, stats, *later, k_in, gk, rk)
    return dq_in, dk_in, dv_in, dgain_q.reshape(width), dgain_k.reshape(width)


def solution(mesh):
    dp, seq = mesh.devices.shape
    split = Mesh(mesh.devices.reshape(dp, seq // CORES, CORES), AXES)
    rows = P(AXES, None)
    return jax.shard_map(
        body,
        mesh=split,
        in_specs=(rows, rows, rows, P(), P(), rows, P(AXES)),
        out_specs=(rows, rows, rows, P(), P()),
        check_vma=False,
    )
```

time: 339 us -> 125 us (0.37)
  the two profiles are of different devices: /device:TPU:1 before, /device:TPU:39 now
where the time goes in v2:
time: 125 us
  starting transfers between devices  56.6 us (45%)
  waiting for transfers between devices  33.7 us (27%)
  Pallas kernels  30.9 us (25%)
  local copies, waits for them, and re-layouts  1.91 us (2%)
  between operations  1.45 us (1%)
    ppermute x3, starting transfers between devices, back(): return lax.ppermute(value, AXES, [(i, i - by) for i in range(by, groups)])  17.3 us
    ppermute x1, waiting for transfers between devices, body(): x1 = lax.ppermute(a, AXES, cross)  13.7 us
    ppermute x1, waiting for transfers between devices, body(): x2 = lax.ppermute(s1, AXES, cross)  12.9 us
    all_to_all x1, starting transfers between devices, body(): w = lax.all_to_all(w, ('dp', 'core'), 0, 0)  11.8 us
    pallas_call x1, Pallas kernels, body(): gridded(functools.partial(key_kernel, rows, steps, factor), 'key_side', 1...  9.25 us
    ppermute x1, starting transfers between devices, body(): s3 = lax.ppermute(x2, AXES, chip)  7.46 us
    pallas_call x1, Pallas kernels, body(): gridded(functools.partial(near_kernel, rows, factor), 'near', 1024, [both...  7.32 us
    pallas_call x1, Pallas kernels, body(): gridded(functools.partial(query_kernel, rows, steps, factor), 'query_side...  7.2 us
  transfers between devices with their start and end apart: 11, of which 4 were waited for; matrix products, arithmetic and copies ran while one was open for 0% of the time, Pallas kernels for 13%

profile of v2, /device:TPU:39, one launch (start us, length us, event | category | flops | bytes accessed | tf_op | source)
XLA Modules:
  0.0 124.6 jit_solution(13479882492124897119)
XLA Ops:
  1.3 4.0 %pack.1 = (bf16[5136,128]{1,0:T(8,128)(2,1)}, bf16[5136,128]{1,0:T(8,128)(2,1)}, f32[128,128]{1,0:T(8,128)}, f32[128,128]{1,0:T(8,128)}) custom-call(s32[1]{0:T(128)} %bitcast.odd_ref, s32[1]{0:T(128)S(6)} %copy.16.video_ref, bf16[128,2560]{1,0:T(8,128)(2,1)} %q_ref.1, bf16[128,2560]{1,0:T(8,128)(2,1)} %k_ref.1, bf16[128,2560]{1,0:T(8,128)(2,1)} %d_hbm.1, ...), custom_call_target="tpu_custom_call" | custom-call | flops 83886080 | bytes 1048576 | tf_op jit(solution)/shard_map/pack/pallas_call | solution.py:359
  5.3 4.1 %collective-permute-start = (bf16[5136,128]{1,0:T(8,128)(2,1)}, bf16[5136,128]{1,0:T(8,128)(2,1)}, u32[]{:S(2)}, u32[]{:S(2)}) collective-permute-start(bf16[5136,128]{1,0:T(8,128)(2,1)} %get-tuple-element.19.a.am), channel_id=1, source_target_pairs={{1,2},{3,4},{5,6},{7,8},{9,10},{11,12},{13,14},{15,16},{17,18},{19... | collective-permute-start | bytes 3944456 | tf_op jit(solution)/shard_map/ppermute | solution.py:379
  9.4 1.9 %collective-permute-start.1 = (bf16[5136,128]{1,0:T(8,128)(2,1)}, bf16[5136,128]{1,0:T(8,128)(2,1)}, u32[]{:S(2)}, u32[]{:S(2)}) collective-permute-start(bf16[5136,128]{1,0:T(8,128)(2,1)} %get-tuple-element.20.b), channel_id=1, source_target_pairs={{0,1},{1,0},{2,3},{3,2},{4,5},{5,4},{6,7},{7,6},{8,9},{9,8},{10,11... | collective-permute-start | bytes 3944456 | tf_op jit(solution)/shard_map/ppermute | solution.py:380
  11.3 13.7 %collective-permute-done.refs_0_ = bf16[5136,128]{1,0:T(8,128)(2,1)} collective-permute-done((bf16[5136,128]{1,0:T(8,128)(2,1)}, bf16[5136,128]{1,0:T(8,128)(2,1)}, u32[]{:S(2)}, u32[]{:S(2)}) %collective-permute-start) | collective-permute-done | bytes 1314848 | tf_op jit(solution)/shard_map/ppermute | solution.py:379
  25.0 0.0 collective-permute-done.1.refs_1_.s1.s1m
  25.0 2.1 %collective-permute-start.2 = (bf16[5136,128]{1,0:T(8,128)(2,1)}, bf16[5136,128]{1,0:T(8,128)(2,1)}, u32[]{:S(2)}, u32[]{:S(2)}) collective-permute-start(bf16[5136,128]{1,0:T(8,128)(2,1)} %gate.2.x1.x1m), channel_id=1, source_target_pairs={{0,1},{1,0},{2,3},{3,2},{4,5},{5,4},{6,7},{7,6},{8,9},{9,8},{10,11... | collective-permute-start | bytes 3944456 | tf_op jit(solution)/shard_map/ppermute | solution.py:383
  27.1 3.7 %collective-permute-start.4 = (bf16[5136,128]{1,0:T(8,128)(2,1)}, bf16[5136,128]{1,0:T(8,128)(2,1)}, u32[]{:S(2)}, u32[]{:S(2)}) collective-permute-start(bf16[5136,128]{1,0:T(8,128)(2,1)} %collective-permute-done.1.refs_1_.s1.s1m), channel_id=1, source_target_pairs={{1,2},{3,4},{5,6},{7,8},{9,10},{11,12},{13,14},{15,16},{17,18},{19... | collective-permute-start | bytes 3944456 | tf_op jit(solution)/shard_map/ppermute | solution.py:381
  30.9 0.0 collective-permute-done.2.refs_1_.s2.s2m
  30.9 3.0 %collective-permute-start.3 = (bf16[5136,128]{1,0:T(8,128)(2,1)}, bf16[5136,128]{1,0:T(8,128)(2,1)}, u32[]{:S(2)}, u32[]{:S(2)}) collective-permute-start(bf16[5136,128]{1,0:T(8,128)(2,1)} %collective-permute-done.2.refs_1_.s2.s2m), channel_id=1, source_target_pairs={{1,2},{3,4},{5,6},{7,8},{9,10},{11,12},{13,14},{15,16},{17,18},{19... | collective-permute-start | bytes 3944456 | tf_op jit(solution)/shard_map/ppermute | solution.py:384
  33.9 12.9 %collective-permute-done.4.refs_0_ = bf16[5136,128]{1,0:T(8,128)(2,1)} collective-permute-done((bf16[5136,128]{1,0:T(8,128)(2,1)}, bf16[5136,128]{1,0:T(8,128)(2,1)}, u32[]{:S(2)}, u32[]{:S(2)}) %collective-permute-start.4) | collective-permute-done | bytes 1314848 | tf_op jit(solution)/shard_map/ppermute | solution.py:381
  46.8 7.5 %collective-permute-start.5 = (bf16[5136,128]{1,0:T(8,128)(2,1)}, bf16[5136,128]{1,0:T(8,128)(2,1)}, u32[]{:S(2)}, u32[]{:S(2)}) collective-permute-start(bf16[5136,128]{1,0:T(8,128)(2,1)} %gate.3.x2.x2m), channel_id=1, source_target_pairs={{0,1},{1,0},{2,3},{3,2},{4,5},{5,4},{6,7},{7,6},{8,9},{9,8},{10,11... | collective-permute-start | bytes 3944456 | tf_op jit(solution)/shard_map/ppermute | solution.py:386
  54.3 7.3 %near.1 = (f32[2560,128]{1,0:T(8,128)}, f32[2560,128]{1,0:T(8,128)}, f32[4,128,128]{2,1,0:T(8,128)}) custom-call(s32[1]{0:T(128)} %bitcast.odd_ref, bf16[5136,128]{1,0:T(8,128)(2,1)} %get-tuple-element.19.a.am, bf16[5136,128]{1,0:T(8,128)(2,1)} %get-tuple-element.20.b, bf16[5136,128]{1,0:T(8,128)(2,1)} %gate.2.x1.x1m, ...), custom_call_target="tpu_custom_call" | custom-call | flops 1024 | bytes 1048576 | tf_op jit(solution)/shard_map/near/pallas_call | solution.py:397
  61.6 0.0 collective-permute-done.3.x3.x3m
  61.6 0.0 collective-permute-done.5.s3.s3m
  61.6 7.2 %query_side.1 = (bf16[128,2560]{1,0:T(8,128)(2,1)}, bf16[32,20,128]{2,1,0:T(8,128)(2,1)}, f32[40,128]{1,0:T(8,128)}) custom-call(s32[1]{0:T(128)} %bitcast.odd_ref, bf16[5136,128]{1,0:T(8,128)(2,1)} %get-tuple-element.19.a.am, bf16[5136,128]{1,0:T(8,128)(2,1)} %get-tuple-element.20.b, bf16[5136,128]{1,0:T(8,128)(2,1)} %collective-permute-done.3.x3.x3m, ...), custom_call_target="tpu_custom_call" | custom-call | flops 1024 | bytes 1048576 | tf_op jit(solution)/shard_map/query_side/pallas_call | solution.py:403
  68.8 11.8 %all-to-all-start = ((bf16[32,20,128]{2,1,0:T(8,128)(2,1)}), bf16[32,20,128]{2,1,0:T(8,128)(2,1)S(1)}, u32[]{:S(2)}, u32[]{:S(2)}) async-start(bf16[32,20,128]{2,1,0:T(8,128)(2,1)} %get-tuple-element.30), calls=%async_computation | async-start | bytes 393216 | tf_op jit(solution)/shard_map/all_to_all | solution.py:415
  80.6 7.5 %collective-permute-start.8 = (f32[40,128]{1,0:T(8,128)}, f32[40,128]{1,0:T(8,128)S(1)}, u32[]{:S(2)}, u32[]{:S(2)}) collective-permute-start(f32[40,128]{1,0:T(8,128)} %get-tuple-element.26.t0_ref), channel_id=1, source_target_pairs={{3,0},{4,1},{5,2},{6,3},{7,4},{8,5},{9,6},{10,7},{11,8},{12,9},{13... | collective-permute-start | bytes 61448 | tf_op jit(solution)/shard_map/ppermute | solution.py:413
  88.1 7.9 %collective-permute-start.7 = (f32[40,128]{1,0:T(8,128)}, f32[40,128]{1,0:T(8,128)S(1)}, u32[]{:S(2)}, u32[]{:S(2)}) collective-permute-start(f32[40,128]{1,0:T(8,128)} %get-tuple-element.26.t0_ref), channel_id=1, source_target_pairs={{2,0},{3,1},{4,2},{5,3},{6,4},{7,5},{8,6},{9,7},{10,8},{11,9},{12,... | collective-permute-start | bytes 61448 | tf_op jit(solution)/shard_map/ppermute | solution.py:413
  96.0 1.9 %collective-permute-start.6 = (f32[40,128]{1,0:T(8,128)}, f32[40,128]{1,0:T(8,128)S(1)}, u32[]{:S(2)}, u32[]{:S(2)}) collective-permute-start(f32[40,128]{1,0:T(8,128)} %get-tuple-element.26.t0_ref), channel_id=1, source_target_pairs={{1,0},{2,1},{3,2},{4,3},{5,4},{6,5},{7,6},{8,7},{9,8},{10,9},{11,1... | collective-permute-start | bytes 61448 | tf_op jit(solution)/shard_map/ppermute | solution.py:413
  97.9 0.0 collective-permute-done.8.t3_ref.three_ref
  97.9 0.0 copy-start.2
  97.9 0.0 collective-permute-done.7.t2_ref.two_ref
  97.9 3.3 %collective-permute-done.6.t1_ref.one_ref = f32[40,128]{1,0:T(8,128)S(1)} collective-permute-done((f32[40,128]{1,0:T(8,128)}, f32[40,128]{1,0:T(8,128)S(1)}, u32[]{:S(2)}, u32[]{:S(2)}) %collective-permute-start.6) | collective-permute-done | bytes 20512 | tf_op jit(solution)/shard_map/ppermute | solution.py:413
  101.3 0.0 all-to-all-done.part_ref
  101.3 0.6 copy-done.4
  101.9 0.7 copy-done
  102.6 1.6 %spread.1 = bf16[16,20,128]{2,1,0:T(8,128)(2,1)} custom-call(bf16[32,20,128]{2,1,0:T(8,128)(2,1)} %copy-done, f32[40,128]{1,0:T(8,128)} %copy-done.4, f32[40,128]{1,0:T(8,128)} %copy-done.3, f32[40,128]{1,0:T(8,128)} %copy-done.2), custom_call_target="tpu_custom_call" | custom-call | flops 1048576 | bytes 1048576 | tf_op jit(solution)/shard_map/spread/pallas_call | solution.py:417
  104.2 5.2 %all-to-all-start.1 = ((bf16[16,20,128]{2,1,0:T(8,128)(2,1)}), bf16[16,20,128]{2,1,0:T(8,128)(2,1)S(1)}, u32[]{:S(2)}, u32[]{:S(2)}) async-start(bf16[16,20,128]{2,1,0:T(8,128)(2,1)} %spread.1), calls=%async_computation.1 | async-start | bytes 196608 | tf_op jit(solution)/shard_map/all_to_all | solution.py:426
  109.4 9.3 %key_side.1 = (bf16[128,2560]{1,0:T(8,128)(2,1)}, bf16[128,2560]{1,0:T(8,128)(2,1)}) custom-call(s32[1]{0:T(128)} %bitcast.odd_ref, bf16[5136,128]{1,0:T(8,128)(2,1)} %get-tuple-element.19.a.am, bf16[5136,128]{1,0:T(8,128)(2,1)} %get-tuple-element.20.b, bf16[5136,128]{1,0:T(8,128)(2,1)} %gate.2.x1.x1m, ...), custom_call_target="tpu_custom_call" | custom-call | flops 1342177280 | bytes 1048576 | tf_op jit(solution)/shard_map/key_side/pallas_call | solution.py:437
  118.7 3.7 %all-to-all-done.1.part_ref = bf16[16,20,128]{2,1,0:T(8,128)(2,1)S(1)} async-done(((bf16[16,20,128]{2,1,0:T(8,128)(2,1)}), bf16[16,20,128]{2,1,0:T(8,128)(2,1)S(1)}, u32[]{:S(2)}, u32[]{:S(2)}) %all-to-all-start.1) | async-done | bytes 81952 | tf_op jit(solution)/shard_map/all_to_all | solution.py:426
  122.4 0.6 copy-done.1
  123.0 1.5 %gains.1 = (f32[20,128]{1,0:T(8,128)}, f32[20,128]{1,0:T(8,128)}) custom-call(bf16[16,20,128]{2,1,0:T(8,128)(2,1)} %copy-done.1, f32[20,128]{1,0:T(8,128)} %bitcast.7, f32[20,128]{1,0:T(8,128)} %bitcast.10), custom_call_target="tpu_custom_call" | custom-call | flops 1048576 | bytes 1048576 | tf_op jit(solution)/shard_map/gains/pallas_call | solution.py:427
  (8 shorter events, 0.0 us)
Async XLA Ops:
  5.3 19.8 %collective-permute-start = (bf16[5136,128]{1,0:T(8,128)(2,1)}, bf16[5136,128]{1,0:T(8,128)(2,1)}, u32[]{:S(2)}, u32[]{:S(2)}) collective-permute-start(bf16[5136,128]{1,0:T(8,128)(2,1)} %get-tuple-element.19.a.am), channel_id=1, source_target_pairs={{1,2},{3,4},{5,6},{7,8},{9,10},{11,12},{13,14},{15,16},{17,18},{19... | collective-permute-start | bytes 3944456 | tf_op jit(solution)/shard_map/ppermute | solution.py:379
  9.4 15.6 %collective-permute-start.1 = (bf16[5136,128]{1,0:T(8,128)(2,1)}, bf16[5136,128]{1,0:T(8,128)(2,1)}, u32[]{:S(2)}, u32[]{:S(2)}) collective-permute-start(bf16[5136,128]{1,0:T(8,128)(2,1)} %get-tuple-element.20.b), channel_id=1, source_target_pairs={{0,1},{1,0},{2,3},{3,2},{4,5},{5,4},{6,7},{7,6},{8,9},{9,8},{10,11... | collective-permute-start | bytes 3944456 | tf_op jit(solution)/shard_map/ppermute | solution.py:380
  25.0 5.9 %collective-permute-start.2 = (bf16[5136,128]{1,0:T(8,128)(2,1)}, bf16[5136,128]{1,0:T(8,128)(2,1)}, u32[]{:S(2)}, u32[]{:S(2)}) collective-permute-start(bf16[5136,128]{1,0:T(8,128)(2,1)} %gate.2.x1.x1m), channel_id=1, source_target_pairs={{0,1},{1,0},{2,3},{3,2},{4,5},{5,4},{6,7},{7,6},{8,9},{9,8},{10,11... | collective-permute-start | bytes 3944456 | tf_op jit(solution)/shard_map/ppermute | solution.py:383
  27.1 19.7 %collective-permute-start.4 = (bf16[5136,128]{1,0:T(8,128)(2,1)}, bf16[5136,128]{1,0:T(8,128)(2,1)}, u32[]{:S(2)}, u32[]{:S(2)}) collective-permute-start(bf16[5136,128]{1,0:T(8,128)(2,1)} %collective-permute-done.1.refs_1_.s1.s1m), channel_id=1, source_target_pairs={{1,2},{3,4},{5,6},{7,8},{9,10},{11,12},{13,14},{15,16},{17,18},{19... | collective-permute-start | bytes 3944456 | tf_op jit(solution)/shard_map/ppermute | solution.py:381
  30.9 30.7 %collective-permute-start.3 = (bf16[5136,128]{1,0:T(8,128)(2,1)}, bf16[5136,128]{1,0:T(8,128)(2,1)}, u32[]{:S(2)}, u32[]{:S(2)}) collective-permute-start(bf16[5136,128]{1,0:T(8,128)(2,1)} %collective-permute-done.2.refs_1_.s2.s2m), channel_id=1, source_target_pairs={{1,2},{3,4},{5,6},{7,8},{9,10},{11,12},{13,14},{15,16},{17,18},{19... | collective-permute-start | bytes 3944456 | tf_op jit(solution)/shard_map/ppermute | solution.py:384
  46.8 14.8 %collective-permute-start.5 = (bf16[5136,128]{1,0:T(8,128)(2,1)}, bf16[5136,128]{1,0:T(8,128)(2,1)}, u32[]{:S(2)}, u32[]{:S(2)}) collective-permute-start(bf16[5136,128]{1,0:T(8,128)(2,1)} %gate.3.x2.x2m), channel_id=1, source_target_pairs={{0,1},{1,0},{2,3},{3,2},{4,5},{5,4},{6,7},{7,6},{8,9},{9,8},{10,11... | collective-permute-start | bytes 3944456 | tf_op jit(solution)/shard_map/ppermute | solution.py:386
  68.8 32.4 %all-to-all-start = ((bf16[32,20,128]{2,1,0:T(8,128)(2,1)}), bf16[32,20,128]{2,1,0:T(8,128)(2,1)S(1)}, u32[]{:S(2)}, u32[]{:S(2)}) async-start(bf16[32,20,128]{2,1,0:T(8,128)(2,1)} %get-tuple-element.30), calls=%async_computation | async-start | bytes 393216 | tf_op jit(solution)/shard_map/all_to_all | solution.py:415
  80.6 17.3 %collective-permute-start.8 = (f32[40,128]{1,0:T(8,128)}, f32[40,128]{1,0:T(8,128)S(1)}, u32[]{:S(2)}, u32[]{:S(2)}) collective-permute-start(f32[40,128]{1,0:T(8,128)} %get-tuple-element.26.t0_ref), channel_id=1, source_target_pairs={{3,0},{4,1},{5,2},{6,3},{7,4},{8,5},{9,6},{10,7},{11,8},{12,9},{13... | collective-permute-start | bytes 61448 | tf_op jit(solution)/shard_map/ppermute | solution.py:413
  88.1 9.8 %collective-permute-start.7 = (f32[40,128]{1,0:T(8,128)}, f32[40,128]{1,0:T(8,128)S(1)}, u32[]{:S(2)}, u32[]{:S(2)}) collective-permute-start(f32[40,128]{1,0:T(8,128)} %get-tuple-element.26.t0_ref), channel_id=1, source_target_pairs={{2,0},{3,1},{4,2},{5,3},{6,4},{7,5},{8,6},{9,7},{10,8},{11,9},{12,... | collective-permute-start | bytes 61448 | tf_op jit(solution)/shard_map/ppermute | solution.py:413
  96.0 5.3 %collective-permute-start.6 = (f32[40,128]{1,0:T(8,128)}, f32[40,128]{1,0:T(8,128)S(1)}, u32[]{:S(2)}, u32[]{:S(2)}) collective-permute-start(f32[40,128]{1,0:T(8,128)} %get-tuple-element.26.t0_ref), channel_id=1, source_target_pairs={{1,0},{2,1},{3,2},{4,3},{5,4},{6,5},{7,6},{8,7},{9,8},{10,9},{11,1... | collective-permute-start | bytes 61448 | tf_op jit(solution)/shard_map/ppermute | solution.py:413
  97.9 3.4 %copy-start.2 = (f32[40,128]{1,0:T(8,128)}, f32[40,128]{1,0:T(8,128)S(1)}, u32[]{:S(2)}) copy-start(f32[40,128]{1,0:T(8,128)S(1)} %collective-permute-done.8.t3_ref.three_ref) | copy-start | bytes 61444
  97.9 3.4 %copy-start.3 = (f32[40,128]{1,0:T(8,128)}, f32[40,128]{1,0:T(8,128)S(1)}, u32[]{:S(2)}) copy-start(f32[40,128]{1,0:T(8,128)S(1)} %collective-permute-done.7.t2_ref.two_ref) | copy-start | bytes 61444
  101.3 0.6 copy-start.4
  101.9 0.7 copy-start
  104.2 18.2 %all-to-all-start.1 = ((bf16[16,20,128]{2,1,0:T(8,128)(2,1)}), bf16[16,20,128]{2,1,0:T(8,128)(2,1)S(1)}, u32[]{:S(2)}, u32[]{:S(2)}) async-start(bf16[16,20,128]{2,1,0:T(8,128)(2,1)} %spread.1), calls=%async_computation.1 | async-start | bytes 196608 | tf_op jit(solution)/shard_map/all_to_all | solution.py:426
  122.4 0.6 copy-start.1

commit v3 on v2

--- a/solution.py
+++ b/solution.py
@@ -376,13 +376,12 @@
 
     cross = [(i, i + 1) for i in range(1, groups - 1, 2)] + [(i, i - 1) for i in range(2, groups, 2)]
     chip = [(i, i ^ 1) for i in range(groups)]
+    next_chip = [(i, i + 2) for i in range(0, groups - 2, 2)] + [(i, i - 2) for i in range(3, groups, 2)]
     x1 = lax.ppermute(a, AXES, cross)
     s1 = lax.ppermute(b, AXES, chip)
     x2 = lax.ppermute(s1, AXES, cross)
-    x1 = after(x1, s1)
+    x3 = lax.ppermute(x1, AXES, next_chip)
     s2 = lax.ppermute(x1, AXES, chip)
-    x3 = lax.ppermute(s2, AXES, cross)
-    x2 = after(x2, s2)
     s3 = lax.ppermute(x2, AXES, chip)
 
     both = head_blocks(2 * rows)

time: 125 us -> 117 us (0.936)
  the two profiles are of different devices: /device:TPU:39 before, /device:TPU:1 now
where the time goes in v3:
time: 117 us
  starting transfers between devices  42.4 us (36%)
  waiting for transfers between devices  38.8 us (33%)
  Pallas kernels  30.9 us (26%)
  local copies, waits for them, and re-layouts  3.07 us (3%)
  between operations  1.43 us (1%)
    ppermute x1, waiting for transfers between devices, body(): x2 = lax.ppermute(s1, AXES, cross)  18.3 us
    ppermute x1, waiting for transfers between devices, body(): x1 = lax.ppermute(a, AXES, cross)  12.5 us
    all_to_all x1, starting transfers between devices, body(): w = lax.all_to_all(w, 'z', 0, 0)  11.8 us
    pallas_call x1, Pallas kernels, body(): gridded(functools.partial(key_kernel, rows, steps, factor), 'key_side', 1...  9.27 us
    ppermute x1, starting transfers between devices, body(): s1 = lax.ppermute(b, AXES, chip)  8.81 us
    all_to_all x1, starting transfers between devices, body(): w = lax.all_to_all(w, ('dp', 'core'), 0, 0)  7.31 us
    pallas_call x1, Pallas kernels, body(): gridded(functools.partial(near_kernel, rows, factor), 'near', 1024, [both...  7.3 us
    pallas_call x1, Pallas kernels, body(): gridded(functools.partial(query_kernel, rows, steps, factor), 'query_side...  7.21 us
  transfers between devices with their start and end apart: 11, of which 7 were waited for; matrix products, arithmetic and copies ran while one was open for 0% of the time, Pallas kernels for 14%

profile of v3, /device:TPU:1, one launch (start us, length us, event | category | flops | bytes accessed | tf_op | source)
XLA Modules:
  0.0 116.6 jit_solution(7101655008565006506)
XLA Ops:
  1.3 4.0 %pack.1 = (bf16[5136,128]{1,0:T(8,128)(2,1)}, bf16[5136,128]{1,0:T(8,128)(2,1)}, f32[128,128]{1,0:T(8,128)}, f32[128,128]{1,0:T(8,128)}) custom-call(s32[1]{0:T(128)} %bitcast.odd_ref, s32[1]{0:T(128)S(6)} %copy.12.video_ref, bf16[128,2560]{1,0:T(8,128)(2,1)} %q_ref.1, bf16[128,2560]{1,0:T(8,128)(2,1)} %k_ref.1, bf16[128,2560]{1,0:T(8,128)(2,1)} %d_hbm.1, ...), custom_call_target="tpu_custom_call" | custom-call | flops 83886080 | bytes 1048576 | tf_op jit(solution)/shard_map/pack/pallas_call | solution.py:359
  5.3 8.8 %collective-permute-start.2 = (bf16[5136,128]{1,0:T(8,128)(2,1)}, bf16[5136,128]{1,0:T(8,128)(2,1)S(1)}, u32[]{:S(2)}, u32[]{:S(2)}) collective-permute-start(bf16[5136,128]{1,0:T(8,128)(2,1)} %get-tuple-element.20.b), channel_id=1, source_target_pairs={{0,1},{1,0},{2,3},{3,2},{4,5},{5,4},{6,7},{7,6},{8,9},{9,8},{10,11... | collective-permute-start | bytes 3944456 | tf_op jit(solution)/shard_map/ppermute | solution.py:381
  14.1 1.9 %collective-permute-start = (bf16[5136,128]{1,0:T(8,128)(2,1)}, bf16[5136,128]{1,0:T(8,128)(2,1)}, u32[]{:S(2)}, u32[]{:S(2)}) collective-permute-start(bf16[5136,128]{1,0:T(8,128)(2,1)} %get-tuple-element.19.a.am), channel_id=1, source_target_pairs={{1,2},{3,4},{5,6},{7,8},{9,10},{11,12},{13,14},{15,16},{17,18},{19... | collective-permute-start | bytes 3944456 | tf_op jit(solution)/shard_map/ppermute | solution.py:380
  16.0 0.9 collective-permute-done.2.s1.s1m
  17.0 1.2 %copy-done = bf16[5136,128]{1,0:T(8,128)(2,1)} copy-done((bf16[5136,128]{1,0:T(8,128)(2,1)}, bf16[5136,128]{1,0:T(8,128)(2,1)S(1)}, u32[]{:S(2)}) %copy-start) | copy-done | bytes 1314840
  18.1 2.7 %collective-permute-start.3 = (bf16[5136,128]{1,0:T(8,128)(2,1)S(1)}, bf16[5136,128]{1,0:T(8,128)(2,1)}, u32[]{:S(2)}, u32[]{:S(2)}) collective-permute-start(bf16[5136,128]{1,0:T(8,128)(2,1)S(1)} %collective-permute-done.2.s1.s1m), channel_id=1, source_target_pairs={{1,2},{3,4},{5,6},{7,8},{9,10},{11,12},{13,14},{15,16},{17,18},{19... | collective-permute-start | bytes 3944456 | tf_op jit(solution)/shard_map/ppermute | solution.py:382
  20.9 12.5 %collective-permute-done.x1.x1m = bf16[5136,128]{1,0:T(8,128)(2,1)} collective-permute-done((bf16[5136,128]{1,0:T(8,128)(2,1)}, bf16[5136,128]{1,0:T(8,128)(2,1)}, u32[]{:S(2)}, u32[]{:S(2)}) %collective-permute-start) | collective-permute-done | bytes 1314848 | tf_op jit(solution)/shard_map/ppermute | solution.py:380
  33.4 1.9 %collective-permute-start.5 = (bf16[5136,128]{1,0:T(8,128)(2,1)}, bf16[5136,128]{1,0:T(8,128)(2,1)}, u32[]{:S(2)}, u32[]{:S(2)}) collective-permute-start(bf16[5136,128]{1,0:T(8,128)(2,1)} %collective-permute-done.x1.x1m), channel_id=1, source_target_pairs={{0,1},{1,0},{2,3},{3,2},{4,5},{5,4},{6,7},{7,6},{8,9},{9,8},{10,11... | collective-permute-start | bytes 3944456 | tf_op jit(solution)/shard_map/ppermute | solution.py:384
  35.3 1.3 %collective-permute-start.1 = (bf16[5136,128]{1,0:T(8,128)(2,1)}, bf16[5136,128]{1,0:T(8,128)(2,1)}, u32[]{:S(2)}, u32[]{:S(2)}) collective-permute-start(bf16[5136,128]{1,0:T(8,128)(2,1)} %collective-permute-done.x1.x1m), channel_id=1, source_target_pairs={{0,2},{2,4},{4,6},{6,8},{8,10},{10,12},{12,14},{14,16},{16,18},{18... | collective-permute-start | bytes 3944456 | tf_op jit(solution)/shard_map/ppermute | solution.py:383
  36.6 18.3 %collective-permute-done.3.x2.x2m = bf16[5136,128]{1,0:T(8,128)(2,1)} collective-permute-done((bf16[5136,128]{1,0:T(8,128)(2,1)S(1)}, bf16[5136,128]{1,0:T(8,128)(2,1)}, u32[]{:S(2)}, u32[]{:S(2)}) %collective-permute-start.3) | collective-permute-done | bytes 1314848 | tf_op jit(solution)/shard_map/ppermute | solution.py:382
  55.0 1.9 %collective-permute-start.4 = (bf16[5136,128]{1,0:T(8,128)(2,1)}, bf16[5136,128]{1,0:T(8,128)(2,1)}, u32[]{:S(2)}, u32[]{:S(2)}) collective-permute-start(bf16[5136,128]{1,0:T(8,128)(2,1)} %collective-permute-done.3.x2.x2m), channel_id=1, source_target_pairs={{0,1},{1,0},{2,3},{3,2},{4,5},{5,4},{6,7},{7,6},{8,9},{9,8},{10,11... | collective-permute-start | bytes 3944456 | tf_op jit(solution)/shard_map/ppermute | solution.py:385
  56.9 0.0 collective-permute-done.5.s2.s2m
  56.9 7.3 %near.1 = (f32[2560,128]{1,0:T(8,128)}, f32[2560,128]{1,0:T(8,128)}, f32[4,128,128]{2,1,0:T(8,128)}) custom-call(s32[1]{0:T(128)} %bitcast.odd_ref, bf16[5136,128]{1,0:T(8,128)(2,1)} %get-tuple-element.19.a.am, bf16[5136,128]{1,0:T(8,128)(2,1)} %get-tuple-element.20.b, bf16[5136,128]{1,0:T(8,128)(2,1)} %collective-permute-done.x1.x1m, ...), custom_call_target="tpu_custom_call" | custom-call | flops 1024 | bytes 1048576 | tf_op jit(solution)/shard_map/near/pallas_call | solution.py:396
  64.2 0.0 collective-permute-done.1.x3.x3m
  64.2 0.0 collective-permute-done.4.s3.s3m
  64.2 7.2 %query_side.1 = (bf16[128,2560]{1,0:T(8,128)(2,1)}, bf16[32,20,128]{2,1,0:T(8,128)(2,1)}, f32[40,128]{1,0:T(8,128)}) custom-call(s32[1]{0:T(128)} %bitcast.odd_ref, bf16[5136,128]{1,0:T(8,128)(2,1)} %get-tuple-element.19.a.am, bf16[5136,128]{1,0:T(8,128)(2,1)} %get-tuple-element.20.b, bf16[5136,128]{1,0:T(8,128)(2,1)} %collective-permute-done.1.x3.x3m, ...), custom_call_target="tpu_custom_call" | custom-call | flops 1024 | bytes 1048576 | tf_op jit(solution)/shard_map/query_side/pallas_call | solution.py:402
  71.4 7.3 %all-to-all-start = ((bf16[32,20,128]{2,1,0:T(8,128)(2,1)}), bf16[32,20,128]{2,1,0:T(8,128)(2,1)S(1)}, u32[]{:S(2)}, u32[]{:S(2)}) async-start(bf16[32,20,128]{2,1,0:T(8,128)(2,1)} %get-tuple-element.30), calls=%async_computation | async-start | bytes 393216 | tf_op jit(solution)/shard_map/all_to_all | solution.py:414
  78.7 1.3 %collective-permute-start.8 = (f32[40,128]{1,0:T(8,128)}, f32[40,128]{1,0:T(8,128)S(1)}, u32[]{:S(2)}, u32[]{:S(2)}) collective-permute-start(f32[40,128]{1,0:T(8,128)} %get-tuple-element.26.t0_ref), channel_id=1, source_target_pairs={{3,0},{4,1},{5,2},{6,3},{7,4},{8,5},{9,6},{10,7},{11,8},{12,9},{13... | collective-permute-start | bytes 61448 | tf_op jit(solution)/shard_map/ppermute | solution.py:412
  80.0 1.3 %collective-permute-start.7 = (f32[40,128]{1,0:T(8,128)}, f32[40,128]{1,0:T(8,128)S(1)}, u32[]{:S(2)}, u32[]{:S(2)}) collective-permute-start(f32[40,128]{1,0:T(8,128)} %get-tuple-element.26.t0_ref), channel_id=1, source_target_pairs={{2,0},{3,1},{4,2},{5,3},{6,4},{7,5},{8,6},{9,7},{10,8},{11,9},{12,... | collective-permute-start | bytes 61448 | tf_op jit(solution)/shard_map/ppermute | solution.py:412
  81.3 2.1 %collective-permute-start.6 = (f32[40,128]{1,0:T(8,128)}, f32[40,128]{1,0:T(8,128)S(1)}, u32[]{:S(2)}, u32[]{:S(2)}) collective-permute-start(f32[40,128]{1,0:T(8,128)} %get-tuple-element.26.t0_ref), channel_id=1, source_target_pairs={{1,0},{2,1},{3,2},{4,3},{5,4},{6,5},{7,6},{8,7},{9,8},{10,9},{11,1... | collective-permute-start | bytes 61448 | tf_op jit(solution)/shard_map/ppermute | solution.py:412
  83.5 1.8 %collective-permute-done.8.t3_ref.three_ref = f32[40,128]{1,0:T(8,128)S(1)} collective-permute-done((f32[40,128]{1,0:T(8,128)}, f32[40,128]{1,0:T(8,128)S(1)}, u32[]{:S(2)}, u32[]{:S(2)}) %collective-permute-start.8) | collective-permute-done | bytes 20512 | tf_op jit(solution)/shard_map/ppermute | solution.py:412
  85.2 0.7 collective-permute-done.7.t2_ref.two_ref
  86.0 1.4 %collective-permute-done.6.t1_ref.one_ref = f32[40,128]{1,0:T(8,128)S(1)} collective-permute-done((f32[40,128]{1,0:T(8,128)}, f32[40,128]{1,0:T(8,128)S(1)}, u32[]{:S(2)}, u32[]{:S(2)}) %collective-permute-start.6) | collective-permute-done | bytes 20512 | tf_op jit(solution)/shard_map/ppermute | solution.py:412
  87.4 0.0 all-to-all-done.part_ref
  87.4 0.6 copy-done.5
  88.0 0.7 copy-done.1
  88.7 1.6 %spread.1 = bf16[16,20,128]{2,1,0:T(8,128)(2,1)} custom-call(bf16[32,20,128]{2,1,0:T(8,128)(2,1)} %copy-done.1, f32[40,128]{1,0:T(8,128)} %copy-done.5, f32[40,128]{1,0:T(8,128)} %copy-done.4, f32[40,128]{1,0:T(8,128)} %copy-done.3), custom_call_target="tpu_custom_call" | custom-call | flops 1048576 | bytes 1048576 | tf_op jit(solution)/shard_map/spread/pallas_call | solution.py:416
  90.3 11.8 %all-to-all-start.1 = ((bf16[16,20,128]{2,1,0:T(8,128)(2,1)}), bf16[16,20,128]{2,1,0:T(8,128)(2,1)S(1)}, u32[]{:S(2)}, u32[]{:S(2)}) async-start(bf16[16,20,128]{2,1,0:T(8,128)(2,1)} %spread.1), calls=%async_computation.1 | async-start | bytes 196608 | tf_op jit(solution)/shard_map/all_to_all | solution.py:425
  102.0 9.3 %key_side.1 = (bf16[128,2560]{1,0:T(8,128)(2,1)}, bf16[128,2560]{1,0:T(8,128)(2,1)}) custom-call(s32[1]{0:T(128)} %bitcast.odd_ref, bf16[5136,128]{1,0:T(8,128)(2,1)} %get-tuple-element.19.a.am, bf16[5136,128]{1,0:T(8,128)(2,1)} %get-tuple-element.20.b, bf16[5136,128]{1,0:T(8,128)(2,1)} %collective-permute-done.x1.x1m, bf16[5136,128]{1,0:T(8,128)(2,1)} %copy-done, ...), custom_call_target="tpu_custom_call" | custom-call | flops 1342177280 | bytes 1048576 | tf_op jit(solution)/shard_map/key_side/pallas_call | solution.py:436
  111.3 3.1 %all-to-all-done.1.part_ref = bf16[16,20,128]{2,1,0:T(8,128)(2,1)S(1)} async-done(((bf16[16,20,128]{2,1,0:T(8,128)(2,1)}), bf16[16,20,128]{2,1,0:T(8,128)(2,1)S(1)}, u32[]{:S(2)}, u32[]{:S(2)}) %all-to-all-start.1) | async-done | bytes 81952 | tf_op jit(solution)/shard_map/all_to_all | solution.py:425
  114.4 0.6 copy-done.2
  115.1 1.5 %gains.1 = (f32[20,128]{1,0:T(8,128)}, f32[20,128]{1,0:T(8,128)}) custom-call(bf16[16,20,128]{2,1,0:T(8,128)(2,1)} %copy-done.2, f32[20,128]{1,0:T(8,128)} %bitcast.7, f32[20,128]{1,0:T(8,128)} %bitcast.10), custom_call_target="tpu_custom_call" | custom-call | flops 1048576 | bytes 1048576 | tf_op jit(solution)/shard_map/gains/pallas_call | solution.py:426
  (8 shorter events, 0.0 us)
Async XLA Ops:
  5.3 11.7 %collective-permute-start.2 = (bf16[5136,128]{1,0:T(8,128)(2,1)}, bf16[5136,128]{1,0:T(8,128)(2,1)S(1)}, u32[]{:S(2)}, u32[]{:S(2)}) collective-permute-start(bf16[5136,128]{1,0:T(8,128)(2,1)} %get-tuple-element.20.b), channel_id=1, source_target_pairs={{0,1},{1,0},{2,3},{3,2},{4,5},{5,4},{6,7},{7,6},{8,9},{9,8},{10,11... | collective-permute-start | bytes 3944456 | tf_op jit(solution)/shard_map/ppermute | solution.py:381
  14.1 19.3 %collective-permute-start = (bf16[5136,128]{1,0:T(8,128)(2,1)}, bf16[5136,128]{1,0:T(8,128)(2,1)}, u32[]{:S(2)}, u32[]{:S(2)}) collective-permute-start(bf16[5136,128]{1,0:T(8,128)(2,1)} %get-tuple-element.19.a.am), channel_id=1, source_target_pairs={{1,2},{3,4},{5,6},{7,8},{9,10},{11,12},{13,14},{15,16},{17,18},{19... | collective-permute-start | bytes 3944456 | tf_op jit(solution)/shard_map/ppermute | solution.py:380
  17.0 1.2 %copy-start = (bf16[5136,128]{1,0:T(8,128)(2,1)}, bf16[5136,128]{1,0:T(8,128)(2,1)S(1)}, u32[]{:S(2)}) copy-start(bf16[5136,128]{1,0:T(8,128)(2,1)S(1)} %collective-permute-done.2.s1.s1m) | copy-start | bytes 3944452
  18.1 36.8 %collective-permute-start.3 = (bf16[5136,128]{1,0:T(8,128)(2,1)S(1)}, bf16[5136,128]{1,0:T(8,128)(2,1)}, u32[]{:S(2)}, u32[]{:S(2)}) collective-permute-start(bf16[5136,128]{1,0:T(8,128)(2,1)S(1)} %collective-permute-done.2.s1.s1m), channel_id=1, source_target_pairs={{1,2},{3,4},{5,6},{7,8},{9,10},{11,12},{13,14},{15,16},{17,18},{19... | collective-permute-start | bytes 3944456 | tf_op jit(solution)/shard_map/ppermute | solution.py:382
  33.4 23.5 %collective-permute-start.5 = (bf16[5136,128]{1,0:T(8,128)(2,1)}, bf16[5136,128]{1,0:T(8,128)(2,1)}, u32[]{:S(2)}, u32[]{:S(2)}) collective-permute-start(bf16[5136,128]{1,0:T(8,128)(2,1)} %collective-permute-done.x1.x1m), channel_id=1, source_target_pairs={{0,1},{1,0},{2,3},{3,2},{4,5},{5,4},{6,7},{7,6},{8,9},{9,8},{10,11... | collective-permute-start | bytes 3944456 | tf_op jit(solution)/shard_map/ppermute | solution.py:384
  35.3 28.9 %collective-permute-start.1 = (bf16[5136,128]{1,0:T(8,128)(2,1)}, bf16[5136,128]{1,0:T(8,128)(2,1)}, u32[]{:S(2)}, u32[]{:S(2)}) collective-permute-start(bf16[5136,128]{1,0:T(8,128)(2,1)} %collective-permute-done.x1.x1m), channel_id=1, source_target_pairs={{0,2},{2,4},{4,6},{6,8},{8,10},{10,12},{12,14},{14,16},{16,18},{18... | collective-permute-start | bytes 3944456 | tf_op jit(solution)/shard_map/ppermute | solution.py:383
  55.0 9.2 %collective-permute-start.4 = (bf16[5136,128]{1,0:T(8,128)(2,1)}, bf16[5136,128]{1,0:T(8,128)(2,1)}, u32[]{:S(2)}, u32[]{:S(2)}) collective-permute-start(bf16[5136,128]{1,0:T(8,128)(2,1)} %collective-permute-done.3.x2.x2m), channel_id=1, source_target_pairs={{0,1},{1,0},{2,3},{3,2},{4,5},{5,4},{6,7},{7,6},{8,9},{9,8},{10,11... | collective-permute-start | bytes 3944456 | tf_op jit(solution)/shard_map/ppermute | solution.py:385
  71.4 16.0 %all-to-all-start = ((bf16[32,20,128]{2,1,0:T(8,128)(2,1)}), bf16[32,20,128]{2,1,0:T(8,128)(2,1)S(1)}, u32[]{:S(2)}, u32[]{:S(2)}) async-start(bf16[32,20,128]{2,1,0:T(8,128)(2,1)} %get-tuple-element.30), calls=%async_computation | async-start | bytes 393216 | tf_op jit(solution)/shard_map/all_to_all | solution.py:414
  78.7 6.5 %collective-permute-start.8 = (f32[40,128]{1,0:T(8,128)}, f32[40,128]{1,0:T(8,128)S(1)}, u32[]{:S(2)}, u32[]{:S(2)}) collective-permute-start(f32[40,128]{1,0:T(8,128)} %get-tuple-element.26.t0_ref), channel_id=1, source_target_pairs={{3,0},{4,1},{5,2},{6,3},{7,4},{8,5},{9,6},{10,7},{11,8},{12,9},{13... | collective-permute-start | bytes 61448 | tf_op jit(solution)/shard_map/ppermute | solution.py:412
  80.0 5.9 %collective-permute-start.7 = (f32[40,128]{1,0:T(8,128)}, f32[40,128]{1,0:T(8,128)S(1)}, u32[]{:S(2)}, u32[]{:S(2)}) collective-permute-start(f32[40,128]{1,0:T(8,128)} %get-tuple-element.26.t0_ref), channel_id=1, source_target_pairs={{2,0},{3,1},{4,2},{5,3},{6,4},{7,5},{8,6},{9,7},{10,8},{11,9},{12,... | collective-permute-start | bytes 61448 | tf_op jit(solution)/shard_map/ppermute | solution.py:412
  81.3 6.1 %collective-permute-start.6 = (f32[40,128]{1,0:T(8,128)}, f32[40,128]{1,0:T(8,128)S(1)}, u32[]{:S(2)}, u32[]{:S(2)}) collective-permute-start(f32[40,128]{1,0:T(8,128)} %get-tuple-element.26.t0_ref), channel_id=1, source_target_pairs={{1,0},{2,1},{3,2},{4,3},{5,4},{6,5},{7,6},{8,7},{9,8},{10,9},{11,1... | collective-permute-start | bytes 61448 | tf_op jit(solution)/shard_map/ppermute | solution.py:412
  85.2 2.2 %copy-start.3 = (f32[40,128]{1,0:T(8,128)}, f32[40,128]{1,0:T(8,128)S(1)}, u32[]{:S(2)}) copy-start(f32[40,128]{1,0:T(8,128)S(1)} %collective-permute-done.8.t3_ref.three_ref) | copy-start | bytes 61444
  86.0 1.4 %copy-start.4 = (f32[40,128]{1,0:T(8,128)}, f32[40,128]{1,0:T(8,128)S(1)}, u32[]{:S(2)}) copy-start(f32[40,128]{1,0:T(8,128)S(1)} %collective-permute-done.7.t2_ref.two_ref) | copy-start | bytes 61444
  87.4 0.6 copy-start.5
  88.0 0.7 copy-start.1
  90.3 24.2 %all-to-all-start.1 = ((bf16[16,20,128]{2,1,0:T(8,128)(2,1)}), bf16[16,20,128]{2,1,0:T(8,128)(2,1)S(1)}, u32[]{:S(2)}, u32[]{:S(2)}) async-start(bf16[16,20,128]{2,1,0:T(8,128)(2,1)} %spread.1), calls=%async_computation.1 | async-start | bytes 196608 | tf_op jit(solution)/shard_map/all_to_all | solution.py:425
  114.4 0.6 copy-start.2

commit v4 on v3

--- a/solution.py
+++ b/solution.py
@@ -19,6 +19,7 @@
 AXES = ("dp", "z", "core")
 CORES = 2
 VMEM_LIMIT = 63 * 1024 * 1024
+SMALL_LIMIT = 8 * 1024 * 1024
 F32 = jnp.float32
 BF16 = jnp.bfloat16
 
@@ -343,14 +344,14 @@
             name="gate",
         )(value, *others)
 
-    def gridded(kernel, name, flops, in_specs, out_specs, out_shape, scratch=()):
+    def gridded(kernel, name, flops, in_specs, out_specs, out_shape, scratch=(), limit=VMEM_LIMIT):
         return pl.pallas_call(
             kernel,
             grid_spec=pltpu.PrefetchScalarGridSpec(
                 num_scalar_prefetch=1, grid=(steps,), in_specs=in_specs, out_specs=out_specs, scratch_shapes=scratch
             ),
             out_shape=out_shape,
-            compiler_params=params(),
+            compiler_params=params(limit),
             cost_estimate=cost(flops),
             name=name,
         )
@@ -403,32 +404,32 @@
         functools.partial(query_kernel, rows, steps, factor), "query_side", 1024,
         [if_even, if_odd] + [if_even, if_odd] + [mark] * 3
         + [tall, tall, parts, whole, still(heads, HSIZE), square],
-        (whole, still(near_by, heads, HSIZE), still(2 * heads, rows)),
-        (shape(rows, width, dtype=BF16), shape(near_by, heads, HSIZE, dtype=BF16), shape(2 * heads, rows)),
+        (whole, still(along, heads, HSIZE), still(2 * heads, rows)),
+        (shape(rows, width, dtype=BF16), shape(along, heads, HSIZE, dtype=BF16), shape(2 * heads, rows)),
         [pltpu.VMEM((rows, HSIZE), F32)] * 3 + [pltpu.VMEM((heads, HSIZE), F32), pltpu.VMEM((rows, width), F32)],
     )(odd, a, b, x3, s3, a, x3, s3, *near, q_in, gq, rq)
 
     def back(value, by):
         return lax.ppermute(value, AXES, [(i, i - by) for i in range(by, groups)])
 
-    w = lax.all_to_all(w, ("dp", "core"), 0, 0)
+    w = lax.all_to_all(w, "z", 0, 0)
     later = [back(stats, by) for by in range(1, WIN)]
     w = pl.pallas_call(
         spread_kernel,
-        out_shape=shape(along, heads, HSIZE, dtype=BF16),
+        out_shape=shape(near_by, heads, HSIZE, dtype=BF16),
         in_specs=[vmem] + [hbm] * 3,
         out_specs=vmem,
-        compiler_params=params(),
+        compiler_params=params(SMALL_LIMIT),
         cost_estimate=cost(2**20),
         name="spread",
     )(w, *later)
-    w = lax.all_to_all(w, "z", 0, 0)
+    w = lax.all_to_all(w, ("dp", "core"), 0, 0)
     dgain_q, dgain_k = pl.pallas_call(
         gains_kernel,
         out_shape=(shape(heads, HSIZE),) * 2,
         in_specs=[vmem] * 3,
         out_specs=(vmem,) * 2,
-        compiler_params=params(),
+        compiler_params=params(SMALL_LIMIT),
         cost_estimate=cost(2**20),
         name="gains",
     )(w, gq, gk)
@@ -440,6 +441,7 @@
         (whole, cols),
         (shape(rows, width, dtype=BF16),) * 2,
         [pltpu.VMEM((rows, width), F32), pltpu.VMEM((rows, HSIZE), F32)],
+        62 * 1024 * 1024,
     )(odd, a, b, x1, s1, x2, s2, x3, s3, a, x1, s1, x2, s2, x3, s3, stats, *later, k_in, gk, rk)
     return dq_in, dk_in, dv_in, dgain_q.reshape(width), dgain_k.reshape(width)
 

time: 117 us -> 114 us (0.974)
  local copies, waits for them, and re-layouts: 3.07 us -> 1.2 us
  Pallas kernels: 30.9 us -> 29.4 us
    all_to_all x1, starting transfers between devices: 11.8 us -> 9.11 us  [body(): w = lax.all_to_all(w, 'z', 0, 0)]
    all_to_all x1, starting transfers between devices: 7.31 us -> 9.8 us  [body(): w = lax.all_to_all(w, ('dp', 'core'), 0, 0)]
    unnamed x12, local copies, waits for them, and re-layouts: 3.07 us -> 1.2 us
  transfers between devices with their start and end apart: 11 -> 11, of which waited for: 7 -> 7; matrix products, arithmetic and copies ran while one was open for 0% -> 0% of each run, Pallas kernels for 14% -> 15%
where the time goes in v4:
time: 114 us; the launch traced here: 113 us
  starting transfers between devices  42.7 us (37%)
  waiting for transfers between devices  38.4 us (34%)
  Pallas kernels  29.4 us (26%)
  between operations  1.48 us (1%)
  local copies, waits for them, and re-layouts  1.2 us (1%)
    ppermute x1, waiting for transfers between devices, body(): x2 = lax.ppermute(s1, AXES, cross)  18.3 us
    ppermute x1, waiting for transfers between devices, body(): x1 = lax.ppermute(a, AXES, cross)  12.5 us
    all_to_all x1, starting transfers between devices, body(): w = lax.all_to_all(w, ('dp', 'core'), 0, 0)  9.8 us
    pallas_call x1, Pallas kernels, body(): gridded(functools.partial(key_kernel, rows, steps, factor), 'key_side', 1...  9.57 us
    all_to_all x1, starting transfers between devices, body(): w = lax.all_to_all(w, 'z', 0, 0)  9.11 us
    ppermute x1, starting transfers between devices, body(): s1 = lax.ppermute(b, AXES, chip)  8.81 us
    pallas_call x1, Pallas kernels, body(): gridded(functools.partial(near_kernel, rows, factor), 'near', 1024, [both...  7.3 us
    pallas_call x1, Pallas kernels, body(): gridded(functools.partial(query_kernel, rows, steps, factor), 'query_side...  7.17 us
  transfers between devices with their start and end apart: 11, of which 7 were waited for; matrix products, arithmetic and copies ran while one was open for 0% of the time, Pallas kernels for 15%

profile of v4, /device:TPU:1, one launch (start us, length us, event | category | flops | bytes accessed | tf_op | source)
XLA Modules:
  0.0 113.2 jit_solution(16837176366041859280)
XLA Ops:
  1.3 4.0 %pack.1 = (bf16[5136,128]{1,0:T(8,128)(2,1)}, bf16[5136,128]{1,0:T(8,128)(2,1)}, f32[128,128]{1,0:T(8,128)}, f32[128,128]{1,0:T(8,128)}) custom-call(s32[1]{0:T(128)} %bitcast.odd_ref, s32[1]{0:T(128)S(6)} %copy.12.video_ref, bf16[128,2560]{1,0:T(8,128)(2,1)} %q_ref.1, bf16[128,2560]{1,0:T(8,128)(2,1)} %k_ref.1, bf16[128,2560]{1,0:T(8,128)(2,1)} %d_hbm.1, ...), custom_call_target="tpu_custom_call" | custom-call | flops 83886080 | bytes 1048576 | tf_op jit(solution)/shard_map/pack/pallas_call | solution.py:360
  5.3 8.8 %collective-permute-start.2 = (bf16[5136,128]{1,0:T(8,128)(2,1)}, bf16[5136,128]{1,0:T(8,128)(2,1)S(1)}, u32[]{:S(2)}, u32[]{:S(2)}) collective-permute-start(bf16[5136,128]{1,0:T(8,128)(2,1)} %get-tuple-element.20.b), channel_id=1, source_target_pairs={{0,1},{1,0},{2,3},{3,2},{4,5},{5,4},{6,7},{7,6},{8,9},{9,8},{10,11... | collective-permute-start | bytes 3944456 | tf_op jit(solution)/shard_map/ppermute | solution.py:382
  14.1 1.9 %collective-permute-start = (bf16[5136,128]{1,0:T(8,128)(2,1)}, bf16[5136,128]{1,0:T(8,128)(2,1)}, u32[]{:S(2)}, u32[]{:S(2)}) collective-permute-start(bf16[5136,128]{1,0:T(8,128)(2,1)} %get-tuple-element.19.a.am), channel_id=1, source_target_pairs={{1,2},{3,4},{5,6},{7,8},{9,10},{11,12},{13,14},{15,16},{17,18},{19... | collective-permute-start | bytes 3944456 | tf_op jit(solution)/shard_map/ppermute | solution.py:381
  16.0 0.9 collective-permute-done.2.s1.s1m
  17.0 1.2 %copy-done.5 = bf16[5136,128]{1,0:T(8,128)(2,1)} copy-done((bf16[5136,128]{1,0:T(8,128)(2,1)}, bf16[5136,128]{1,0:T(8,128)(2,1)S(1)}, u32[]{:S(2)}) %copy-start.5) | copy-done | bytes 1314840
  18.1 2.7 %collective-permute-start.3 = (bf16[5136,128]{1,0:T(8,128)(2,1)S(1)}, bf16[5136,128]{1,0:T(8,128)(2,1)}, u32[]{:S(2)}, u32[]{:S(2)}) collective-permute-start(bf16[5136,128]{1,0:T(8,128)(2,1)S(1)} %collective-permute-done.2.s1.s1m), channel_id=1, source_target_pairs={{1,2},{3,4},{5,6},{7,8},{9,10},{11,12},{13,14},{15,16},{17,18},{19... | collective-permute-start | bytes 3944456 | tf_op jit(solution)/shard_map/ppermute | solution.py:383
  20.9 12.5 %collective-permute-done.x1.x1m = bf16[5136,128]{1,0:T(8,128)(2,1)} collective-permute-done((bf16[5136,128]{1,0:T(8,128)(2,1)}, bf16[5136,128]{1,0:T(8,128)(2,1)}, u32[]{:S(2)}, u32[]{:S(2)}) %collective-permute-start) | collective-permute-done | bytes 1314848 | tf_op jit(solution)/shard_map/ppermute | solution.py:381
  33.4 1.9 %collective-permute-start.5 = (bf16[5136,128]{1,0:T(8,128)(2,1)}, bf16[5136,128]{1,0:T(8,128)(2,1)}, u32[]{:S(2)}, u32[]{:S(2)}) collective-permute-start(bf16[5136,128]{1,0:T(8,128)(2,1)} %collective-permute-done.x1.x1m), channel_id=1, source_target_pairs={{0,1},{1,0},{2,3},{3,2},{4,5},{5,4},{6,7},{7,6},{8,9},{9,8},{10,11... | collective-permute-start | bytes 3944456 | tf_op jit(solution)/shard_map/ppermute | solution.py:385
  35.3 1.3 %collective-permute-start.1 = (bf16[5136,128]{1,0:T(8,128)(2,1)}, bf16[5136,128]{1,0:T(8,128)(2,1)}, u32[]{:S(2)}, u32[]{:S(2)}) collective-permute-start(bf16[5136,128]{1,0:T(8,128)(2,1)} %collective-permute-done.x1.x1m), channel_id=1, source_target_pairs={{0,2},{2,4},{4,6},{6,8},{8,10},{10,12},{12,14},{14,16},{16,18},{18... | collective-permute-start | bytes 3944456 | tf_op jit(solution)/shard_map/ppermute | solution.py:384
  36.6 18.3 %collective-permute-done.3.x2.x2m = bf16[5136,128]{1,0:T(8,128)(2,1)} collective-permute-done((bf16[5136,128]{1,0:T(8,128)(2,1)S(1)}, bf16[5136,128]{1,0:T(8,128)(2,1)}, u32[]{:S(2)}, u32[]{:S(2)}) %collective-permute-start.3) | collective-permute-done | bytes 1314848 | tf_op jit(solution)/shard_map/ppermute | solution.py:383
  55.0 1.9 %collective-permute-start.4 = (bf16[5136,128]{1,0:T(8,128)(2,1)}, bf16[5136,128]{1,0:T(8,128)(2,1)}, u32[]{:S(2)}, u32[]{:S(2)}) collective-permute-start(bf16[5136,128]{1,0:T(8,128)(2,1)} %collective-permute-done.3.x2.x2m), channel_id=1, source_target_pairs={{0,1},{1,0},{2,3},{3,2},{4,5},{5,4},{6,7},{7,6},{8,9},{9,8},{10,11... | collective-permute-start | bytes 3944456 | tf_op jit(solution)/shard_map/ppermute | solution.py:386
  56.9 0.0 collective-permute-done.5.s2.s2m
  56.9 7.3 %near.1 = (f32[2560,128]{1,0:T(8,128)}, f32[2560,128]{1,0:T(8,128)}, f32[4,128,128]{2,1,0:T(8,128)}) custom-call(s32[1]{0:T(128)} %bitcast.odd_ref, bf16[5136,128]{1,0:T(8,128)(2,1)} %get-tuple-element.19.a.am, bf16[5136,128]{1,0:T(8,128)(2,1)} %get-tuple-element.20.b, bf16[5136,128]{1,0:T(8,128)(2,1)} %collective-permute-done.x1.x1m, ...), custom_call_target="tpu_custom_call" | custom-call | flops 1024 | bytes 1048576 | tf_op jit(solution)/shard_map/near/pallas_call | solution.py:397
  64.2 0.0 collective-permute-done.1.x3.x3m
  64.2 0.0 collective-permute-done.4.s3.s3m
  64.2 7.2 %query_side.1 = (bf16[128,2560]{1,0:T(8,128)(2,1)}, bf16[16,20,128]{2,1,0:T(8,128)(2,1)}, f32[40,128]{1,0:T(8,128)}) custom-call(s32[1]{0:T(128)} %bitcast.odd_ref, bf16[5136,128]{1,0:T(8,128)(2,1)} %get-tuple-element.19.a.am, bf16[5136,128]{1,0:T(8,128)(2,1)} %get-tuple-element.20.b, bf16[5136,128]{1,0:T(8,128)(2,1)} %collective-permute-done.1.x3.x3m, ...), custom_call_target="tpu_custom_call" | custom-call | flops 1024 | bytes 1048576 | tf_op jit(solution)/shard_map/query_side/pallas_call | solution.py:403
  71.4 9.1 %all-to-all-start = ((bf16[16,20,128]{2,1,0:T(8,128)(2,1)}), bf16[16,20,128]{2,1,0:T(8,128)(2,1)S(1)}, u32[]{:S(2)}, u32[]{:S(2)}) async-start(bf16[16,20,128]{2,1,0:T(8,128)(2,1)} %get-tuple-element.30), calls=%async_computation | async-start | bytes 196608 | tf_op jit(solution)/shard_map/all_to_all | solution.py:415
  80.5 1.3 %collective-permute-start.8 = (f32[40,128]{1,0:T(8,128)}, f32[40,128]{1,0:T(8,128)S(1)}, u32[]{:S(2)}, u32[]{:S(2)}) collective-permute-start(f32[40,128]{1,0:T(8,128)} %get-tuple-element.26.t0_ref), channel_id=1, source_target_pairs={{3,0},{4,1},{5,2},{6,3},{7,4},{8,5},{9,6},{10,7},{11,8},{12,9},{13... | collective-permute-start | bytes 61448 | tf_op jit(solution)/shard_map/ppermute | solution.py:413
  81.8 1.3 %collective-permute-start.7 = (f32[40,128]{1,0:T(8,128)}, f32[40,128]{1,0:T(8,128)S(1)}, u32[]{:S(2)}, u32[]{:S(2)}) collective-permute-start(f32[40,128]{1,0:T(8,128)} %get-tuple-element.26.t0_ref), channel_id=1, source_target_pairs={{2,0},{3,1},{4,2},{5,3},{6,4},{7,5},{8,6},{9,7},{10,8},{11,9},{12,... | collective-permute-start | bytes 61448 | tf_op jit(solution)/shard_map/ppermute | solution.py:413
  83.1 2.7 %collective-permute-start.6 = (f32[40,128]{1,0:T(8,128)}, f32[40,128]{1,0:T(8,128)S(1)}, u32[]{:S(2)}, u32[]{:S(2)}) collective-permute-start(f32[40,128]{1,0:T(8,128)} %get-tuple-element.26.t0_ref), channel_id=1, source_target_pairs={{1,0},{2,1},{3,2},{4,3},{5,4},{6,5},{7,6},{8,7},{9,8},{10,9},{11,1... | collective-permute-start | bytes 61448 | tf_op jit(solution)/shard_map/ppermute | solution.py:413
  85.8 2.2 %collective-permute-done.8.t3_ref.three_ref = f32[40,128]{1,0:T(8,128)S(1)} collective-permute-done((f32[40,128]{1,0:T(8,128)}, f32[40,128]{1,0:T(8,128)S(1)}, u32[]{:S(2)}, u32[]{:S(2)}) %collective-permute-start.8) | collective-permute-done | bytes 20512 | tf_op jit(solution)/shard_map/ppermute | solution.py:413
  88.0 0.8 collective-permute-done.7.t2_ref.two_ref
  88.8 1.4 %collective-permute-done.6.t1_ref.one_ref = f32[40,128]{1,0:T(8,128)S(1)} collective-permute-done((f32[40,128]{1,0:T(8,128)}, f32[40,128]{1,0:T(8,128)S(1)}, u32[]{:S(2)}, u32[]{:S(2)}) %collective-permute-start.6) | collective-permute-done | bytes 20512 | tf_op jit(solution)/shard_map/ppermute | solution.py:413
  90.1 2.3 %all-to-all-done.part_ref = bf16[16,20,128]{2,1,0:T(8,128)(2,1)S(1)} async-done(((bf16[16,20,128]{2,1,0:T(8,128)(2,1)}), bf16[16,20,128]{2,1,0:T(8,128)(2,1)S(1)}, u32[]{:S(2)}, u32[]{:S(2)}) %all-to-all-start) | async-done | bytes 81952 | tf_op jit(solution)/shard_map/all_to_all | solution.py:415
  92.4 0.7 spread.1
  93.1 9.8 %all-to-all-start.1 = ((bf16[32,20,128]{2,1,0:T(8,128)(2,1)}), bf16[32,20,128]{2,1,0:T(8,128)(2,1)S(1)}, u32[]{:S(2)}, u32[]{:S(2)}) async-start(bf16[32,20,128]{2,1,0:T(8,128)(2,1)} %spread.1), calls=%async_computation.1 | async-start | bytes 393216 | tf_op jit(solution)/shard_map/all_to_all | solution.py:426
  102.9 0.0 copy-done.2
  103.0 0.0 copy-start
  103.0 0.0 copy-start.1
  103.0 9.6 %key_side.1 = (bf16[128,2560]{1,0:T(8,128)(2,1)}, bf16[128,2560]{1,0:T(8,128)(2,1)}) custom-call(s32[1]{0:T(128)} %bitcast.odd_ref, bf16[5136,128]{1,0:T(8,128)(2,1)} %get-tuple-element.19.a.am, bf16[5136,128]{1,0:T(8,128)(2,1)} %get-tuple-element.20.b, bf16[5136,128]{1,0:T(8,128)(2,1)} %collective-permute-done.x1.x1m, bf16[5136,128]{1,0:T(8,128)(2,1)} %copy-done.5, ...), custom_call_target="tpu_custom_call" | custom-call | flops 1342177280 | bytes 1048576 | tf_op jit(solution)/shard_map/key_side/pallas_call | solution.py:437
  112.5 0.0 all-to-all-done.1.part_ref
  112.6 0.7 gains.1
  (8 shorter events, 0.0 us)
Async XLA Ops:
  5.3 11.7 %collective-permute-start.2 = (bf16[5136,128]{1,0:T(8,128)(2,1)}, bf16[5136,128]{1,0:T(8,128)(2,1)S(1)}, u32[]{:S(2)}, u32[]{:S(2)}) collective-permute-start(bf16[5136,128]{1,0:T(8,128)(2,1)} %get-tuple-element.20.b), channel_id=1, source_target_pairs={{0,1},{1,0},{2,3},{3,2},{4,5},{5,4},{6,7},{7,6},{8,9},{9,8},{10,11... | collective-permute-start | bytes 3944456 | tf_op jit(solution)/shard_map/ppermute | solution.py:382
  14.1 19.3 %collective-permute-start = (bf16[5136,128]{1,0:T(8,128)(2,1)}, bf16[5136,128]{1,0:T(8,128)(2,1)}, u32[]{:S(2)}, u32[]{:S(2)}) collective-permute-start(bf16[5136,128]{1,0:T(8,128)(2,1)} %get-tuple-element.19.a.am), channel_id=1, source_target_pairs={{1,2},{3,4},{5,6},{7,8},{9,10},{11,12},{13,14},{15,16},{17,18},{19... | collective-permute-start | bytes 3944456 | tf_op jit(solution)/shard_map/ppermute | solution.py:381
  17.0 1.2 %copy-start.5 = (bf16[5136,128]{1,0:T(8,128)(2,1)}, bf16[5136,128]{1,0:T(8,128)(2,1)S(1)}, u32[]{:S(2)}) copy-start(bf16[5136,128]{1,0:T(8,128)(2,1)S(1)} %collective-permute-done.2.s1.s1m) | copy-start | bytes 3944452
  18.1 36.8 %collective-permute-start.3 = (bf16[5136,128]{1,0:T(8,128)(2,1)S(1)}, bf16[5136,128]{1,0:T(8,128)(2,1)}, u32[]{:S(2)}, u32[]{:S(2)}) collective-permute-start(bf16[5136,128]{1,0:T(8,128)(2,1)S(1)} %collective-permute-done.2.s1.s1m), channel_id=1, source_target_pairs={{1,2},{3,4},{5,6},{7,8},{9,10},{11,12},{13,14},{15,16},{17,18},{19... | collective-permute-start | bytes 3944456 | tf_op jit(solution)/shard_map/ppermute | solution.py:383
  33.4 23.5 %collective-permute-start.5 = (bf16[5136,128]{1,0:T(8,128)(2,1)}, bf16[5136,128]{1,0:T(8,128)(2,1)}, u32[]{:S(2)}, u32[]{:S(2)}) collective-permute-start(bf16[5136,128]{1,0:T(8,128)(2,1)} %collective-permute-done.x1.x1m), channel_id=1, source_target_pairs={{0,1},{1,0},{2,3},{3,2},{4,5},{5,4},{6,7},{7,6},{8,9},{9,8},{10,11... | collective-permute-start | bytes 3944456 | tf_op jit(solution)/shard_map/ppermute | solution.py:385
  35.3 28.9 %collective-permute-start.1 = (bf16[5136,128]{1,0:T(8,128)(2,1)}, bf16[5136,128]{1,0:T(8,128)(2,1)}, u32[]{:S(2)}, u32[]{:S(2)}) collective-permute-start(bf16[5136,128]{1,0:T(8,128)(2,1)} %collective-permute-done.x1.x1m), channel_id=1, source_target_pairs={{0,2},{2,4},{4,6},{6,8},{8,10},{10,12},{12,14},{14,16},{16,18},{18... | collective-permute-start | bytes 3944456 | tf_op jit(solution)/shard_map/ppermute | solution.py:384
  55.0 9.2 %collective-permute-start.4 = (bf16[5136,128]{1,0:T(8,128)(2,1)}, bf16[5136,128]{1,0:T(8,128)(2,1)}, u32[]{:S(2)}, u32[]{:S(2)}) collective-permute-start(bf16[5136,128]{1,0:T(8,128)(2,1)} %collective-permute-done.3.x2.x2m), channel_id=1, source_target_pairs={{0,1},{1,0},{2,3},{3,2},{4,5},{5,4},{6,7},{7,6},{8,9},{9,8},{10,11... | collective-permute-start | bytes 3944456 | tf_op jit(solution)/shard_map/ppermute | solution.py:386
  71.4 21.0 %all-to-all-start = ((bf16[16,20,128]{2,1,0:T(8,128)(2,1)}), bf16[16,20,128]{2,1,0:T(8,128)(2,1)S(1)}, u32[]{:S(2)}, u32[]{:S(2)}) async-start(bf16[16,20,128]{2,1,0:T(8,128)(2,1)} %get-tuple-element.30), calls=%async_computation | async-start | bytes 196608 | tf_op jit(solution)/shard_map/all_to_all | solution.py:415
  80.5 7.5 %collective-permute-start.8 = (f32[40,128]{1,0:T(8,128)}, f32[40,128]{1,0:T(8,128)S(1)}, u32[]{:S(2)}, u32[]{:S(2)}) collective-permute-start(f32[40,128]{1,0:T(8,128)} %get-tuple-element.26.t0_ref), channel_id=1, source_target_pairs={{3,0},{4,1},{5,2},{6,3},{7,4},{8,5},{9,6},{10,7},{11,8},{12,9},{13... | collective-permute-start | bytes 61448 | tf_op jit(solution)/shard_map/ppermute | solution.py:413
  81.8 7.0 %collective-permute-start.7 = (f32[40,128]{1,0:T(8,128)}, f32[40,128]{1,0:T(8,128)S(1)}, u32[]{:S(2)}, u32[]{:S(2)}) collective-permute-start(f32[40,128]{1,0:T(8,128)} %get-tuple-element.26.t0_ref), channel_id=1, source_target_pairs={{2,0},{3,1},{4,2},{5,3},{6,4},{7,5},{8,6},{9,7},{10,8},{11,9},{12,... | collective-permute-start | bytes 61448 | tf_op jit(solution)/shard_map/ppermute | solution.py:413
  83.1 7.0 %collective-permute-start.6 = (f32[40,128]{1,0:T(8,128)}, f32[40,128]{1,0:T(8,128)S(1)}, u32[]{:S(2)}, u32[]{:S(2)}) collective-permute-start(f32[40,128]{1,0:T(8,128)} %get-tuple-element.26.t0_ref), channel_id=1, source_target_pairs={{1,0},{2,1},{3,2},{4,3},{5,4},{6,5},{7,6},{8,7},{9,8},{10,9},{11,1... | collective-permute-start | bytes 61448 | tf_op jit(solution)/shard_map/ppermute | solution.py:413
  88.0 14.9 %copy-start.2 = (f32[40,128]{1,0:T(8,128)}, f32[40,128]{1,0:T(8,128)S(1)}, u32[]{:S(2)}) copy-start(f32[40,128]{1,0:T(8,128)S(1)} %collective-permute-done.8.t3_ref.three_ref) | copy-start | bytes 61444
  88.8 14.2 %copy-start.3 = (f32[40,128]{1,0:T(8,128)}, f32[40,128]{1,0:T(8,128)S(1)}, u32[]{:S(2)}) copy-start(f32[40,128]{1,0:T(8,128)S(1)} %collective-permute-done.7.t2_ref.two_ref) | copy-start | bytes 61444
  90.1 12.8 %copy-start.4 = (f32[40,128]{1,0:T(8,128)}, f32[40,128]{1,0:T(8,128)S(1)}, u32[]{:S(2)}) copy-start(f32[40,128]{1,0:T(8,128)S(1)} %collective-permute-done.6.t1_ref.one_ref) | copy-start | bytes 61444
  93.1 19.4 %all-to-all-start.1 = ((bf16[32,20,128]{2,1,0:T(8,128)(2,1)}), bf16[32,20,128]{2,1,0:T(8,128)(2,1)S(1)}, u32[]{:S(2)}, u32[]{:S(2)}) async-start(bf16[32,20,128]{2,1,0:T(8,128)(2,1)} %spread.1), calls=%async_computation.1 | async-start | bytes 393216 | tf_op jit(solution)/shard_map/all_to_all | solution.py:426
  103.0 9.6 %copy-start = (f32[2560]{0:T(1024)S(1)}, f32[2560]{0:T(1024)}, u32[]{:S(2)}) copy-start(f32[2560]{0:T(1024)} %param.10) | copy-start | bytes 30724
  103.0 9.6 %copy-start.1 = (f32[2560]{0:T(1024)S(1)}, f32[2560]{0:T(1024)}, u32[]{:S(2)}) copy-start(f32[2560]{0:T(1024)} %param.11) | copy-start | bytes 30724

commit v5 on v4

v5 whole, which is shorter than its diff:
```python
import functools
import math

import jax
import jax.numpy as jnp
from jax import lax
from jax.experimental import pallas as pl
from jax.experimental.pallas import tpu as pltpu
from jax.sharding import Mesh
from jax.sharding import PartitionSpec as P

HSIZE = 128
WIN = 4
EPS = 1e-06
NEG = -1e30
MARK_ROWS = 16
PER = 5
SPLIT = 4
AXES = ("dp", "z", "core")
CORES = 2
VMEM_LIMIT = 63 * 1024 * 1024
SMALL_LIMIT = 8 * 1024 * 1024
KEY_LIMIT = 62 * 1024 * 1024
F32 = jnp.float32
BF16 = jnp.bfloat16


def dot_nt(a, b):
    return lax.dot_general(a, b, (((1,), (1,)), ((), ())), preferred_element_type=F32)


def dot_nn(a, b):
    return lax.dot_general(a, b, (((1,), (0,)), ((), ())), preferred_element_type=F32)


def head_rows(j, rows):
    return slice(j * rows, (j + 1) * rows)


def head_cols(j):
    return slice(j * HSIZE, (j + 1) * HSIZE)


def pack_kernel(heads, odd_ref, video_ref, q_hbm, k_hbm, d_hbm, v_hbm, gq_hbm, gk_hbm,
                a_hbm, b_hbm, rq_hbm, rk_hbm, main, stage, gain, mark, scales, in_sems, out_sems):
    odd = odd_ref[0] == 1
    rows, width = q_hbm.shape
    size = rows // SPLIT
    steps = heads // PER
    span = PER * rows

    def load(which, src):
        return [
            pltpu.make_async_copy(
                src.at[pl.ds(part * size, size), :], main.at[which, pl.ds(part * size, size), :], in_sems.at[which, part]
            )
            for part in range(SPLIT)
        ]

    loads = [load(which, src) for which, src in enumerate((q_hbm, k_hbm, d_hbm, v_hbm))]
    gains = [
        pltpu.make_async_copy(src, gain.at[which], in_sems.at[which, SPLIT]) for which, src in enumerate((gq_hbm, gk_hbm))
    ]
    for copy in gains + loads[0] + loads[1] + loads[2] + loads[3]:
        copy.start()

    def store(which, step, dst):
        if step == steps:
            return pltpu.make_async_copy(
                mark, dst.at[pl.ds(2 * steps * span, MARK_ROWS), :], out_sems.at[which, steps]
            )
        return pltpu.make_async_copy(
            stage.at[which, pl.ds(step * span, span), :],
            dst.at[pl.ds((2 * step + which // 2) * span, span), :],
            out_sems.at[which, step],
        )

    def start_store(which, step):
        with_a = odd == (which % 2 == 1)

        @pl.when(with_a)
        def _():
            store(which, step, a_hbm).start()

        @pl.when(jnp.logical_not(with_a))
        def _():
            store(which, step, b_hbm).start()

    mark[...] = jnp.full((MARK_ROWS, HSIZE), (video_ref[0] + 1).astype(F32), F32).astype(BF16)
    for which in range(2):
        start_store(which, steps)
    for copy in gains:
        copy.wait()
    scale_stores = [
        pltpu.make_async_copy(scales.at[which], dst, out_sems.at[2 + which, steps])
        for which, dst in enumerate((rq_hbm, rk_hbm))
    ]
    for which in range(2):
        for copy in loads[which]:
            copy.wait()
        raw = main[which].astype(F32)
        scale = lax.rsqrt(jnp.sum(raw * raw, axis=-1, keepdims=True) * (1.0 / width) + EPS)
        scales[which] = jnp.broadcast_to(scale, (rows, HSIZE))
        scale_stores[which].start()
        for step in range(steps):
            for h in range(step * PER, (step + 1) * PER):
                normed = main[which, :, head_cols(h)].astype(F32) * scale * gain[which, h : h + 1, :]
                stage[which, head_rows(h, rows), :] = normed.astype(BF16)
            start_store(which, step)
    for which in (2, 3):
        for copy in loads[which]:
            copy.wait()
        for step in range(steps):
            for h in range(step * PER, (step + 1) * PER):
                stage[which, head_rows(h, rows), :] = main[which, :, head_cols(h)]
            start_store(which, step)
    for which in range(4):
        for step in range(steps + (which < 2)):
            store(which, step, a_hbm).wait()
    for copy in scale_stores:
        copy.wait()


def mark_of(ref):
    return ref[0:1, 0:1].astype(F32)


def bias_of(own_ref, odd, if_odd, if_even):
    mark = jnp.where(odd, mark_of(if_odd), mark_of(if_even))
    return jnp.where(mark == mark_of(own_ref), 0.0, NEG)


def bias_row(biases, rows):
    return jnp.concatenate([jnp.broadcast_to(bias, (1, rows)) for bias in biases], axis=1)


def near_kernel(rows, factor, odd_ref, a, b, x1, s1, x2, s2, am, x1m, s1m, x2m, s2m, g_ref, h_ref, stat_ref):
    odd = odd_ref[0] == 1
    bias = bias_row([jnp.zeros((1, 1), F32), bias_of(am, odd, s1m, x1m), bias_of(am, odd, s2m, x2m)], rows)
    pairs = ((a, b), (s1, x1), (s2, x2))
    left = lax.broadcasted_iota(jnp.int32, (rows, HSIZE), 1) < HSIZE // 2
    keys, scores, dprobs = [], [], []
    for j in range(PER):
        top = head_rows(j, rows)
        low = head_rows(PER + j, rows)
        q = jnp.where(odd, b[top, :], a[top, :])
        d_out = jnp.where(odd, b[low, :], a[low, :])
        keys.append(jnp.concatenate([jnp.where(odd, o[top, :], e[top, :]) for o, e in pairs], axis=0))
        vals = jnp.concatenate([jnp.where(odd, o[low, :], e[low, :]) for o, e in pairs], axis=0)
        scores.append(dot_nt(q, keys[j]))
        dprobs.append(dot_nt(d_out, vals))
    for j in range(PER):
        out = head_rows(j, rows)
        score = scores[j] * factor + bias
        best = jnp.max(score, axis=-1, keepdims=True)
        probs = jnp.exp2(score - best)
        total = jnp.sum(probs, axis=-1, keepdims=True)
        inverse = 1.0 / total
        probs = probs * inverse
        delta = jnp.sum(probs * dprobs[j], axis=-1, keepdims=True)
        both = jnp.concatenate([(probs * (dprobs[j] - delta)).astype(BF16), probs.astype(BF16)], axis=0)
        sums = dot_nn(both, keys[j])
        g_ref[out, :] = sums[:rows]
        h_ref[out, :] = sums[rows:]
        stat_ref[out, :] = jnp.where(left, best + jnp.log2(total), delta)


class Loads:
    def __init__(self, odd, sems):
        self.odd, self.sems, self.taken = odd, sems, 0

    def make(self, dst, if_odd, if_even=None):
        sem = self.sems.at[self.taken]
        self.taken += 1
        return (dst, sem, if_odd, if_even)

    def start(self, load):
        dst, sem, if_odd, if_even = load
        if if_even is None:
            pltpu.make_async_copy(if_odd, dst, sem).start()
            return

        @pl.when(self.odd)
        def _():
            pltpu.make_async_copy(if_odd, dst, sem).start()

        @pl.when(jnp.logical_not(self.odd))
        def _():
            pltpu.make_async_copy(if_even, dst, sem).start()

    def wait(self, load):
        dst, sem, src, _ = load
        pltpu.make_async_copy(src, dst, sem).wait()


def chunk(ref, step, size):
    return ref.at[pl.ds(step * size, size), :]


def query_kernel(rows, heads, factor, odd_ref, a, b, x3, s3, g_hbm, h_hbm, near_hbm, q_hbm, gq_hbm, rq_hbm,
                 dq_hbm, w_hbm, stat_hbm, own, last, g_mem, h_mem, near_mem, q_mem, gain, scales, marks, tilt, dq_mem,
                 w_mem, stat_mem,
                 sems, out_sems):
    steps = heads // PER
    width = heads * HSIZE
    span = PER * rows
    odd = odd_ref[0] == 1
    loads = Loads(odd, sems)
    tail = 2 * heads * rows
    mark = pl.ds(tail, MARK_ROWS)
    small = [
        loads.make(marks.at[0], a.at[mark, :]),
        loads.make(marks.at[1], s3.at[mark, :], x3.at[mark, :]),
    ]
    later = [loads.make(scales, rq_hbm), loads.make(gain, gq_hbm), loads.make(q_mem, q_hbm)]
    blocks = [
        [
            loads.make(chunk(own, step, 2 * span), chunk(b, step, 2 * span), chunk(a, step, 2 * span)),
            loads.make(chunk(last, step, 2 * span), chunk(s3, step, 2 * span), chunk(x3, step, 2 * span)),
            loads.make(chunk(near_mem, step, span), chunk(near_hbm, step, span)),
        ]
        for step in range(steps)
    ]
    sums = [
        [
            loads.make(chunk(g_mem, step, span), chunk(g_hbm, step, span)),
            loads.make(chunk(h_mem, step, span), chunk(h_hbm, step, span)),
        ]
        for step in range(steps)
    ]
    for load in small + blocks[0] + sums[0] + later + blocks[1]:
        loads.start(load)
    for load in small:
        loads.wait(load)
    bias = jnp.where(mark_of(marks.at[0]) == mark_of(marks.at[1]), 0.0, NEG)
    lane = lax.broadcasted_iota(jnp.int32, (rows, HSIZE), 1)
    scale = 1.0 / math.sqrt(HSIZE)
    left = lane < HSIZE // 2
    lse = jnp.zeros((rows, HSIZE), F32)
    deltas = jnp.zeros((rows, HSIZE), F32)
    u_sum = jnp.zeros((rows, HSIZE), F32)
    w_rows = []
    for step in range(steps):
        for load in blocks[step]:
            loads.wait(load)
        if step + 1 < steps:
            for load in sums[step + 1] + (blocks[step + 2] if step + 2 < steps else []):
                loads.start(load)
        base = step * 2 * span
        keys, scores, dprobs = [], [], []
        for j in range(PER):
            top = slice(base + j * rows, base + (j + 1) * rows)
            low = slice(base + span + j * rows, base + span + (j + 1) * rows)
            keys.append(last[top, :])
            scores.append(dot_nt(own[top, :], keys[j]))
            dprobs.append(dot_nt(own[low, :], last[low, :]))
        fars, nears = [], []
        for j in range(PER):
            head = step * PER + j
            old = near_mem[head_rows(head, rows), :]
            turned = pltpu.roll(old, HSIZE // 2, 1)
            old_lse = jnp.where(left, old, turned)
            old_delta = jnp.where(left, turned, old)
            score = scores[j] * factor + bias
            best = jnp.maximum(old_lse, jnp.max(score, axis=-1, keepdims=True))
            prob = jnp.exp2(score - best)
            kept = jnp.exp2(old_lse - best)
            total = kept + jnp.sum(prob, axis=-1, keepdims=True)
            inverse = 1.0 / total
            kept = kept * inverse
            delta = kept * old_delta + jnp.sum(prob * dprobs[j], axis=-1, keepdims=True) * inverse
            fars.append(((prob * inverse) * (dprobs[j] - delta)).astype(BF16))
            nears.append((kept, old_delta - delta))
            lse = jnp.where(lane == head, best + jnp.log2(total), lse)
            deltas = jnp.where(lane == head, delta, deltas)
        if step == 0:
            for load in later:
                loads.wait(load)
            rq = scales[...]
        for load in sums[step]:
            loads.wait(load)
        for j in range(PER):
            head = step * PER + j
            out = head_rows(head, rows)
            cols = head_cols(head)
            kept, moved = nears[j]
            dq = (dot_nn(fars[j], keys[j]) + kept * (g_mem[out, :] + moved * h_mem[out, :])) * scale
            raw = q_mem[:, cols].astype(F32)
            tilted = dq * gain[head : head + 1, :]
            tilt[:, cols] = tilted
            u_sum = u_sum + raw * tilted
            w_rows.append(jnp.sum(dq * (raw * rq), axis=0, keepdims=True))
    stat_mem[:heads, :] = jnp.transpose(lse)[:heads, :]
    stat_mem[heads:, :] = jnp.transpose(deltas)[:heads, :]
    w_mem[...] = jnp.broadcast_to(jnp.concatenate(w_rows, axis=0).astype(BF16)[None], w_mem.shape)
    early = [
        pltpu.make_async_copy(stat_mem, stat_hbm, out_sems.at[steps]),
        pltpu.make_async_copy(w_mem, w_hbm, out_sems.at[steps + 1]),
    ]
    for copy in early:
        copy.start()
    low_part = rq * rq * rq * jnp.sum(u_sum, axis=-1, keepdims=True) * (1.0 / width)
    close_norm(heads, rq, low_part, tilt, q_mem, dq_mem, dq_hbm, out_sems)
    for copy in early:
        copy.wait()


def close_norm(heads, scale, low_part, tilt, raw, result, out_hbm, sems):
    steps = heads // PER
    size = PER * HSIZE
    copies = []
    for step in range(steps):
        for h in range(step * PER, (step + 1) * PER):
            cols = head_cols(h)
            result[:, cols] = (scale * tilt[:, cols] - raw[:, cols].astype(F32) * low_part).astype(BF16)
        some = pl.ds(step * size, size)
        copies.append(pltpu.make_async_copy(result.at[:, some], out_hbm.at[:, some], sems.at[step]))
        copies[-1].start()
    for copy in copies:
        copy.wait()


def key_kernel(rows, heads, factor, odd_ref, a, b, x1, s1, x2, s2, x3, s3, t0, t1, t2, t3, k_hbm, gk_hbm, rk_hbm,
               dk_hbm, dv_hbm, own, later, stats, k_mem, gain, scales, marks, tilt, dk_mem, dv_mem, sems, out_sems):
    steps = heads // PER
    width = heads * HSIZE
    span = PER * rows
    odd = odd_ref[0] == 1
    loads = Loads(odd, sems)
    mark = pl.ds(2 * heads * rows, MARK_ROWS)
    pairs = ((b, a), (x1, s1), (x2, s2), (x3, s3))
    small = [loads.make(stats.at[d], t) for d, t in enumerate((t0, t1, t2, t3))]
    small += [loads.make(marks.at[d], o.at[mark, :], e.at[mark, :]) for d, (o, e) in enumerate(pairs)]
    small += [loads.make(gain, gk_hbm)]
    last = [loads.make(scales, rk_hbm)]
    blocks = [
        [loads.make(chunk(own, step, 2 * span), chunk(a, step, 2 * span), chunk(b, step, 2 * span))]
        + [
            loads.make(chunk(later.at[d], step, 2 * span), chunk(o, step, 2 * span), chunk(e, step, 2 * span))
            for d, (o, e) in enumerate(pairs)
        ]
        for step in range(steps)
    ]
    whole_k = loads.make(k_mem, k_hbm)
    for load in small + blocks[0] + [whole_k] + blocks[1] + last:
        loads.start(load)
    for load in small:
        loads.wait(load)
    own_mark = mark_of(marks.at[0])
    bias = bias_row([jnp.where(mark_of(marks.at[d]) == own_mark, 0.0, NEG) for d in range(WIN)], rows)
    scale = 1.0 / math.sqrt(HSIZE)
    u_sum = jnp.zeros((rows, HSIZE), F32)
    copies = []
    for step in range(steps):
        for load in blocks[step] + ([whole_k] if step == 0 else []):
            loads.wait(load)
        if step + 2 < steps:
            for load in blocks[step + 2]:
                loads.start(load)
        base = step * 2 * span
        for j in range(PER):
            head = step * PER + j
            top = slice(base + j * rows, base + (j + 1) * rows)
            low = slice(base + span + j * rows, base + span + (j + 1) * rows)
            cols = head_cols(head)
            queries = jnp.concatenate([later[d, top, :] for d in range(WIN)], axis=0)
            d_outs = jnp.concatenate([later[d, low, :] for d in range(WIN)], axis=0)
            log_total = jnp.concatenate([stats[d, head : head + 1, :] for d in range(WIN)], axis=1)
            delta = jnp.concatenate([stats[d, heads + head : heads + head + 1, :] for d in range(WIN)], axis=1)
            probs = jnp.exp2(dot_nt(own[top, :], queries) * factor + (bias - log_total))
            dscores = probs * (dot_nt(own[low, :], d_outs) - delta)
            dv_mem[:, cols] = dot_nn(probs.astype(BF16), d_outs).astype(BF16)
            tilted = dot_nn(dscores.astype(BF16), queries) * (scale * gain[head : head + 1, :])
            tilt[:, cols] = tilted
            u_sum = u_sum + k_mem[:, cols].astype(F32) * tilted
        some = pl.ds(step * PER * HSIZE, PER * HSIZE)
        copies.append(pltpu.make_async_copy(dv_mem.at[:, some], dv_hbm.at[:, some], out_sems.at[steps + step]))
        copies[-1].start()
    loads.wait(last[0])
    rk = scales[...]
    low_part = rk * rk * rk * jnp.sum(u_sum, axis=-1, keepdims=True) * (1.0 / width)
    close_norm(heads, rk, low_part, tilt, k_mem, dk_mem, dk_hbm, out_sems)
    for copy in copies:
        copy.wait()


def spread_kernel(part_ref, one_ref, two_ref, three_ref, out_ref):
    del one_ref, two_ref, three_ref
    out_ref[...] = jnp.broadcast_to(jnp.sum(part_ref[...].astype(F32), axis=0).astype(BF16)[None], out_ref.shape)


def gains_kernel(part_ref, gq_ref, gk_ref, dq_ref, dk_ref):
    total = jnp.sum(part_ref[...].astype(F32), axis=0)
    dq_ref[...] = total
    dk_ref[...] = total * gq_ref[...] / gk_ref[...]


def params(limit=VMEM_LIMIT):
    return pltpu.CompilerParams(vmem_limit_bytes=limit)


def cost(flops, data=2**20):
    return pl.CostEstimate(flops=flops, bytes_accessed=data, transcendentals=0)


def shape(*dims, dtype=F32):
    return jax.ShapeDtypeStruct(dims, dtype)


def still(*dims):
    return pl.BlockSpec(dims, lambda i, odd: (0,) * len(dims))


def head_blocks(rows, used_if=None):
    def place(i, odd):
        if used_if is None:
            return (i, 0)
        return (i * odd[0] if used_if else i * (1 - odd[0]), 0)

    return pl.BlockSpec((PER * rows, HSIZE), place)


def body(q_in, k_in, v_in, gain_q, gain_k, d_out, video):
    rows, width = q_in.shape
    heads = width // HSIZE
    steps = heads // PER
    factor = math.log2(math.e) / math.sqrt(HSIZE)
    near_by, along = lax.axis_size("dp") * CORES, lax.axis_size("z")
    groups = near_by * along
    odd = lax.axis_index("core").astype(jnp.int32).reshape(1)
    gq = gain_q.reshape(heads, HSIZE)
    gk = gain_k.reshape(heads, HSIZE)
    packed_rows = 2 * heads * rows + MARK_ROWS
    pair_flops = 2 * rows * rows * HSIZE * heads
    smem = pl.BlockSpec(memory_space=pltpu.SMEM)
    vmem = pl.BlockSpec(memory_space=pltpu.VMEM)
    hbm = pl.BlockSpec(memory_space=pl.ANY)

    def gridded(kernel, name, flops, in_specs, out_specs, out_shape, scratch=(), limit=VMEM_LIMIT):
        return pl.pallas_call(
            kernel,
            grid_spec=pltpu.PrefetchScalarGridSpec(
                num_scalar_prefetch=1, grid=(steps,), in_specs=in_specs, out_specs=out_specs, scratch_shapes=scratch
            ),
            out_shape=out_shape,
            compiler_params=params(limit),
            cost_estimate=cost(flops),
            name=name,
        )

    packed = shape(packed_rows, HSIZE, dtype=BF16)
    a, b, rq, rk = pl.pallas_call(
        functools.partial(pack_kernel, heads),
        out_shape=(packed, packed, shape(rows, HSIZE), shape(rows, HSIZE)),
        in_specs=[smem, smem] + [hbm] * 6,
        out_specs=(hbm,) * 4,
        scratch_shapes=[
            pltpu.VMEM((4, rows, width), BF16),
            pltpu.VMEM((4, heads * rows, HSIZE), BF16),
            pltpu.VMEM((2, heads, HSIZE), F32),
            pltpu.VMEM((MARK_ROWS, HSIZE), BF16),
            pltpu.VMEM((2, rows, HSIZE), F32),
            pltpu.SemaphoreType.DMA((4, SPLIT + 1)),
            pltpu.SemaphoreType.DMA((4, steps + 1)),
        ],
        compiler_params=params(),
        cost_estimate=cost(pair_flops),
        name="pack",
    )(odd, video, q_in, k_in, d_out, v_in, gq, gk)

    cross = [(i, i + 1) for i in range(1, groups - 1, 2)] + [(i, i - 1) for i in range(2, groups, 2)]
    chip = [(i, i ^ 1) for i in range(groups)]
    next_chip = [(i, i + 2) for i in range(0, groups - 2, 2)] + [(i, i - 2) for i in range(3, groups, 2)]
    x1 = lax.ppermute(a, AXES, cross)
    s1 = lax.ppermute(b, AXES, chip)
    x2 = lax.ppermute(s1, AXES, cross)
    x3 = lax.ppermute(x1, AXES, next_chip)
    s2 = lax.ppermute(x1, AXES, chip)
    s3 = lax.ppermute(x2, AXES, chip)

    both = head_blocks(2 * rows)
    if_odd = head_blocks(2 * rows, True)
    if_even = head_blocks(2 * rows, False)
    tall = head_blocks(rows)
    mark = pl.BlockSpec((MARK_ROWS, HSIZE), lambda i, odd: (2 * heads * rows // MARK_ROWS, 0))
    cols = pl.BlockSpec((rows, PER * HSIZE), lambda i, odd: (0, i))
    square = still(rows, HSIZE)
    whole = still(rows, width)
    near = gridded(
        functools.partial(near_kernel, rows, factor), "near", 1024,
        [both, both, if_even, if_odd, if_even, if_odd] + [mark] * 5,
        (tall,) * 3,
        (shape(heads * rows, HSIZE),) * 3,
    )(odd, a, b, x1, s1, x2, s2, a, x1, s1, x2, s2)
    block = pltpu.VMEM((2 * heads * rows, HSIZE), BF16)
    flat = pltpu.VMEM((rows, width), BF16)
    wide = pltpu.VMEM((rows, width), F32)
    marks = lambda count: pltpu.VMEM((count, MARK_ROWS, HSIZE), BF16)
    gain_mem, scale_mem = pltpu.VMEM((heads, HSIZE), F32), pltpu.VMEM((rows, HSIZE), F32)
    sum_mem = pltpu.VMEM((heads * rows, HSIZE), F32)
    whole_shape = shape(rows, width, dtype=BF16)
    dq_in, w, stats = pl.pallas_call(
        functools.partial(query_kernel, rows, heads, factor),
        out_shape=(whole_shape, shape(along, heads, HSIZE, dtype=BF16), shape(2 * heads, rows)),
        in_specs=[smem] + [hbm] * 10,
        out_specs=(hbm,) * 3,
        scratch_shapes=[block, block, sum_mem, sum_mem, sum_mem, flat, gain_mem, scale_mem, marks(2), wide, flat,
                        pltpu.VMEM((along, heads, HSIZE), BF16), pltpu.VMEM((2 * heads, rows), F32),
                        pltpu.SemaphoreType.DMA((5 + 5 * steps,)), pltpu.SemaphoreType.DMA((steps + 2,))],
        compiler_params=params(),
        cost_estimate=cost(1024),
        name="query_side",
    )(odd, a, b, x3, s3, *near, q_in, gq, rq)

    def back(value, by):
        return lax.ppermute(value, AXES, [(i, i - by) for i in range(by, groups)])

    w = lax.all_to_all(w, "z", 0, 0)
    later = [back(stats, by) for by in range(1, WIN)]
    w = pl.pallas_call(
        spread_kernel,
        out_shape=shape(near_by, heads, HSIZE, dtype=BF16),
        in_specs=[vmem] + [hbm] * 3,
        out_specs=vmem,
        compiler_params=params(SMALL_LIMIT),
        cost_estimate=cost(2**20),
        name="spread",
    )(w, *later)
    w = lax.all_to_all(w, ("dp", "core"), 0, 0)
    dgain_q, dgain_k = pl.pallas_call(
        gains_kernel,
        out_shape=(shape(heads, HSIZE),) * 2,
        in_specs=[vmem] * 3,
        out_specs=(vmem,) * 2,
        compiler_params=params(SMALL_LIMIT),
        cost_estimate=cost(2**20),
        name="gains",
    )(w, gq, gk)

    dk_in, dv_in = pl.pallas_call(
        functools.partial(key_kernel, rows, heads, factor),
        out_shape=(whole_shape, whole_shape),
        in_specs=[smem] + [hbm] * 15,
        out_specs=(hbm, hbm),
        scratch_shapes=[block, pltpu.VMEM((WIN, 2 * heads * rows, HSIZE), BF16), pltpu.VMEM((WIN, 2 * heads, rows), F32),
                        flat, gain_mem, scale_mem, marks(WIN), wide, flat, flat,
                        pltpu.SemaphoreType.DMA((2 * WIN + 3 + (WIN + 1) * steps,)), pltpu.SemaphoreType.DMA((2 * steps,))],
        compiler_params=params(KEY_LIMIT),
        cost_estimate=cost(16 * pair_flops),
        name="key_side",
    )(odd, a, b, x1, s1, x2, s2, x3, s3, stats, *later, k_in, gk, rk)
    return dq_in, dk_in, dv_in, dgain_q.reshape(width), dgain_k.reshape(width)


def solution(mesh):
    dp, seq = mesh.devices.shape
    split = Mesh(mesh.devices.reshape(dp, seq // CORES, CORES), AXES)
    rows = P(AXES, None)
    return jax.shard_map(
        body,
        mesh=split,
        in_specs=(rows, rows, rows, P(), P(), rows, P(AXES)),
        out_specs=(rows, rows, rows, P(), P()),
        check_vma=False,
    )
```

time: 114 us -> 111 us (0.974)
  Pallas kernels: 29.4 us -> 26.9 us
    pallas_call x2, Pallas kernels: 16.7 us -> 14.5 us  [the longest x1 8.12 us: body(): pl.pallas_call(functools.partial(key_kernel, rows, heads, factor), out_sh...]
  transfers between devices with their start and end apart: 11 -> 11, of which waited for: 7 -> 8; matrix products, arithmetic and copies ran while one was open for 0% -> 0% of each run, Pallas kernels for 15% -> 14%
where the time goes in v5:
time: 111 us
  starting transfers between devices  42.7 us (38%)
  waiting for transfers between devices  38.5 us (35%)
  Pallas kernels  26.9 us (24%)
  between operations  1.46 us (1%)
  local copies, waits for them, and re-layouts  1.2 us (1%)
    ppermute x1, waiting for transfers between devices, body(): x2 = lax.ppermute(s1, AXES, cross)  18.3 us
    ppermute x1, waiting for transfers between devices, body(): x1 = lax.ppermute(a, AXES, cross)  12.5 us
    all_to_all x1, starting transfers between devices, body(): w = lax.all_to_all(w, ('dp', 'core'), 0, 0)  9.81 us
    all_to_all x1, starting transfers between devices, body(): w = lax.all_to_all(w, 'z', 0, 0)  9.11 us
    ppermute x1, starting transfers between devices, body(): s1 = lax.ppermute(b, AXES, chip)  8.79 us
    pallas_call x1, Pallas kernels, body(): pl.pallas_call(functools.partial(key_kernel, rows, heads, factor), out_sh...  8.12 us
    pallas_call x1, Pallas kernels, body(): gridded(functools.partial(near_kernel, rows, factor), 'near', 1024, [both...  7.76 us
    pallas_call x1, Pallas kernels, body(): pl.pallas_call(functools.partial(query_kernel, rows, heads, factor), out_...  6.33 us
  transfers between devices with their start and end apart: 11, of which 8 were waited for; matrix products, arithmetic and copies ran while one was open for 0% of the time, Pallas kernels for 14%

profile of v5, /device:TPU:1, one launch (start us, length us, event | category | flops | bytes accessed | tf_op | source)
XLA Modules:
  0.0 110.8 jit_solution(13898404670537115466)
XLA Ops:
  1.3 3.3 %pack.1 = (bf16[5136,128]{1,0:T(8,128)(2,1)}, bf16[5136,128]{1,0:T(8,128)(2,1)}, f32[128,128]{1,0:T(8,128)}, f32[128,128]{1,0:T(8,128)}) custom-call(s32[1]{0:T(128)} %bitcast.odd_ref, s32[1]{0:T(128)S(6)} %copy.12.video_ref, bf16[128,2560]{1,0:T(8,128)(2,1)} %q_hbm.3, bf16[128,2560]{1,0:T(8,128)(2,1)} %k_hbm.3, bf16[128,2560]{1,0:T(8,128)(2,1)} %d_hbm.1, ...), custom_call_target="tpu_custom_call" | custom-call | flops 83886080 | bytes 1048576 | tf_op jit(solution)/shard_map/pack/pallas_call | solution.py:452
  4.6 8.8 %collective-permute-start.2 = (bf16[5136,128]{1,0:T(8,128)(2,1)}, bf16[5136,128]{1,0:T(8,128)(2,1)S(1)}, u32[]{:S(2)}, u32[]{:S(2)}) collective-permute-start(bf16[5136,128]{1,0:T(8,128)(2,1)} %get-tuple-element.20.b), channel_id=1, source_target_pairs={{0,1},{1,0},{2,3},{3,2},{4,5},{5,4},{6,7},{7,6},{8,9},{9,8},{10,11... | collective-permute-start | bytes 3944456 | tf_op jit(solution)/shard_map/ppermute | solution.py:475
  13.4 1.9 %collective-permute-start = (bf16[5136,128]{1,0:T(8,128)(2,1)}, bf16[5136,128]{1,0:T(8,128)(2,1)}, u32[]{:S(2)}, u32[]{:S(2)}) collective-permute-start(bf16[5136,128]{1,0:T(8,128)(2,1)} %get-tuple-element.19.a.am), channel_id=1, source_target_pairs={{1,2},{3,4},{5,6},{7,8},{9,10},{11,12},{13,14},{15,16},{17,18},{19... | collective-permute-start | bytes 3944456 | tf_op jit(solution)/shard_map/ppermute | solution.py:474
  15.4 0.9 collective-permute-done.2.s1.s1m
  16.3 1.2 %copy-done.5 = bf16[5136,128]{1,0:T(8,128)(2,1)} copy-done((bf16[5136,128]{1,0:T(8,128)(2,1)}, bf16[5136,128]{1,0:T(8,128)(2,1)S(1)}, u32[]{:S(2)}) %copy-start.5) | copy-done | bytes 1314840
  17.5 2.7 %collective-permute-start.3 = (bf16[5136,128]{1,0:T(8,128)(2,1)S(1)}, bf16[5136,128]{1,0:T(8,128)(2,1)}, u32[]{:S(2)}, u32[]{:S(2)}) collective-permute-start(bf16[5136,128]{1,0:T(8,128)(2,1)S(1)} %collective-permute-done.2.s1.s1m), channel_id=1, source_target_pairs={{1,2},{3,4},{5,6},{7,8},{9,10},{11,12},{13,14},{15,16},{17,18},{19... | collective-permute-start | bytes 3944456 | tf_op jit(solution)/shard_map/ppermute | solution.py:476
  20.2 12.5 %collective-permute-done.x1.x1m = bf16[5136,128]{1,0:T(8,128)(2,1)} collective-permute-done((bf16[5136,128]{1,0:T(8,128)(2,1)}, bf16[5136,128]{1,0:T(8,128)(2,1)}, u32[]{:S(2)}, u32[]{:S(2)}) %collective-permute-start) | collective-permute-done | bytes 1314848 | tf_op jit(solution)/shard_map/ppermute | solution.py:474
  32.7 1.9 %collective-permute-start.5 = (bf16[5136,128]{1,0:T(8,128)(2,1)}, bf16[5136,128]{1,0:T(8,128)(2,1)}, u32[]{:S(2)}, u32[]{:S(2)}) collective-permute-start(bf16[5136,128]{1,0:T(8,128)(2,1)} %collective-permute-done.x1.x1m), channel_id=1, source_target_pairs={{0,1},{1,0},{2,3},{3,2},{4,5},{5,4},{6,7},{7,6},{8,9},{9,8},{10,11... | collective-permute-start | bytes 3944456 | tf_op jit(solution)/shard_map/ppermute | solution.py:478
  34.6 1.3 %collective-permute-start.1 = (bf16[5136,128]{1,0:T(8,128)(2,1)}, bf16[5136,128]{1,0:T(8,128)(2,1)}, u32[]{:S(2)}, u32[]{:S(2)}) collective-permute-start(bf16[5136,128]{1,0:T(8,128)(2,1)} %collective-permute-done.x1.x1m), channel_id=1, source_target_pairs={{0,2},{2,4},{4,6},{6,8},{8,10},{10,12},{12,14},{14,16},{16,18},{18... | collective-permute-start | bytes 3944456 | tf_op jit(solution)/shard_map/ppermute | solution.py:477
  35.9 18.3 %collective-permute-done.3.x2.x2m = bf16[5136,128]{1,0:T(8,128)(2,1)} collective-permute-done((bf16[5136,128]{1,0:T(8,128)(2,1)S(1)}, bf16[5136,128]{1,0:T(8,128)(2,1)}, u32[]{:S(2)}, u32[]{:S(2)}) %collective-permute-start.3) | collective-permute-done | bytes 1314848 | tf_op jit(solution)/shard_map/ppermute | solution.py:476
  54.3 1.9 %collective-permute-start.4 = (bf16[5136,128]{1,0:T(8,128)(2,1)}, bf16[5136,128]{1,0:T(8,128)(2,1)}, u32[]{:S(2)}, u32[]{:S(2)}) collective-permute-start(bf16[5136,128]{1,0:T(8,128)(2,1)} %collective-permute-done.3.x2.x2m), channel_id=1, source_target_pairs={{0,1},{1,0},{2,3},{3,2},{4,5},{5,4},{6,7},{7,6},{8,9},{9,8},{10,11... | collective-permute-start | bytes 3944456 | tf_op jit(solution)/shard_map/ppermute | solution.py:479
  56.2 0.0 collective-permute-done.5.s2.s2m
  56.2 7.8 %near.1 = (f32[2560,128]{1,0:T(8,128)}, f32[2560,128]{1,0:T(8,128)}, f32[2560,128]{1,0:T(8,128)}) custom-call(s32[1]{0:T(128)} %bitcast.odd_ref, bf16[5136,128]{1,0:T(8,128)(2,1)} %get-tuple-element.19.a.am, bf16[5136,128]{1,0:T(8,128)(2,1)} %get-tuple-element.20.b, bf16[5136,128]{1,0:T(8,128)(2,1)} %collective-permute-done.x1.x1m, ...), custom_call_target="tpu_custom_call" | custom-call | flops 1024 | bytes 1048576 | tf_op jit(solution)/shard_map/near/pallas_call | solution.py:489
  64.0 0.0 collective-permute-done.1.x3
  64.0 0.0 collective-permute-done.4.s3
  64.0 6.3 %query_side.1 = (bf16[128,2560]{1,0:T(8,128)(2,1)}, bf16[16,20,128]{2,1,0:T(8,128)(2,1)}, f32[40,128]{1,0:T(8,128)}) custom-call(s32[1]{0:T(128)} %bitcast.odd_ref, bf16[5136,128]{1,0:T(8,128)(2,1)} %get-tuple-element.19.a.am, bf16[5136,128]{1,0:T(8,128)(2,1)} %get-tuple-element.20.b, bf16[5136,128]{1,0:T(8,128)(2,1)} %collective-permute-done.1.x3, ...), custom_call_target="tpu_custom_call" | custom-call | flops 1024 | bytes 1048576 | tf_op jit(solution)/shard_map/query_side/pallas_call | solution.py:502
  70.3 9.1 %all-to-all-start = ((bf16[16,20,128]{2,1,0:T(8,128)(2,1)}), bf16[16,20,128]{2,1,0:T(8,128)(2,1)S(1)}, u32[]{:S(2)}, u32[]{:S(2)}) async-start(bf16[16,20,128]{2,1,0:T(8,128)(2,1)} %get-tuple-element.30), calls=%async_computation | async-start | bytes 196608 | tf_op jit(solution)/shard_map/all_to_all | solution.py:518
  79.4 1.3 %collective-permute-start.8 = (f32[40,128]{1,0:T(8,128)}, f32[40,128]{1,0:T(8,128)S(1)}, u32[]{:S(2)}, u32[]{:S(2)}) collective-permute-start(f32[40,128]{1,0:T(8,128)} %get-tuple-element.26.t0), channel_id=1, source_target_pairs={{3,0},{4,1},{5,2},{6,3},{7,4},{8,5},{9,6},{10,7},{11,8},{12,9},{13... | collective-permute-start | bytes 61448 | tf_op jit(solution)/shard_map/ppermute | solution.py:516
  80.7 1.3 %collective-permute-start.7 = (f32[40,128]{1,0:T(8,128)}, f32[40,128]{1,0:T(8,128)S(1)}, u32[]{:S(2)}, u32[]{:S(2)}) collective-permute-start(f32[40,128]{1,0:T(8,128)} %get-tuple-element.26.t0), channel_id=1, source_target_pairs={{2,0},{3,1},{4,2},{5,3},{6,4},{7,5},{8,6},{9,7},{10,8},{11,9},{12,... | collective-permute-start | bytes 61448 | tf_op jit(solution)/shard_map/ppermute | solution.py:516
  82.0 2.7 %collective-permute-start.6 = (f32[40,128]{1,0:T(8,128)}, f32[40,128]{1,0:T(8,128)S(1)}, u32[]{:S(2)}, u32[]{:S(2)}) collective-permute-start(f32[40,128]{1,0:T(8,128)} %get-tuple-element.26.t0), channel_id=1, source_target_pairs={{1,0},{2,1},{3,2},{4,3},{5,4},{6,5},{7,6},{8,7},{9,8},{10,9},{11,1... | collective-permute-start | bytes 61448 | tf_op jit(solution)/shard_map/ppermute | solution.py:516
  84.7 2.2 %collective-permute-done.8.t3.three_ref = f32[40,128]{1,0:T(8,128)S(1)} collective-permute-done((f32[40,128]{1,0:T(8,128)}, f32[40,128]{1,0:T(8,128)S(1)}, u32[]{:S(2)}, u32[]{:S(2)}) %collective-permute-start.8) | collective-permute-done | bytes 20512 | tf_op jit(solution)/shard_map/ppermute | solution.py:516
  86.9 0.8 collective-permute-done.7.t2.two_ref
  87.7 1.3 %collective-permute-done.6.t1.one_ref = f32[40,128]{1,0:T(8,128)S(1)} collective-permute-done((f32[40,128]{1,0:T(8,128)}, f32[40,128]{1,0:T(8,128)S(1)}, u32[]{:S(2)}, u32[]{:S(2)}) %collective-permute-start.6) | collective-permute-done | bytes 20512 | tf_op jit(solution)/shard_map/ppermute | solution.py:516
  89.0 2.3 %all-to-all-done.part_ref = bf16[16,20,128]{2,1,0:T(8,128)(2,1)S(1)} async-done(((bf16[16,20,128]{2,1,0:T(8,128)(2,1)}), bf16[16,20,128]{2,1,0:T(8,128)(2,1)S(1)}, u32[]{:S(2)}, u32[]{:S(2)}) %all-to-all-start) | async-done | bytes 81952 | tf_op jit(solution)/shard_map/all_to_all | solution.py:518
  91.3 0.7 spread.1
  92.0 9.8 %all-to-all-start.1 = ((bf16[32,20,128]{2,1,0:T(8,128)(2,1)}), bf16[32,20,128]{2,1,0:T(8,128)(2,1)S(1)}, u32[]{:S(2)}, u32[]{:S(2)}) async-start(bf16[32,20,128]{2,1,0:T(8,128)(2,1)} %spread.1), calls=%async_computation.1 | async-start | bytes 393216 | tf_op jit(solution)/shard_map/all_to_all | solution.py:529
  101.9 0.0 copy-start
  101.9 0.0 copy-start.1
  101.9 8.1 %key_side.1 = (bf16[128,2560]{1,0:T(8,128)(2,1)}, bf16[128,2560]{1,0:T(8,128)(2,1)}) custom-call(s32[1]{0:T(128)} %bitcast.odd_ref, bf16[5136,128]{1,0:T(8,128)(2,1)} %get-tuple-element.19.a.am, bf16[5136,128]{1,0:T(8,128)(2,1)} %get-tuple-element.20.b, bf16[5136,128]{1,0:T(8,128)(2,1)} %collective-permute-done.x1.x1m, bf16[5136,128]{1,0:T(8,128)(2,1)} %copy-done.5, ...), custom_call_target="tpu_custom_call" | custom-call | flops 1342177280 | bytes 1048576 | tf_op jit(solution)/shard_map/key_side/pallas_call | solution.py:540
  110.1 0.1 all-to-all-done.1.part_ref
  110.1 0.0 copy-done
  110.1 0.7 gains.1
  (8 shorter events, 0.0 us)
Async XLA Ops:
  4.6 11.7 %collective-permute-start.2 = (bf16[5136,128]{1,0:T(8,128)(2,1)}, bf16[5136,128]{1,0:T(8,128)(2,1)S(1)}, u32[]{:S(2)}, u32[]{:S(2)}) collective-permute-start(bf16[5136,128]{1,0:T(8,128)(2,1)} %get-tuple-element.20.b), channel_id=1, source_target_pairs={{0,1},{1,0},{2,3},{3,2},{4,5},{5,4},{6,7},{7,6},{8,9},{9,8},{10,11... | collective-permute-start | bytes 3944456 | tf_op jit(solution)/shard_map/ppermute | solution.py:475
  13.4 19.3 %collective-permute-start = (bf16[5136,128]{1,0:T(8,128)(2,1)}, bf16[5136,128]{1,0:T(8,128)(2,1)}, u32[]{:S(2)}, u32[]{:S(2)}) collective-permute-start(bf16[5136,128]{1,0:T(8,128)(2,1)} %get-tuple-element.19.a.am), channel_id=1, source_target_pairs={{1,2},{3,4},{5,6},{7,8},{9,10},{11,12},{13,14},{15,16},{17,18},{19... | collective-permute-start | bytes 3944456 | tf_op jit(solution)/shard_map/ppermute | solution.py:474
  16.3 1.2 %copy-start.5 = (bf16[5136,128]{1,0:T(8,128)(2,1)}, bf16[5136,128]{1,0:T(8,128)(2,1)S(1)}, u32[]{:S(2)}) copy-start(bf16[5136,128]{1,0:T(8,128)(2,1)S(1)} %collective-permute-done.2.s1.s1m) | copy-start | bytes 3944452
  17.5 36.8 %collective-permute-start.3 = (bf16[5136,128]{1,0:T(8,128)(2,1)S(1)}, bf16[5136,128]{1,0:T(8,128)(2,1)}, u32[]{:S(2)}, u32[]{:S(2)}) collective-permute-start(bf16[5136,128]{1,0:T(8,128)(2,1)S(1)} %collective-permute-done.2.s1.s1m), channel_id=1, source_target_pairs={{1,2},{3,4},{5,6},{7,8},{9,10},{11,12},{13,14},{15,16},{17,18},{19... | collective-permute-start | bytes 3944456 | tf_op jit(solution)/shard_map/ppermute | solution.py:476
  32.7 23.5 %collective-permute-start.5 = (bf16[5136,128]{1,0:T(8,128)(2,1)}, bf16[5136,128]{1,0:T(8,128)(2,1)}, u32[]{:S(2)}, u32[]{:S(2)}) collective-permute-start(bf16[5136,128]{1,0:T(8,128)(2,1)} %collective-permute-done.x1.x1m), channel_id=1, source_target_pairs={{0,1},{1,0},{2,3},{3,2},{4,5},{5,4},{6,7},{7,6},{8,9},{9,8},{10,11... | collective-permute-start | bytes 3944456 | tf_op jit(solution)/shard_map/ppermute | solution.py:478
  34.6 29.3 %collective-permute-start.1 = (bf16[5136,128]{1,0:T(8,128)(2,1)}, bf16[5136,128]{1,0:T(8,128)(2,1)}, u32[]{:S(2)}, u32[]{:S(2)}) collective-permute-start(bf16[5136,128]{1,0:T(8,128)(2,1)} %collective-permute-done.x1.x1m), channel_id=1, source_target_pairs={{0,2},{2,4},{4,6},{6,8},{8,10},{10,12},{12,14},{14,16},{16,18},{18... | collective-permute-start | bytes 3944456 | tf_op jit(solution)/shard_map/ppermute | solution.py:477
  54.3 9.7 %collective-permute-start.4 = (bf16[5136,128]{1,0:T(8,128)(2,1)}, bf16[5136,128]{1,0:T(8,128)(2,1)}, u32[]{:S(2)}, u32[]{:S(2)}) collective-permute-start(bf16[5136,128]{1,0:T(8,128)(2,1)} %collective-permute-done.3.x2.x2m), channel_id=1, source_target_pairs={{0,1},{1,0},{2,3},{3,2},{4,5},{5,4},{6,7},{7,6},{8,9},{9,8},{10,11... | collective-permute-start | bytes 3944456 | tf_op jit(solution)/shard_map/ppermute | solution.py:479
  70.3 21.0 %all-to-all-start = ((bf16[16,20,128]{2,1,0:T(8,128)(2,1)}), bf16[16,20,128]{2,1,0:T(8,128)(2,1)S(1)}, u32[]{:S(2)}, u32[]{:S(2)}) async-start(bf16[16,20,128]{2,1,0:T(8,128)(2,1)} %get-tuple-element.30), calls=%async_computation | async-start | bytes 196608 | tf_op jit(solution)/shard_map/all_to_all | solution.py:518
  79.4 7.5 %collective-permute-start.8 = (f32[40,128]{1,0:T(8,128)}, f32[40,128]{1,0:T(8,128)S(1)}, u32[]{:S(2)}, u32[]{:S(2)}) collective-permute-start(f32[40,128]{1,0:T(8,128)} %get-tuple-element.26.t0), channel_id=1, source_target_pairs={{3,0},{4,1},{5,2},{6,3},{7,4},{8,5},{9,6},{10,7},{11,8},{12,9},{13... | collective-permute-start | bytes 61448 | tf_op jit(solution)/shard_map/ppermute | solution.py:516
  80.7 7.0 %collective-permute-start.7 = (f32[40,128]{1,0:T(8,128)}, f32[40,128]{1,0:T(8,128)S(1)}, u32[]{:S(2)}, u32[]{:S(2)}) collective-permute-start(f32[40,128]{1,0:T(8,128)} %get-tuple-element.26.t0), channel_id=1, source_target_pairs={{2,0},{3,1},{4,2},{5,3},{6,4},{7,5},{8,6},{9,7},{10,8},{11,9},{12,... | collective-permute-start | bytes 61448 | tf_op jit(solution)/shard_map/ppermute | solution.py:516
  82.0 7.0 %collective-permute-start.6 = (f32[40,128]{1,0:T(8,128)}, f32[40,128]{1,0:T(8,128)S(1)}, u32[]{:S(2)}, u32[]{:S(2)}) collective-permute-start(f32[40,128]{1,0:T(8,128)} %get-tuple-element.26.t0), channel_id=1, source_target_pairs={{1,0},{2,1},{3,2},{4,3},{5,4},{6,5},{7,6},{8,7},{9,8},{10,9},{11,1... | collective-permute-start | bytes 61448 | tf_op jit(solution)/shard_map/ppermute | solution.py:516
  86.9 14.9 %copy-start.2 = (f32[40,128]{1,0:T(8,128)}, f32[40,128]{1,0:T(8,128)S(1)}, u32[]{:S(2)}) copy-start(f32[40,128]{1,0:T(8,128)S(1)} %collective-permute-done.8.t3.three_ref) | copy-start | bytes 61444
  87.7 14.2 %copy-start.3 = (f32[40,128]{1,0:T(8,128)}, f32[40,128]{1,0:T(8,128)S(1)}, u32[]{:S(2)}) copy-start(f32[40,128]{1,0:T(8,128)S(1)} %collective-permute-done.7.t2.two_ref) | copy-start | bytes 61444
  89.0 12.8 %copy-start.4 = (f32[40,128]{1,0:T(8,128)}, f32[40,128]{1,0:T(8,128)S(1)}, u32[]{:S(2)}) copy-start(f32[40,128]{1,0:T(8,128)S(1)} %collective-permute-done.6.t1.one_ref) | copy-start | bytes 61444
  92.0 18.1 %all-to-all-start.1 = ((bf16[32,20,128]{2,1,0:T(8,128)(2,1)}), bf16[32,20,128]{2,1,0:T(8,128)(2,1)S(1)}, u32[]{:S(2)}, u32[]{:S(2)}) async-start(bf16[32,20,128]{2,1,0:T(8,128)(2,1)} %spread.1), calls=%async_computation.1 | async-start | bytes 393216 | tf_op jit(solution)/shard_map/all_to_all | solution.py:529
  101.9 8.2 %copy-start = (f32[2560]{0:T(1024)S(1)}, f32[2560]{0:T(1024)}, u32[]{:S(2)}) copy-start(f32[2560]{0:T(1024)} %param.11) | copy-start | bytes 30724
  101.9 8.2 %copy-start.1 = (f32[2560]{0:T(1024)S(1)}, f32[2560]{0:T(1024)}, u32[]{:S(2)}) copy-start(f32[2560]{0:T(1024)} %param.10) | copy-start | bytes 30724

commit v6 on v5

--- a/solution.py
+++ b/solution.py
@@ -121,6 +121,10 @@
         copy.wait()
 
 
+def gate_kernel(*refs):
+    del refs
+
+
 def mark_of(ref):
     return ref[0:1, 0:1].astype(F32)
 
@@ -134,11 +138,51 @@
     return jnp.concatenate([jnp.broadcast_to(bias, (1, rows)) for bias in biases], axis=1)
 
 
-def near_kernel(rows, factor, odd_ref, a, b, x1, s1, x2, s2, am, x1m, s1m, x2m, s2m, g_ref, h_ref, stat_ref):
+def softmax_part(best, score, dprob):
+    prob = jnp.exp2(score - best)
+    return prob, jnp.sum(prob, axis=-1, keepdims=True), jnp.sum(prob * dprob, axis=-1, keepdims=True)
+
+
+def left_half(rows):
+    return lax.broadcasted_iota(jnp.int32, (rows, HSIZE), 1) < HSIZE // 2
+
+
+def halves(tile, left):
+    turned = pltpu.roll(tile, HSIZE // 2, 1)
+    return jnp.where(left, tile, turned), jnp.where(left, turned, tile)
+
+
+def own_kernel(rows, factor, odd_ref, a, b, g_ref, h_ref, stat_ref):
     odd = odd_ref[0] == 1
-    bias = bias_row([jnp.zeros((1, 1), F32), bias_of(am, odd, s1m, x1m), bias_of(am, odd, s2m, x2m)], rows)
-    pairs = ((a, b), (s1, x1), (s2, x2))
-    left = lax.broadcasted_iota(jnp.int32, (rows, HSIZE), 1) < HSIZE // 2
+    left = left_half(rows)
+    keys, scores, dprobs = [], [], []
+    for j in range(PER):
+        top = head_rows(j, rows)
+        low = head_rows(PER + j, rows)
+        at, bt, al, bl = a[top, :], b[top, :], a[low, :], b[low, :]
+        keys.append(jnp.where(odd, at, bt))
+        scores.append(dot_nt(jnp.where(odd, bt, at), keys[j]))
+        dprobs.append(dot_nt(jnp.where(odd, bl, al), jnp.where(odd, al, bl)))
+    for j in range(PER):
+        out = head_rows(j, rows)
+        score = scores[j] * factor
+        best = jnp.max(score, axis=-1, keepdims=True)
+        prob, total, mixed = softmax_part(best, score, dprobs[j])
+        inverse = 1.0 / total
+        delta = mixed * inverse
+        prob = prob * inverse
+        both = jnp.concatenate([(prob * (dprobs[j] - delta)).astype(BF16), prob.astype(BF16)], axis=0)
+        sums = dot_nn(both, keys[j])
+        g_ref[out, :] = sums[:rows]
+        h_ref[out, :] = sums[rows:]
+        stat_ref[out, :] = jnp.where(left, best + jnp.log2(total), delta)
+
+
+def near_kernel(rows, factor, odd_ref, a, b, x1, s1, x2, s2, am, x1m, s1m, x2m, s2m, g0, h0, stat0, g_ref, h_ref, stat_ref):
+    odd = odd_ref[0] == 1
+    bias = bias_row([bias_of(am, odd, s1m, x1m), bias_of(am, odd, s2m, x2m)], rows)
+    pairs = ((s1, x1), (s2, x2))
+    left = left_half(rows)
     keys, scores, dprobs = [], [], []
     for j in range(PER):
         top = head_rows(j, rows)
@@ -151,17 +195,21 @@
         dprobs.append(dot_nt(d_out, vals))
     for j in range(PER):
         out = head_rows(j, rows)
+        old_lse, old_delta = halves(stat0[out, :], left)
         score = scores[j] * factor + bias
-        best = jnp.max(score, axis=-1, keepdims=True)
-        probs = jnp.exp2(score - best)
-        total = jnp.sum(probs, axis=-1, keepdims=True)
+        best = jnp.maximum(old_lse, jnp.max(score, axis=-1, keepdims=True))
+        kept = jnp.exp2(old_lse - best)
+        prob, total, mixed = softmax_part(jnp.concatenate([best, best], axis=1), score, dprobs[j])
+        total = kept + total
         inverse = 1.0 / total
-        probs = probs * inverse
-        delta = jnp.sum(probs * dprobs[j], axis=-1, keepdims=True)
-        both = jnp.concatenate([(probs * (dprobs[j] - delta)).astype(BF16), probs.astype(BF16)], axis=0)
+        kept = kept * inverse
+        delta = kept * old_delta + mixed * inverse
+        inverse, change = [jnp.concatenate([value, value], axis=1) for value in (inverse, delta)]
+        prob = prob * inverse
+        both = jnp.concatenate([(prob * (dprobs[j] - change)).astype(BF16), prob.astype(BF16)], axis=0)
         sums = dot_nn(both, keys[j])
-        g_ref[out, :] = sums[:rows]
-        h_ref[out, :] = sums[rows:]
+        g_ref[out, :] = sums[:rows] + kept * (g0[out, :] + (old_delta - delta) * h0[out, :])
+        h_ref[out, :] = sums[rows:] + kept * h0[out, :]
         stat_ref[out, :] = jnp.where(left, best + jnp.log2(total), delta)
 
 
@@ -257,10 +305,7 @@
         fars, nears = [], []
         for j in range(PER):
             head = step * PER + j
-            old = near_mem[head_rows(head, rows), :]
-            turned = pltpu.roll(old, HSIZE // 2, 1)
-            old_lse = jnp.where(left, old, turned)
-            old_delta = jnp.where(left, turned, old)
+            old_lse, old_delta = halves(near_mem[head_rows(head, rows), :], left)
             score = scores[j] * factor + bias
             best = jnp.maximum(old_lse, jnp.max(score, axis=-1, keepdims=True))
             prob = jnp.exp2(score - best)
@@ -436,6 +481,18 @@
     vmem = pl.BlockSpec(memory_space=pltpu.VMEM)
     hbm = pl.BlockSpec(memory_space=pl.ANY)
 
+    def after(value, flops, *others):
+        return pl.pallas_call(
+            gate_kernel,
+            out_shape=jax.ShapeDtypeStruct(value.shape, value.dtype),
+            in_specs=[hbm] * (1 + len(others)),
+            out_specs=hbm,
+            input_output_aliases={0: 0},
+            compiler_params=params(),
+            cost_estimate=cost(flops),
+            name="gate",
+        )(value, *others)
+
     def gridded(kernel, name, flops, in_specs, out_specs, out_shape, scratch=(), limit=VMEM_LIMIT):
         return pl.pallas_call(
             kernel,
@@ -471,13 +528,6 @@
     cross = [(i, i + 1) for i in range(1, groups - 1, 2)] + [(i, i - 1) for i in range(2, groups, 2)]
     chip = [(i, i ^ 1) for i in range(groups)]
     next_chip = [(i, i + 2) for i in range(0, groups - 2, 2)] + [(i, i - 2) for i in range(3, groups, 2)]
-    x1 = lax.ppermute(a, AXES, cross)
-    s1 = lax.ppermute(b, AXES, chip)
-    x2 = lax.ppermute(s1, AXES, cross)
-    x3 = lax.ppermute(x1, AXES, next_chip)
-    s2 = lax.ppermute(x1, AXES, chip)
-    s3 = lax.ppermute(x2, AXES, chip)
-
     both = head_blocks(2 * rows)
     if_odd = head_blocks(2 * rows, True)
     if_even = head_blocks(2 * rows, False)
@@ -486,12 +536,24 @@
     cols = pl.BlockSpec((rows, PER * HSIZE), lambda i, odd: (0, i))
     square = still(rows, HSIZE)
     whole = still(rows, width)
+    sums_shape = (shape(heads * rows, HSIZE),) * 3
+    x1 = after(lax.ppermute(a, AXES, cross), 2 * pair_flops)
+    sums = gridded(
+        functools.partial(own_kernel, rows, factor), "own", 1024, [both, both], (tall,) * 3, sums_shape
+    )(odd, a, b)
+    b = after(b, 0, sums[2])
+    x2 = lax.ppermute(b, AXES, next_chip)
+    x3 = after(lax.ppermute(x1, AXES, next_chip), pair_flops)
+    s1 = lax.ppermute(b, AXES, chip)
+    s2 = lax.ppermute(x1, AXES, chip)
+    s3 = lax.ppermute(x2, AXES, chip)
+
     near = gridded(
         functools.partial(near_kernel, rows, factor), "near", 1024,
-        [both, both, if_even, if_odd, if_even, if_odd] + [mark] * 5,
+        [if_even, if_odd, if_even, if_odd, if_even, if_odd] + [mark] * 5 + [tall] * 3,
         (tall,) * 3,
-        (shape(heads * rows, HSIZE),) * 3,
-    )(odd, a, b, x1, s1, x2, s2, a, x1, s1, x2, s2)
+        sums_shape,
+    )(odd, a, b, x1, s1, x2, s2, a, x1, s1, x2, s2, *sums)
     block = pltpu.VMEM((2 * heads * rows, HSIZE), BF16)
     flat = pltpu.VMEM((rows, width), BF16)
     wide = pltpu.VMEM((rows, width), F32)

time: 111 us -> 109 us (0.982)
  waiting for transfers between devices: 38.5 us -> 22.9 us
  starting transfers between devices: 42.7 us -> 50.4 us
  Pallas kernels: 26.9 us -> 33.3 us
  local copies, waits for them, and re-layouts: 1.2 us -> 0.02 us
    ppermute x3, waiting for transfers between devices: 30.9 us -> 16.6 us  [the longest x1 7.25 us: body(): x1 = after(lax.ppermute(a, AXES, cross), 2 * pair_flops)]
    pallas_call x1 -> x5, Pallas kernels: 7.76 us -> 14.1 us  [the longest x1 8.5 us: body(): gridded(functools.partial(near_kernel, rows, factor), 'near', 1024, [if_e...]
    all_to_all x1, starting transfers between devices: 9.11 us -> 15 us  [body(): w = lax.all_to_all(w, 'z', 0, 0)]
    all_to_all x1, waiting for transfers between devices: 2.26 us -> 0.01 us  [body(): w = lax.all_to_all(w, 'z', 0, 0)]
    ppermute x1, starting transfers between devices: 8.79 us -> 6.63 us  [body(): s1 = lax.ppermute(b, AXES, chip)]
    ppermute x3, waiting for transfers between devices: 4.3 us -> 6.18 us  [back(): return lax.ppermute(value, AXES, [(i, i - by) for i in range(by, groups)])]
    ppermute x3, starting transfers between devices: 5.93 us -> 7.54 us  [the longest x1 4.96 us: body(): x1 = after(lax.ppermute(a, AXES, cross), 2 * pair_flops)]
    ppermute x3, starting transfers between devices: 5.28 us -> 6.85 us  [back(): return lax.ppermute(value, AXES, [(i, i - by) for i in range(by, groups)])]
  transfers between devices with their start and end apart: 11 -> 11, of which waited for: 8 -> 7; matrix products, arithmetic and copies ran while one was open for 0% -> 0% of each run, Pallas kernels for 14% -> 21%
where the time goes in v6:
time: 109 us; the launch traced here: 108 us
  starting transfers between devices  50.4 us (46%)
  Pallas kernels  33.3 us (31%)
  waiting for transfers between devices  22.9 us (21%)
  between operations  1.46 us (1%)
    all_to_all x1, starting transfers between devices, body(): w = lax.all_to_all(w, 'z', 0, 0)  15 us
    all_to_all x1, starting transfers between devices, body(): w = lax.all_to_all(w, ('dp', 'core'), 0, 0)  10.6 us
    pallas_call x1, Pallas kernels, body(): gridded(functools.partial(near_kernel, rows, factor), 'near', 1024, [if_e...  8.5 us
    pallas_call x1, Pallas kernels, body(): pl.pallas_call(functools.partial(key_kernel, rows, heads, factor), out_sh...  8.12 us
    ppermute x1, waiting for transfers between devices, body(): x1 = after(lax.ppermute(a, AXES, cross), 2 * pair_flops)  7.25 us
    ppermute x3, starting transfers between devices, back(): return lax.ppermute(value, AXES, [(i, i - by) for i in range(by, groups)])  6.85 us
    ppermute x1, starting transfers between devices, body(): s1 = lax.ppermute(b, AXES, chip)  6.63 us
    pallas_call x1, Pallas kernels, body(): pl.pallas_call(functools.partial(query_kernel, rows, heads, factor), out_...  6.33 us
  transfers between devices with their start and end apart: 11, of which 7 were waited for; matrix products, arithmetic and copies ran while one was open for 0% of the time, Pallas kernels for 21%

profile of v6, /device:TPU:1, one launch (start us, length us, event | category | flops | bytes accessed | tf_op | source)
XLA Modules:
  0.0 108.1 jit_solution(6839137618285984980)
XLA Ops:
  1.3 3.3 %pack.1 = (bf16[5136,128]{1,0:T(8,128)(2,1)}, bf16[5136,128]{1,0:T(8,128)(2,1)}, f32[128,128]{1,0:T(8,128)}, f32[128,128]{1,0:T(8,128)}) custom-call(s32[1]{0:T(128)} %bitcast.odd_ref, s32[1]{0:T(128)S(6)} %copy.18.video_ref, bf16[128,2560]{1,0:T(8,128)(2,1)} %q_hbm.3, bf16[128,2560]{1,0:T(8,128)(2,1)} %k_hbm.3, bf16[128,2560]{1,0:T(8,128)(2,1)} %d_hbm.1, ...), custom_call_target="tpu_custom_call" | custom-call | flops 83886080 | bytes 1048576 | tf_op jit(solution)/shard_map/pack/pallas_call | solution.py:509
  4.6 5.0 %collective-permute-start = (bf16[5136,128]{1,0:T(8,128)(2,1)}, bf16[5136,128]{1,0:T(8,128)(2,1)}, u32[]{:S(2)}, u32[]{:S(2)}) collective-permute-start(bf16[5136,128]{1,0:T(8,128)(2,1)} %get-tuple-element.22.a.am), channel_id=1, source_target_pairs={{1,2},{3,4},{5,6},{7,8},{9,10},{11,12},{13,14},{15,16},{17,18},{19... | collective-permute-start | bytes 3944456 | tf_op jit(solution)/shard_map/ppermute | solution.py:540
  9.6 5.6 %own.1 = (f32[2560,128]{1,0:T(8,128)}, f32[2560,128]{1,0:T(8,128)}, f32[2560,128]{1,0:T(8,128)}) custom-call(s32[1]{0:T(128)} %bitcast.odd_ref, bf16[5136,128]{1,0:T(8,128)(2,1)} %get-tuple-element.22.a.am, bf16[5136,128]{1,0:T(8,128)(2,1)} %get-tuple-element.23.b.refs_0_), custom_call_target="tpu_custom_call" | custom-call | flops 1024 | bytes 1048576 | tf_op jit(solution)/shard_map/own/pallas_call | solution.py:541
  15.2 1.3 %collective-permute-start.2 = (bf16[5136,128]{1,0:T(8,128)(2,1)}, bf16[5136,128]{1,0:T(8,128)(2,1)}, u32[]{:S(2)}, u32[]{:S(2)}) collective-permute-start(bf16[5136,128]{1,0:T(8,128)(2,1)} %gate.3.b), channel_id=1, source_target_pairs={{0,2},{2,4},{4,6},{6,8},{8,10},{10,12},{12,14},{14,16},{16,18},{18... | collective-permute-start | bytes 3944456 | tf_op jit(solution)/shard_map/ppermute | solution.py:545
  16.5 6.6 %collective-permute-start.4 = (bf16[5136,128]{1,0:T(8,128)(2,1)}, bf16[5136,128]{1,0:T(8,128)(2,1)}, u32[]{:S(2)}, u32[]{:S(2)}) collective-permute-start(bf16[5136,128]{1,0:T(8,128)(2,1)} %gate.3.b), channel_id=1, source_target_pairs={{0,1},{1,0},{2,3},{3,2},{4,5},{5,4},{6,7},{7,6},{8,9},{9,8},{10,11... | collective-permute-start | bytes 3944456 | tf_op jit(solution)/shard_map/ppermute | solution.py:547
  23.1 7.3 %collective-permute-done.refs_0_ = bf16[5136,128]{1,0:T(8,128)(2,1)} collective-permute-done((bf16[5136,128]{1,0:T(8,128)(2,1)}, bf16[5136,128]{1,0:T(8,128)(2,1)}, u32[]{:S(2)}, u32[]{:S(2)}) %collective-permute-start) | collective-permute-done | bytes 1314848 | tf_op jit(solution)/shard_map/ppermute | solution.py:540
  30.4 1.9 %collective-permute-start.5 = (bf16[5136,128]{1,0:T(8,128)(2,1)}, bf16[5136,128]{1,0:T(8,128)(2,1)}, u32[]{:S(2)}, u32[]{:S(2)}) collective-permute-start(bf16[5136,128]{1,0:T(8,128)(2,1)} %gate.4.x1.x1m), channel_id=1, source_target_pairs={{0,1},{1,0},{2,3},{3,2},{4,5},{5,4},{6,7},{7,6},{8,9},{9,8},{10,11... | collective-permute-start | bytes 3944456 | tf_op jit(solution)/shard_map/ppermute | solution.py:548
  32.3 1.3 %collective-permute-start.1 = (bf16[5136,128]{1,0:T(8,128)(2,1)}, bf16[5136,128]{1,0:T(8,128)(2,1)}, u32[]{:S(2)}, u32[]{:S(2)}) collective-permute-start(bf16[5136,128]{1,0:T(8,128)(2,1)} %gate.4.x1.x1m), channel_id=1, source_target_pairs={{0,2},{2,4},{4,6},{6,8},{8,10},{10,12},{12,14},{14,16},{16,18},{18... | collective-permute-start | bytes 3944456 | tf_op jit(solution)/shard_map/ppermute | solution.py:546
  33.6 5.7 %collective-permute-done.2.x2.x2m = bf16[5136,128]{1,0:T(8,128)(2,1)} collective-permute-done((bf16[5136,128]{1,0:T(8,128)(2,1)}, bf16[5136,128]{1,0:T(8,128)(2,1)}, u32[]{:S(2)}, u32[]{:S(2)}) %collective-permute-start.2) | collective-permute-done | bytes 1314848 | tf_op jit(solution)/shard_map/ppermute | solution.py:545
  39.3 1.9 %collective-permute-start.3 = (bf16[5136,128]{1,0:T(8,128)(2,1)}, bf16[5136,128]{1,0:T(8,128)(2,1)}, u32[]{:S(2)}, u32[]{:S(2)}) collective-permute-start(bf16[5136,128]{1,0:T(8,128)(2,1)} %collective-permute-done.2.x2.x2m), channel_id=1, source_target_pairs={{0,1},{1,0},{2,3},{3,2},{4,5},{5,4},{6,7},{7,6},{8,9},{9,8},{10,11... | collective-permute-start | bytes 3944456 | tf_op jit(solution)/shard_map/ppermute | solution.py:549
  41.2 0.0 collective-permute-done.4.s1.s1m
  41.3 0.0 collective-permute-done.5.s2.s2m
  41.3 8.5 %near.1 = (f32[2560,128]{1,0:T(8,128)}, f32[2560,128]{1,0:T(8,128)}, f32[2560,128]{1,0:T(8,128)}) custom-call(s32[1]{0:T(128)} %bitcast.odd_ref, bf16[5136,128]{1,0:T(8,128)(2,1)} %get-tuple-element.22.a.am, bf16[5136,128]{1,0:T(8,128)(2,1)} %gate.3.b, bf16[5136,128]{1,0:T(8,128)(2,1)} %gate.4.x1.x1m, bf16[5136,128]{1,0:T(8,128)(2,1)} %collective-permute-done.4.s1.s1m, ...), custom_call_target="tpu_custom_call" | custom-call | flops 1024 | bytes 1048576 | tf_op jit(solution)/shard_map/near/pallas_call | solution.py:551
  49.8 3.6 %collective-permute-done.1.refs_0_ = bf16[5136,128]{1,0:T(8,128)(2,1)} collective-permute-done((bf16[5136,128]{1,0:T(8,128)(2,1)}, bf16[5136,128]{1,0:T(8,128)(2,1)}, u32[]{:S(2)}, u32[]{:S(2)}) %collective-permute-start.1) | collective-permute-done | bytes 1314848 | tf_op jit(solution)/shard_map/ppermute | solution.py:546
  53.4 0.0 collective-permute-done.3.s3
  53.4 6.3 %query_side.1 = (bf16[128,2560]{1,0:T(8,128)(2,1)}, bf16[16,20,128]{2,1,0:T(8,128)(2,1)}, f32[40,128]{1,0:T(8,128)}) custom-call(s32[1]{0:T(128)} %bitcast.odd_ref, bf16[5136,128]{1,0:T(8,128)(2,1)} %get-tuple-element.22.a.am, bf16[5136,128]{1,0:T(8,128)(2,1)} %gate.3.b, bf16[5136,128]{1,0:T(8,128)(2,1)} %gate.5.x3, ...), custom_call_target="tpu_custom_call" | custom-call | flops 1024 | bytes 1048576 | tf_op jit(solution)/shard_map/query_side/pallas_call | solution.py:564
  59.8 15.0 %all-to-all-start = ((bf16[16,20,128]{2,1,0:T(8,128)(2,1)}), bf16[16,20,128]{2,1,0:T(8,128)(2,1)S(1)}, u32[]{:S(2)}, u32[]{:S(2)}) async-start(bf16[16,20,128]{2,1,0:T(8,128)(2,1)} %get-tuple-element.36), calls=%async_computation | async-start | bytes 196608 | tf_op jit(solution)/shard_map/all_to_all | solution.py:580
  74.8 4.3 %collective-permute-start.6 = (f32[40,128]{1,0:T(8,128)}, f32[40,128]{1,0:T(8,128)S(1)}, u32[]{:S(2)}, u32[]{:S(2)}) collective-permute-start(f32[40,128]{1,0:T(8,128)} %get-tuple-element.32.t0), channel_id=1, source_target_pairs={{1,0},{2,1},{3,2},{4,3},{5,4},{6,5},{7,6},{8,7},{9,8},{10,9},{11,1... | collective-permute-start | bytes 61448 | tf_op jit(solution)/shard_map/ppermute | solution.py:578
  79.0 1.3 %collective-permute-start.7 = (f32[40,128]{1,0:T(8,128)}, f32[40,128]{1,0:T(8,128)S(1)}, u32[]{:S(2)}, u32[]{:S(2)}) collective-permute-start(f32[40,128]{1,0:T(8,128)} %get-tuple-element.32.t0), channel_id=1, source_target_pairs={{2,0},{3,1},{4,2},{5,3},{6,4},{7,5},{8,6},{9,7},{10,8},{11,9},{12,... | collective-permute-start | bytes 61448 | tf_op jit(solution)/shard_map/ppermute | solution.py:578
  80.3 1.3 %collective-permute-start.8 = (f32[40,128]{1,0:T(8,128)}, f32[40,128]{1,0:T(8,128)S(1)}, u32[]{:S(2)}, u32[]{:S(2)}) collective-permute-start(f32[40,128]{1,0:T(8,128)} %get-tuple-element.32.t0), channel_id=1, source_target_pairs={{3,0},{4,1},{5,2},{6,3},{7,4},{8,5},{9,6},{10,7},{11,8},{12,9},{13... | collective-permute-start | bytes 61448 | tf_op jit(solution)/shard_map/ppermute | solution.py:578
  81.6 1.4 %collective-permute-done.6.t1.one_ref = f32[40,128]{1,0:T(8,128)S(1)} collective-permute-done((f32[40,128]{1,0:T(8,128)}, f32[40,128]{1,0:T(8,128)S(1)}, u32[]{:S(2)}, u32[]{:S(2)}) %collective-permute-start.6) | collective-permute-done | bytes 20512 | tf_op jit(solution)/shard_map/ppermute | solution.py:578
  83.1 1.2 %collective-permute-done.7.t2.two_ref = f32[40,128]{1,0:T(8,128)S(1)} collective-permute-done((f32[40,128]{1,0:T(8,128)}, f32[40,128]{1,0:T(8,128)S(1)}, u32[]{:S(2)}, u32[]{:S(2)}) %collective-permute-start.7) | collective-permute-done | bytes 20512 | tf_op jit(solution)/shard_map/ppermute | solution.py:578
  84.3 3.5 %collective-permute-done.8.t3.three_ref = f32[40,128]{1,0:T(8,128)S(1)} collective-permute-done((f32[40,128]{1,0:T(8,128)}, f32[40,128]{1,0:T(8,128)S(1)}, u32[]{:S(2)}, u32[]{:S(2)}) %collective-permute-start.8) | collective-permute-done | bytes 20512 | tf_op jit(solution)/shard_map/ppermute | solution.py:578
  87.8 0.0 all-to-all-done.part_ref
  87.8 0.7 spread.1
  88.6 10.6 %all-to-all-start.1 = ((bf16[32,20,128]{2,1,0:T(8,128)(2,1)}), bf16[32,20,128]{2,1,0:T(8,128)(2,1)S(1)}, u32[]{:S(2)}, u32[]{:S(2)}) async-start(bf16[32,20,128]{2,1,0:T(8,128)(2,1)} %spread.1), calls=%async_computation.1 | async-start | bytes 393216 | tf_op jit(solution)/shard_map/all_to_all | solution.py:591
  99.2 0.0 copy-done.2
  99.2 0.0 copy-start
  99.2 0.0 copy-start.1
  99.2 8.1 %key_side.1 = (bf16[128,2560]{1,0:T(8,128)(2,1)}, bf16[128,2560]{1,0:T(8,128)(2,1)}) custom-call(s32[1]{0:T(128)} %bitcast.odd_ref, bf16[5136,128]{1,0:T(8,128)(2,1)} %get-tuple-element.22.a.am, bf16[5136,128]{1,0:T(8,128)(2,1)} %gate.3.b, bf16[5136,128]{1,0:T(8,128)(2,1)} %gate.4.x1.x1m, bf16[5136,128]{1,0:T(8,128)(2,1)} %collective-permute-done.4.s1.s1m, ...), custom_call_target="tpu_custom_call" | custom-call | flops 1342177280 | bytes 1048576 | tf_op jit(solution)/shard_map/key_side/pallas_call | solution.py:602
  107.3 0.1 all-to-all-done.1.part_ref
  107.4 0.7 gains.1
  (10 shorter events, 0.0 us)
Async XLA Ops:
  4.6 25.8 %collective-permute-start = (bf16[5136,128]{1,0:T(8,128)(2,1)}, bf16[5136,128]{1,0:T(8,128)(2,1)}, u32[]{:S(2)}, u32[]{:S(2)}) collective-permute-start(bf16[5136,128]{1,0:T(8,128)(2,1)} %get-tuple-element.22.a.am), channel_id=1, source_target_pairs={{1,2},{3,4},{5,6},{7,8},{9,10},{11,12},{13,14},{15,16},{17,18},{19... | collective-permute-start | bytes 3944456 | tf_op jit(solution)/shard_map/ppermute | solution.py:540
  15.2 24.1 %collective-permute-start.2 = (bf16[5136,128]{1,0:T(8,128)(2,1)}, bf16[5136,128]{1,0:T(8,128)(2,1)}, u32[]{:S(2)}, u32[]{:S(2)}) collective-permute-start(bf16[5136,128]{1,0:T(8,128)(2,1)} %gate.3.b), channel_id=1, source_target_pairs={{0,2},{2,4},{4,6},{6,8},{8,10},{10,12},{12,14},{14,16},{16,18},{18... | collective-permute-start | bytes 3944456 | tf_op jit(solution)/shard_map/ppermute | solution.py:545
  16.5 24.7 %collective-permute-start.4 = (bf16[5136,128]{1,0:T(8,128)(2,1)}, bf16[5136,128]{1,0:T(8,128)(2,1)}, u32[]{:S(2)}, u32[]{:S(2)}) collective-permute-start(bf16[5136,128]{1,0:T(8,128)(2,1)} %gate.3.b), channel_id=1, source_target_pairs={{0,1},{1,0},{2,3},{3,2},{4,5},{5,4},{6,7},{7,6},{8,9},{9,8},{10,11... | collective-permute-start | bytes 3944456 | tf_op jit(solution)/shard_map/ppermute | solution.py:547
  30.4 10.9 %collective-permute-start.5 = (bf16[5136,128]{1,0:T(8,128)(2,1)}, bf16[5136,128]{1,0:T(8,128)(2,1)}, u32[]{:S(2)}, u32[]{:S(2)}) collective-permute-start(bf16[5136,128]{1,0:T(8,128)(2,1)} %gate.4.x1.x1m), channel_id=1, source_target_pairs={{0,1},{1,0},{2,3},{3,2},{4,5},{5,4},{6,7},{7,6},{8,9},{9,8},{10,11... | collective-permute-start | bytes 3944456 | tf_op jit(solution)/shard_map/ppermute | solution.py:548
  32.3 21.1 %collective-permute-start.1 = (bf16[5136,128]{1,0:T(8,128)(2,1)}, bf16[5136,128]{1,0:T(8,128)(2,1)}, u32[]{:S(2)}, u32[]{:S(2)}) collective-permute-start(bf16[5136,128]{1,0:T(8,128)(2,1)} %gate.4.x1.x1m), channel_id=1, source_target_pairs={{0,2},{2,4},{4,6},{6,8},{8,10},{10,12},{12,14},{14,16},{16,18},{18... | collective-permute-start | bytes 3944456 | tf_op jit(solution)/shard_map/ppermute | solution.py:546
  39.3 14.1 %collective-permute-start.3 = (bf16[5136,128]{1,0:T(8,128)(2,1)}, bf16[5136,128]{1,0:T(8,128)(2,1)}, u32[]{:S(2)}, u32[]{:S(2)}) collective-permute-start(bf16[5136,128]{1,0:T(8,128)(2,1)} %collective-permute-done.2.x2.x2m), channel_id=1, source_target_pairs={{0,1},{1,0},{2,3},{3,2},{4,5},{5,4},{6,7},{7,6},{8,9},{9,8},{10,11... | collective-permute-start | bytes 3944456 | tf_op jit(solution)/shard_map/ppermute | solution.py:549
  59.8 28.1 %all-to-all-start = ((bf16[16,20,128]{2,1,0:T(8,128)(2,1)}), bf16[16,20,128]{2,1,0:T(8,128)(2,1)S(1)}, u32[]{:S(2)}, u32[]{:S(2)}) async-start(bf16[16,20,128]{2,1,0:T(8,128)(2,1)} %get-tuple-element.36), calls=%async_computation | async-start | bytes 196608 | tf_op jit(solution)/shard_map/all_to_all | solution.py:580
  74.8 8.3 %collective-permute-start.6 = (f32[40,128]{1,0:T(8,128)}, f32[40,128]{1,0:T(8,128)S(1)}, u32[]{:S(2)}, u32[]{:S(2)}) collective-permute-start(f32[40,128]{1,0:T(8,128)} %get-tuple-element.32.t0), channel_id=1, source_target_pairs={{1,0},{2,1},{3,2},{4,3},{5,4},{6,5},{7,6},{8,7},{9,8},{10,9},{11,1... | collective-permute-start | bytes 61448 | tf_op jit(solution)/shard_map/ppermute | solution.py:578
  79.0 5.3 %collective-permute-start.7 = (f32[40,128]{1,0:T(8,128)}, f32[40,128]{1,0:T(8,128)S(1)}, u32[]{:S(2)}, u32[]{:S(2)}) collective-permute-start(f32[40,128]{1,0:T(8,128)} %get-tuple-element.32.t0), channel_id=1, source_target_pairs={{2,0},{3,1},{4,2},{5,3},{6,4},{7,5},{8,6},{9,7},{10,8},{11,9},{12,... | collective-permute-start | bytes 61448 | tf_op jit(solution)/shard_map/ppermute | solution.py:578
  80.3 7.5 %collective-permute-start.8 = (f32[40,128]{1,0:T(8,128)}, f32[40,128]{1,0:T(8,128)S(1)}, u32[]{:S(2)}, u32[]{:S(2)}) collective-permute-start(f32[40,128]{1,0:T(8,128)} %get-tuple-element.32.t0), channel_id=1, source_target_pairs={{3,0},{4,1},{5,2},{6,3},{7,4},{8,5},{9,6},{10,7},{11,8},{12,9},{13... | collective-permute-start | bytes 61448 | tf_op jit(solution)/shard_map/ppermute | solution.py:578
  83.1 16.1 %copy-start.2 = (f32[40,128]{1,0:T(8,128)}, f32[40,128]{1,0:T(8,128)S(1)}, u32[]{:S(2)}) copy-start(f32[40,128]{1,0:T(8,128)S(1)} %collective-permute-done.6.t1.one_ref) | copy-start | bytes 61444
  84.3 14.9 %copy-start.3 = (f32[40,128]{1,0:T(8,128)}, f32[40,128]{1,0:T(8,128)S(1)}, u32[]{:S(2)}) copy-start(f32[40,128]{1,0:T(8,128)S(1)} %collective-permute-done.7.t2.two_ref) | copy-start | bytes 61444
  87.8 11.4 %copy-start.4 = (f32[40,128]{1,0:T(8,128)}, f32[40,128]{1,0:T(8,128)S(1)}, u32[]{:S(2)}) copy-start(f32[40,128]{1,0:T(8,128)S(1)} %collective-permute-done.8.t3.three_ref) | copy-start | bytes 61444
  88.6 18.9 %all-to-all-start.1 = ((bf16[32,20,128]{2,1,0:T(8,128)(2,1)}), bf16[32,20,128]{2,1,0:T(8,128)(2,1)S(1)}, u32[]{:S(2)}, u32[]{:S(2)}) async-start(bf16[32,20,128]{2,1,0:T(8,128)(2,1)} %spread.1), calls=%async_computation.1 | async-start | bytes 393216 | tf_op jit(solution)/shard_map/all_to_all | solution.py:591
  99.2 8.2 %copy-start = (f32[2560]{0:T(1024)S(1)}, f32[2560]{0:T(1024)}, u32[]{:S(2)}) copy-start(f32[2560]{0:T(1024)} %param.11) | copy-start | bytes 30724
  99.2 8.2 %copy-start.1 = (f32[2560]{0:T(1024)S(1)}, f32[2560]{0:T(1024)}, u32[]{:S(2)}) copy-start(f32[2560]{0:T(1024)} %param.10) | copy-start | bytes 30724

commit v7 on v6

--- a/solution.py
+++ b/solution.py
@@ -178,10 +178,9 @@
         stat_ref[out, :] = jnp.where(left, best + jnp.log2(total), delta)
 
 
-def near_kernel(rows, factor, odd_ref, a, b, x1, s1, x2, s2, am, x1m, s1m, x2m, s2m, g0, h0, stat0, g_ref, h_ref, stat_ref):
+def near_kernel(rows, factor, odd_ref, a, b, x1, s1, am, x1m, s1m, g0, h0, stat0, g_ref, h_ref, stat_ref):
     odd = odd_ref[0] == 1
-    bias = bias_row([bias_of(am, odd, s1m, x1m), bias_of(am, odd, s2m, x2m)], rows)
-    pairs = ((s1, x1), (s2, x2))
+    bias = bias_of(am, odd, s1m, x1m)
     left = left_half(rows)
     keys, scores, dprobs = [], [], []
     for j in range(PER):
@@ -189,8 +188,8 @@
         low = head_rows(PER + j, rows)
         q = jnp.where(odd, b[top, :], a[top, :])
         d_out = jnp.where(odd, b[low, :], a[low, :])
-        keys.append(jnp.concatenate([jnp.where(odd, o[top, :], e[top, :]) for o, e in pairs], axis=0))
-        vals = jnp.concatenate([jnp.where(odd, o[low, :], e[low, :]) for o, e in pairs], axis=0)
+        keys.append(jnp.where(odd, s1[top, :], x1[top, :]))
+        vals = jnp.where(odd, s1[low, :], x1[low, :])
         scores.append(dot_nt(q, keys[j]))
         dprobs.append(dot_nt(d_out, vals))
     for j in range(PER):
@@ -199,14 +198,13 @@
         score = scores[j] * factor + bias
         best = jnp.maximum(old_lse, jnp.max(score, axis=-1, keepdims=True))
         kept = jnp.exp2(old_lse - best)
-        prob, total, mixed = softmax_part(jnp.concatenate([best, best], axis=1), score, dprobs[j])
+        prob, total, mixed = softmax_part(best, score, dprobs[j])
         total = kept + total
         inverse = 1.0 / total
         kept = kept * inverse
         delta = kept * old_delta + mixed * inverse
-        inverse, change = [jnp.concatenate([value, value], axis=1) for value in (inverse, delta)]
         prob = prob * inverse
-        both = jnp.concatenate([(prob * (dprobs[j] - change)).astype(BF16), prob.astype(BF16)], axis=0)
+        both = jnp.concatenate([(prob * (dprobs[j] - delta)).astype(BF16), prob.astype(BF16)], axis=0)
         sums = dot_nn(both, keys[j])
         g_ref[out, :] = sums[:rows] + kept * (g0[out, :] + (old_delta - delta) * h0[out, :])
         h_ref[out, :] = sums[rows:] + kept * h0[out, :]
@@ -245,7 +243,7 @@
     return ref.at[pl.ds(step * size, size), :]
 
 
-def query_kernel(rows, heads, factor, odd_ref, a, b, x3, s3, g_hbm, h_hbm, near_hbm, q_hbm, gq_hbm, rq_hbm,
+def query_kernel(rows, heads, factor, odd_ref, a, b, x2, s2, x3, s3, g_hbm, h_hbm, near_hbm, q_hbm, gq_hbm, rq_hbm,
                  dq_hbm, w_hbm, stat_hbm, own, last, g_mem, h_mem, near_mem, q_mem, gain, scales, marks, tilt, dq_mem,
                  w_mem, stat_mem,
                  sems, out_sems):
@@ -258,13 +256,15 @@
     mark = pl.ds(tail, MARK_ROWS)
     small = [
         loads.make(marks.at[0], a.at[mark, :]),
-        loads.make(marks.at[1], s3.at[mark, :], x3.at[mark, :]),
+        loads.make(marks.at[1], s2.at[mark, :], x2.at[mark, :]),
+        loads.make(marks.at[2], s3.at[mark, :], x3.at[mark, :]),
     ]
     later = [loads.make(scales, rq_hbm), loads.make(gain, gq_hbm), loads.make(q_mem, q_hbm)]
     blocks = [
         [
             loads.make(chunk(own, step, 2 * span), chunk(b, step, 2 * span), chunk(a, step, 2 * span)),
-            loads.make(chunk(last, step, 2 * span), chunk(s3, step, 2 * span), chunk(x3, step, 2 * span)),
+            loads.make(chunk(last.at[0], step, 2 * span), chunk(s2, step, 2 * span), chunk(x2, step, 2 * span)),
+            loads.make(chunk(last.at[1], step, 2 * span), chunk(s3, step, 2 * span), chunk(x3, step, 2 * span)),
             loads.make(chunk(near_mem, step, span), chunk(near_hbm, step, span)),
         ]
         for step in range(steps)
@@ -280,7 +280,7 @@
         loads.start(load)
     for load in small:
         loads.wait(load)
-    bias = jnp.where(mark_of(marks.at[0]) == mark_of(marks.at[1]), 0.0, NEG)
+    bias = bias_row([jnp.where(mark_of(marks.at[0]) == mark_of(marks.at[d]), 0.0, NEG) for d in (1, 2)], rows)
     lane = lax.broadcasted_iota(jnp.int32, (rows, HSIZE), 1)
     scale = 1.0 / math.sqrt(HSIZE)
     left = lane < HSIZE // 2
@@ -299,22 +299,23 @@
         for j in range(PER):
             top = slice(base + j * rows, base + (j + 1) * rows)
             low = slice(base + span + j * rows, base + span + (j + 1) * rows)
-            keys.append(last[top, :])
+            keys.append(jnp.concatenate([last[0, top, :], last[1, top, :]], axis=0))
             scores.append(dot_nt(own[top, :], keys[j]))
-            dprobs.append(dot_nt(own[low, :], last[low, :]))
+            dprobs.append(dot_nt(own[low, :], jnp.concatenate([last[0, low, :], last[1, low, :]], axis=0)))
         fars, nears = [], []
         for j in range(PER):
             head = step * PER + j
             old_lse, old_delta = halves(near_mem[head_rows(head, rows), :], left)
             score = scores[j] * factor + bias
             best = jnp.maximum(old_lse, jnp.max(score, axis=-1, keepdims=True))
-            prob = jnp.exp2(score - best)
             kept = jnp.exp2(old_lse - best)
-            total = kept + jnp.sum(prob, axis=-1, keepdims=True)
+            prob, total, mixed = softmax_part(jnp.concatenate([best, best], axis=1), score, dprobs[j])
+            total = kept + total
             inverse = 1.0 / total
             kept = kept * inverse
-            delta = kept * old_delta + jnp.sum(prob * dprobs[j], axis=-1, keepdims=True) * inverse
-            fars.append(((prob * inverse) * (dprobs[j] - delta)).astype(BF16))
+            delta = kept * old_delta + mixed * inverse
+            both = [jnp.concatenate([value, value], axis=1) for value in (inverse, delta)]
+            fars.append(((prob * both[0]) * (dprobs[j] - both[1])).astype(BF16))
             nears.append((kept, old_delta - delta))
             lse = jnp.where(lane == head, best + jnp.log2(total), lse)
             deltas = jnp.where(lane == head, delta, deltas)
@@ -550,10 +551,10 @@
 
     near = gridded(
         functools.partial(near_kernel, rows, factor), "near", 1024,
-        [if_even, if_odd, if_even, if_odd, if_even, if_odd] + [mark] * 5 + [tall] * 3,
+        [if_even, if_odd, if_even, if_odd] + [mark] * 3 + [tall] * 3,
         (tall,) * 3,
         sums_shape,
-    )(odd, a, b, x1, s1, x2, s2, a, x1, s1, x2, s2, *sums)
+    )(odd, a, b, x1, s1, a, x1, s1, *sums)
     block = pltpu.VMEM((2 * heads * rows, HSIZE), BF16)
     flat = pltpu.VMEM((rows, width), BF16)
     wide = pltpu.VMEM((rows, width), F32)
@@ -564,15 +565,16 @@
     dq_in, w, stats = pl.pallas_call(
         functools.partial(query_kernel, rows, heads, factor),
         out_shape=(whole_shape, shape(along, heads, HSIZE, dtype=BF16), shape(2 * heads, rows)),
-        in_specs=[smem] + [hbm] * 10,
+        in_specs=[smem] + [hbm] * 12,
         out_specs=(hbm,) * 3,
-        scratch_shapes=[block, block, sum_mem, sum_mem, sum_mem, flat, gain_mem, scale_mem, marks(2), wide, flat,
+        scratch_shapes=[block, pltpu.VMEM((2, 2 * heads * rows, HSIZE), BF16), sum_mem, sum_mem, sum_mem, flat, gain_mem,
+                        scale_mem, marks(WIN - 1), wide, flat,
                         pltpu.VMEM((along, heads, HSIZE), BF16), pltpu.VMEM((2 * heads, rows), F32),
-                        pltpu.SemaphoreType.DMA((5 + 5 * steps,)), pltpu.SemaphoreType.DMA((steps + 2,))],
+                        pltpu.SemaphoreType.DMA((6 + 6 * steps,)), pltpu.SemaphoreType.DMA((steps + 2,))],
         compiler_params=params(),
         cost_estimate=cost(1024),
         name="query_side",
-    )(odd, a, b, x3, s3, *near, q_in, gq, rq)
+    )(odd, a, b, x2, s2, x3, s3, *near, q_in, gq, rq)
 
     def back(value, by):
         return lax.ppermute(value, AXES, [(i, i - by) for i in range(by, groups)])

time: 109 us -> 108 us (level)
    ppermute x1, waiting for transfers between devices: 5.71 us -> 7.64 us  [body(): x2 = lax.ppermute(b, AXES, next_chip)]
    pallas_call x1, Pallas kernels: 8.5 us -> 7.22 us  [body(): gridded(functools.partial(near_kernel, rows, factor), 'near', 1024, [if_e...]
    ppermute x1, waiting for transfers between devices: 3.64 us -> 2.52 us  [body(): x3 = after(lax.ppermute(x1, AXES, next_chip), pair_flops)]
  transfers between devices with their start and end apart: 11 -> 11, of which waited for: 7 -> 7; matrix products, arithmetic and copies ran while one was open for 0% -> 0% of each run, Pallas kernels for 21% -> 19%
where the time goes in v7:
time: 108 us
  starting transfers between devices  49.7 us (46%)
  Pallas kernels  32.7 us (30%)
  waiting for transfers between devices  23.7 us (22%)
  between operations  1.45 us (1%)
    all_to_all x1, starting transfers between devices, body(): w = lax.all_to_all(w, 'z', 0, 0)  14.7 us
    all_to_all x1, starting transfers between devices, body(): w = lax.all_to_all(w, ('dp', 'core'), 0, 0)  10 us
    pallas_call x1, Pallas kernels, body(): pl.pallas_call(functools.partial(key_kernel, rows, heads, factor), out_sh...  8.12 us
    ppermute x1, waiting for transfers between devices, body(): x2 = lax.ppermute(b, AXES, next_chip)  7.64 us
    pallas_call x1, Pallas kernels, body(): gridded(functools.partial(near_kernel, rows, factor), 'near', 1024, [if_e...  7.22 us
    ppermute x1, waiting for transfers between devices, body(): x1 = after(lax.ppermute(a, AXES, cross), 2 * pair_flops)  7.16 us
    pallas_call x1, Pallas kernels, body(): pl.pallas_call(functools.partial(query_kernel, rows, heads, factor), out_...  7 us
    ppermute x1, starting transfers between devices, body(): s1 = lax.ppermute(b, AXES, chip)  6.73 us
  transfers between devices with their start and end apart: 11, of which 7 were waited for; matrix products, arithmetic and copies ran while one was open for 0% of the time, Pallas kernels for 19%

profile of v7, /device:TPU:1, one launch (start us, length us, event | category | flops | bytes accessed | tf_op | source)
XLA Modules:
  0.0 107.5 jit_solution(16117260148294507678)
XLA Ops:
  1.3 3.3 %pack.1 = (bf16[5136,128]{1,0:T(8,128)(2,1)}, bf16[5136,128]{1,0:T(8,128)(2,1)}, f32[128,128]{1,0:T(8,128)}, f32[128,128]{1,0:T(8,128)}) custom-call(s32[1]{0:T(128)} %bitcast.odd_ref, s32[1]{0:T(128)S(6)} %copy.18.video_ref, bf16[128,2560]{1,0:T(8,128)(2,1)} %q_hbm.3, bf16[128,2560]{1,0:T(8,128)(2,1)} %k_hbm.3, bf16[128,2560]{1,0:T(8,128)(2,1)} %d_hbm.1, ...), custom_call_target="tpu_custom_call" | custom-call | flops 83886080 | bytes 1048576 | tf_op jit(solution)/shard_map/pack/pallas_call | solution.py:510
  4.6 5.0 %collective-permute-start.1 = (bf16[5136,128]{1,0:T(8,128)(2,1)}, bf16[5136,128]{1,0:T(8,128)(2,1)}, u32[]{:S(2)}, u32[]{:S(2)}) collective-permute-start(bf16[5136,128]{1,0:T(8,128)(2,1)} %get-tuple-element.22.a.am), channel_id=1, source_target_pairs={{1,2},{3,4},{5,6},{7,8},{9,10},{11,12},{13,14},{15,16},{17,18},{19... | collective-permute-start | bytes 3944456 | tf_op jit(solution)/shard_map/ppermute | solution.py:541
  9.6 5.6 %own.1 = (f32[2560,128]{1,0:T(8,128)}, f32[2560,128]{1,0:T(8,128)}, f32[2560,128]{1,0:T(8,128)}) custom-call(s32[1]{0:T(128)} %bitcast.odd_ref, bf16[5136,128]{1,0:T(8,128)(2,1)} %get-tuple-element.22.a.am, bf16[5136,128]{1,0:T(8,128)(2,1)} %get-tuple-element.23.b.refs_0_), custom_call_target="tpu_custom_call" | custom-call | flops 1024 | bytes 1048576 | tf_op jit(solution)/shard_map/own/pallas_call | solution.py:542
  15.2 1.3 %collective-permute-start = (bf16[5136,128]{1,0:T(8,128)(2,1)}, bf16[5136,128]{1,0:T(8,128)(2,1)}, u32[]{:S(2)}, u32[]{:S(2)}) collective-permute-start(bf16[5136,128]{1,0:T(8,128)(2,1)} %gate.3.b), channel_id=1, source_target_pairs={{0,2},{2,4},{4,6},{6,8},{8,10},{10,12},{12,14},{14,16},{16,18},{18... | collective-permute-start | bytes 3944456 | tf_op jit(solution)/shard_map/ppermute | solution.py:546
  16.5 6.7 %collective-permute-start.5 = (bf16[5136,128]{1,0:T(8,128)(2,1)}, bf16[5136,128]{1,0:T(8,128)(2,1)}, u32[]{:S(2)}, u32[]{:S(2)}) collective-permute-start(bf16[5136,128]{1,0:T(8,128)(2,1)} %gate.3.b), channel_id=1, source_target_pairs={{0,1},{1,0},{2,3},{3,2},{4,5},{5,4},{6,7},{7,6},{8,9},{9,8},{10,11... | collective-permute-start | bytes 3944456 | tf_op jit(solution)/shard_map/ppermute | solution.py:548
  23.2 7.2 %collective-permute-done.1.refs_0_ = bf16[5136,128]{1,0:T(8,128)(2,1)} collective-permute-done((bf16[5136,128]{1,0:T(8,128)(2,1)}, bf16[5136,128]{1,0:T(8,128)(2,1)}, u32[]{:S(2)}, u32[]{:S(2)}) %collective-permute-start.1) | collective-permute-done | bytes 1314848 | tf_op jit(solution)/shard_map/ppermute | solution.py:541
  30.4 1.3 %collective-permute-start.3 = (bf16[5136,128]{1,0:T(8,128)(2,1)}, bf16[5136,128]{1,0:T(8,128)(2,1)}, u32[]{:S(2)}, u32[]{:S(2)}) collective-permute-start(bf16[5136,128]{1,0:T(8,128)(2,1)} %gate.4.x1.x1m), channel_id=1, source_target_pairs={{0,2},{2,4},{4,6},{6,8},{8,10},{10,12},{12,14},{14,16},{16,18},{18... | collective-permute-start | bytes 3944456 | tf_op jit(solution)/shard_map/ppermute | solution.py:547
  31.7 7.6 %collective-permute-done.x2 = bf16[5136,128]{1,0:T(8,128)(2,1)} collective-permute-done((bf16[5136,128]{1,0:T(8,128)(2,1)}, bf16[5136,128]{1,0:T(8,128)(2,1)}, u32[]{:S(2)}, u32[]{:S(2)}) %collective-permute-start) | collective-permute-done | bytes 1314848 | tf_op jit(solution)/shard_map/ppermute | solution.py:546
  39.3 1.9 %collective-permute-start.4 = (bf16[5136,128]{1,0:T(8,128)(2,1)}, bf16[5136,128]{1,0:T(8,128)(2,1)}, u32[]{:S(2)}, u32[]{:S(2)}) collective-permute-start(bf16[5136,128]{1,0:T(8,128)(2,1)} %collective-permute-done.x2), channel_id=1, source_target_pairs={{0,1},{1,0},{2,3},{3,2},{4,5},{5,4},{6,7},{7,6},{8,9},{9,8},{10,11... | collective-permute-start | bytes 3944456 | tf_op jit(solution)/shard_map/ppermute | solution.py:550
  41.2 2.4 %collective-permute-start.2 = (bf16[5136,128]{1,0:T(8,128)(2,1)}, bf16[5136,128]{1,0:T(8,128)(2,1)}, u32[]{:S(2)}, u32[]{:S(2)}) collective-permute-start(bf16[5136,128]{1,0:T(8,128)(2,1)} %gate.4.x1.x1m), channel_id=1, source_target_pairs={{0,1},{1,0},{2,3},{3,2},{4,5},{5,4},{6,7},{7,6},{8,9},{9,8},{10,11... | collective-permute-start | bytes 3944456 | tf_op jit(solution)/shard_map/ppermute | solution.py:549
  43.7 0.0 collective-permute-done.5.s1.s1m
  43.7 7.2 %near.1 = (f32[2560,128]{1,0:T(8,128)}, f32[2560,128]{1,0:T(8,128)}, f32[2560,128]{1,0:T(8,128)}) custom-call(s32[1]{0:T(128)} %bitcast.odd_ref, bf16[5136,128]{1,0:T(8,128)(2,1)} %get-tuple-element.22.a.am, bf16[5136,128]{1,0:T(8,128)(2,1)} %gate.3.b, bf16[5136,128]{1,0:T(8,128)(2,1)} %gate.4.x1.x1m, bf16[5136,128]{1,0:T(8,128)(2,1)} %collective-permute-done.5.s1.s1m, ...), custom_call_target="tpu_custom_call" | custom-call | flops 1024 | bytes 1048576 | tf_op jit(solution)/shard_map/near/pallas_call | solution.py:552
  50.9 2.5 %collective-permute-done.3.refs_0_ = bf16[5136,128]{1,0:T(8,128)(2,1)} collective-permute-done((bf16[5136,128]{1,0:T(8,128)(2,1)}, bf16[5136,128]{1,0:T(8,128)(2,1)}, u32[]{:S(2)}, u32[]{:S(2)}) %collective-permute-start.3) | collective-permute-done | bytes 1314848 | tf_op jit(solution)/shard_map/ppermute | solution.py:547
  53.4 0.0 collective-permute-done.4.s3
  53.4 0.0 collective-permute-done.2.s2
  53.4 7.0 %query_side.1 = (bf16[128,2560]{1,0:T(8,128)(2,1)}, bf16[16,20,128]{2,1,0:T(8,128)(2,1)}, f32[40,128]{1,0:T(8,128)}) custom-call(s32[1]{0:T(128)} %bitcast.odd_ref, bf16[5136,128]{1,0:T(8,128)(2,1)} %get-tuple-element.22.a.am, bf16[5136,128]{1,0:T(8,128)(2,1)} %gate.3.b, bf16[5136,128]{1,0:T(8,128)(2,1)} %collective-permute-done.x2, ...), custom_call_target="tpu_custom_call" | custom-call | flops 1024 | bytes 1048576 | tf_op jit(solution)/shard_map/query_side/pallas_call | solution.py:565
  60.4 14.7 %all-to-all-start = ((bf16[16,20,128]{2,1,0:T(8,128)(2,1)}), bf16[16,20,128]{2,1,0:T(8,128)(2,1)S(1)}, u32[]{:S(2)}, u32[]{:S(2)}) async-start(bf16[16,20,128]{2,1,0:T(8,128)(2,1)} %get-tuple-element.36), calls=%async_computation | async-start | bytes 196608 | tf_op jit(solution)/shard_map/all_to_all | solution.py:582
  75.2 3.8 %collective-permute-start.6 = (f32[40,128]{1,0:T(8,128)}, f32[40,128]{1,0:T(8,128)S(1)}, u32[]{:S(2)}, u32[]{:S(2)}) collective-permute-start(f32[40,128]{1,0:T(8,128)} %get-tuple-element.32.t0), channel_id=1, source_target_pairs={{1,0},{2,1},{3,2},{4,3},{5,4},{6,5},{7,6},{8,7},{9,8},{10,9},{11,1... | collective-permute-start | bytes 61448 | tf_op jit(solution)/shard_map/ppermute | solution.py:580
  79.0 1.3 %collective-permute-start.7 = (f32[40,128]{1,0:T(8,128)}, f32[40,128]{1,0:T(8,128)S(1)}, u32[]{:S(2)}, u32[]{:S(2)}) collective-permute-start(f32[40,128]{1,0:T(8,128)} %get-tuple-element.32.t0), channel_id=1, source_target_pairs={{2,0},{3,1},{4,2},{5,3},{6,4},{7,5},{8,6},{9,7},{10,8},{11,9},{12,... | collective-permute-start | bytes 61448 | tf_op jit(solution)/shard_map/ppermute | solution.py:580
  80.3 1.3 %collective-permute-start.8 = (f32[40,128]{1,0:T(8,128)}, f32[40,128]{1,0:T(8,128)S(1)}, u32[]{:S(2)}, u32[]{:S(2)}) collective-permute-start(f32[40,128]{1,0:T(8,128)} %get-tuple-element.32.t0), channel_id=1, source_target_pairs={{3,0},{4,1},{5,2},{6,3},{7,4},{8,5},{9,6},{10,7},{11,8},{12,9},{13... | collective-permute-start | bytes 61448 | tf_op jit(solution)/shard_map/ppermute | solution.py:580
  81.6 1.4 %collective-permute-done.6.t1.one_ref = f32[40,128]{1,0:T(8,128)S(1)} collective-permute-done((f32[40,128]{1,0:T(8,128)}, f32[40,128]{1,0:T(8,128)S(1)}, u32[]{:S(2)}, u32[]{:S(2)}) %collective-permute-start.6) | collective-permute-done | bytes 20512 | tf_op jit(solution)/shard_map/ppermute | solution.py:580
  83.0 1.2 %collective-permute-done.7.t2.two_ref = f32[40,128]{1,0:T(8,128)S(1)} collective-permute-done((f32[40,128]{1,0:T(8,128)}, f32[40,128]{1,0:T(8,128)S(1)}, u32[]{:S(2)}, u32[]{:S(2)}) %collective-permute-start.7) | collective-permute-done | bytes 20512 | tf_op jit(solution)/shard_map/ppermute | solution.py:580
  84.2 3.6 %collective-permute-done.8.t3.three_ref = f32[40,128]{1,0:T(8,128)S(1)} collective-permute-done((f32[40,128]{1,0:T(8,128)}, f32[40,128]{1,0:T(8,128)S(1)}, u32[]{:S(2)}, u32[]{:S(2)}) %collective-permute-start.8) | collective-permute-done | bytes 20512 | tf_op jit(solution)/shard_map/ppermute | solution.py:580
  87.8 0.0 all-to-all-done.part_ref
  87.8 0.7 spread.1
  88.6 10.0 %all-to-all-start.1 = ((bf16[32,20,128]{2,1,0:T(8,128)(2,1)}), bf16[32,20,128]{2,1,0:T(8,128)(2,1)S(1)}, u32[]{:S(2)}, u32[]{:S(2)}) async-start(bf16[32,20,128]{2,1,0:T(8,128)(2,1)} %spread.1), calls=%async_computation.1 | async-start | bytes 393216 | tf_op jit(solution)/shard_map/all_to_all | solution.py:593
  98.6 0.0 copy-start
  98.6 0.0 copy-start.1
  98.7 8.1 %key_side.1 = (bf16[128,2560]{1,0:T(8,128)(2,1)}, bf16[128,2560]{1,0:T(8,128)(2,1)}) custom-call(s32[1]{0:T(128)} %bitcast.odd_ref, bf16[5136,128]{1,0:T(8,128)(2,1)} %get-tuple-element.22.a.am, bf16[5136,128]{1,0:T(8,128)(2,1)} %gate.3.b, bf16[5136,128]{1,0:T(8,128)(2,1)} %gate.4.x1.x1m, bf16[5136,128]{1,0:T(8,128)(2,1)} %collective-permute-done.5.s1.s1m, ...), custom_call_target="tpu_custom_call" | custom-call | flops 1342177280 | bytes 1048576 | tf_op jit(solution)/shard_map/key_side/pallas_call | solution.py:604
  106.8 0.1 all-to-all-done.1.part_ref
  106.9 0.0 copy-done
  106.9 0.7 gains.1
  (10 shorter events, 0.0 us)
Async XLA Ops:
  4.6 25.8 %collective-permute-start.1 = (bf16[5136,128]{1,0:T(8,128)(2,1)}, bf16[5136,128]{1,0:T(8,128)(2,1)}, u32[]{:S(2)}, u32[]{:S(2)}) collective-permute-start(bf16[5136,128]{1,0:T(8,128)(2,1)} %get-tuple-element.22.a.am), channel_id=1, source_target_pairs={{1,2},{3,4},{5,6},{7,8},{9,10},{11,12},{13,14},{15,16},{17,18},{19... | collective-permute-start | bytes 3944456 | tf_op jit(solution)/shard_map/ppermute | solution.py:541
  15.2 24.1 %collective-permute-start = (bf16[5136,128]{1,0:T(8,128)(2,1)}, bf16[5136,128]{1,0:T(8,128)(2,1)}, u32[]{:S(2)}, u32[]{:S(2)}) collective-permute-start(bf16[5136,128]{1,0:T(8,128)(2,1)} %gate.3.b), channel_id=1, source_target_pairs={{0,2},{2,4},{4,6},{6,8},{8,10},{10,12},{12,14},{14,16},{16,18},{18... | collective-permute-start | bytes 3944456 | tf_op jit(solution)/shard_map/ppermute | solution.py:546
  16.5 27.2 %collective-permute-start.5 = (bf16[5136,128]{1,0:T(8,128)(2,1)}, bf16[5136,128]{1,0:T(8,128)(2,1)}, u32[]{:S(2)}, u32[]{:S(2)}) collective-permute-start(bf16[5136,128]{1,0:T(8,128)(2,1)} %gate.3.b), channel_id=1, source_target_pairs={{0,1},{1,0},{2,3},{3,2},{4,5},{5,4},{6,7},{7,6},{8,9},{9,8},{10,11... | collective-permute-start | bytes 3944456 | tf_op jit(solution)/shard_map/ppermute | solution.py:548
  30.4 23.0 %collective-permute-start.3 = (bf16[5136,128]{1,0:T(8,128)(2,1)}, bf16[5136,128]{1,0:T(8,128)(2,1)}, u32[]{:S(2)}, u32[]{:S(2)}) collective-permute-start(bf16[5136,128]{1,0:T(8,128)(2,1)} %gate.4.x1.x1m), channel_id=1, source_target_pairs={{0,2},{2,4},{4,6},{6,8},{8,10},{10,12},{12,14},{14,16},{16,18},{18... | collective-permute-start | bytes 3944456 | tf_op jit(solution)/shard_map/ppermute | solution.py:547
  39.3 14.1 %collective-permute-start.4 = (bf16[5136,128]{1,0:T(8,128)(2,1)}, bf16[5136,128]{1,0:T(8,128)(2,1)}, u32[]{:S(2)}, u32[]{:S(2)}) collective-permute-start(bf16[5136,128]{1,0:T(8,128)(2,1)} %collective-permute-done.x2), channel_id=1, source_target_pairs={{0,1},{1,0},{2,3},{3,2},{4,5},{5,4},{6,7},{7,6},{8,9},{9,8},{10,11... | collective-permute-start | bytes 3944456 | tf_op jit(solution)/shard_map/ppermute | solution.py:550
  41.2 12.2 %collective-permute-start.2 = (bf16[5136,128]{1,0:T(8,128)(2,1)}, bf16[5136,128]{1,0:T(8,128)(2,1)}, u32[]{:S(2)}, u32[]{:S(2)}) collective-permute-start(bf16[5136,128]{1,0:T(8,128)(2,1)} %gate.4.x1.x1m), channel_id=1, source_target_pairs={{0,1},{1,0},{2,3},{3,2},{4,5},{5,4},{6,7},{7,6},{8,9},{9,8},{10,11... | collective-permute-start | bytes 3944456 | tf_op jit(solution)/shard_map/ppermute | solution.py:549
  60.4 27.4 %all-to-all-start = ((bf16[16,20,128]{2,1,0:T(8,128)(2,1)}), bf16[16,20,128]{2,1,0:T(8,128)(2,1)S(1)}, u32[]{:S(2)}, u32[]{:S(2)}) async-start(bf16[16,20,128]{2,1,0:T(8,128)(2,1)} %get-tuple-element.36), calls=%async_computation | async-start | bytes 196608 | tf_op jit(solution)/shard_map/all_to_all | solution.py:582
  75.2 7.8 %collective-permute-start.6 = (f32[40,128]{1,0:T(8,128)}, f32[40,128]{1,0:T(8,128)S(1)}, u32[]{:S(2)}, u32[]{:S(2)}) collective-permute-start(f32[40,128]{1,0:T(8,128)} %get-tuple-element.32.t0), channel_id=1, source_target_pairs={{1,0},{2,1},{3,2},{4,3},{5,4},{6,5},{7,6},{8,7},{9,8},{10,9},{11,1... | collective-permute-start | bytes 61448 | tf_op jit(solution)/shard_map/ppermute | solution.py:580
  79.0 5.2 %collective-permute-start.7 = (f32[40,128]{1,0:T(8,128)}, f32[40,128]{1,0:T(8,128)S(1)}, u32[]{:S(2)}, u32[]{:S(2)}) collective-permute-start(f32[40,128]{1,0:T(8,128)} %get-tuple-element.32.t0), channel_id=1, source_target_pairs={{2,0},{3,1},{4,2},{5,3},{6,4},{7,5},{8,6},{9,7},{10,8},{11,9},{12,... | collective-permute-start | bytes 61448 | tf_op jit(solution)/shard_map/ppermute | solution.py:580
  80.3 7.5 %collective-permute-start.8 = (f32[40,128]{1,0:T(8,128)}, f32[40,128]{1,0:T(8,128)S(1)}, u32[]{:S(2)}, u32[]{:S(2)}) collective-permute-start(f32[40,128]{1,0:T(8,128)} %get-tuple-element.32.t0), channel_id=1, source_target_pairs={{3,0},{4,1},{5,2},{6,3},{7,4},{8,5},{9,6},{10,7},{11,8},{12,9},{13... | collective-permute-start | bytes 61448 | tf_op jit(solution)/shard_map/ppermute | solution.py:580
  83.0 15.6 %copy-start.2 = (f32[40,128]{1,0:T(8,128)}, f32[40,128]{1,0:T(8,128)S(1)}, u32[]{:S(2)}) copy-start(f32[40,128]{1,0:T(8,128)S(1)} %collective-permute-done.6.t1.one_ref) | copy-start | bytes 61444
  84.2 14.4 %copy-start.3 = (f32[40,128]{1,0:T(8,128)}, f32[40,128]{1,0:T(8,128)S(1)}, u32[]{:S(2)}) copy-start(f32[40,128]{1,0:T(8,128)S(1)} %collective-permute-done.7.t2.two_ref) | copy-start | bytes 61444
  87.8 10.8 %copy-start.4 = (f32[40,128]{1,0:T(8,128)}, f32[40,128]{1,0:T(8,128)S(1)}, u32[]{:S(2)}) copy-start(f32[40,128]{1,0:T(8,128)S(1)} %collective-permute-done.8.t3.three_ref) | copy-start | bytes 61444
  88.6 18.3 %all-to-all-start.1 = ((bf16[32,20,128]{2,1,0:T(8,128)(2,1)}), bf16[32,20,128]{2,1,0:T(8,128)(2,1)S(1)}, u32[]{:S(2)}, u32[]{:S(2)}) async-start(bf16[32,20,128]{2,1,0:T(8,128)(2,1)} %spread.1), calls=%async_computation.1 | async-start | bytes 393216 | tf_op jit(solution)/shard_map/all_to_all | solution.py:593
  98.6 8.2 %copy-start = (f32[2560]{0:T(1024)S(1)}, f32[2560]{0:T(1024)}, u32[]{:S(2)}) copy-start(f32[2560]{0:T(1024)} %param.10) | copy-start | bytes 30724
  98.6 8.2 %copy-start.1 = (f32[2560]{0:T(1024)S(1)}, f32[2560]{0:T(1024)}, u32[]{:S(2)}) copy-start(f32[2560]{0:T(1024)} %param.11) | copy-start | bytes 30724
